TPU v7x, 32 devices: a whole 2x2x4 slice. The times are simulated.
32 devices in a mesh: seq: 8 (over z, core), hid: 4 (over y, x).
Axes of the slice: x: 2, y: 2, z: 4, core: 2. Of those that a mesh axis runs over, the one named last changes fastest.
Arguments:
- inputs: float32 [32768, 768], P(('seq', 'hid')), may hold values from -6 to 6
- mask_flags: int32 [32768], P(('seq', 'hid')), may hold values 0 or 1
- out_grad: float32 [16, 256, 1280], P('seq', 'hid'), may hold values from -6 to 6
- square: float32 [4, 1280, 1280], P(None, None, 'hid'), as said below
- square_state: float32 [3, 4, 1280, 1280], P(None, None, 'seq', 'hid'), as said below
- kv_weights: float32 [2, 768, 1280], P(None, None, 'hid'), may hold values from -0.21875 to 0.21875
- kv_state: float32 [3, 2, 768, 1280], P(None, None, 'seq', 'hid'), as said below
- latents: float32 [256, 1280], P('hid'), may hold values from -6 to 6
- latents_state: float32 [3, 256, 1280], P(None, 'hid', 'seq'), as said below
- in_params: float32 [3, 768], replicated, as said below
- in_state: float32 [3, 3, 768], replicated, as said below
- lat_params: float32 [4, 1280], replicated, as said below
- lat_state: float32 [3, 4, 1280], replicated, as said below
Outputs:
- latents_out: float32 [16, 256, 1280], P('seq', 'hid')
- inputs_grad: float32 [32768, 768], P(('seq', 'hid'))
- grad_norm: float32 [], replicated
- square_new: float32 [2, 4, 1280, 1280], P(None, None, 'seq', 'hid')
- square_moments: float32 [2, 4, 1280, 1280], P(None, None, 'seq', 'hid')
- kv_new: float32 [2, 2, 768, 1280], P(None, None, 'seq', 'hid')
- kv_moments: float32 [2, 2, 768, 1280], P(None, None, 'seq', 'hid')
- latents_new: float32 [2, 256, 1280], P(None, 'hid', 'seq')
- latents_moments: float32 [2, 256, 1280], P(None, 'hid', 'seq')
- in_new: float32 [2, 3, 768], replicated
- in_moments: float32 [2, 3, 768], replicated
- lat_new: float32 [2, 4, 1280], replicated
- lat_moments: float32 [2, 4, 1280], replicated
- in_grads_clipped: float32 [3, 768], replicated
- lat_grads_clipped: float32 [4, 1280], replicated
Inputs may be any that keep to these rules, and one draw needn't show every extreme that they name: square: slot 1 is the output projection transposed, slot 3 the second feed-forward matrix transposed. `square_state`: slot 0 first moments of both signs, slot 1 positive roots of second moments, slot 2 averaged weights. `kv_state`: slot 0 first moments, slot 1 positive roots of second moments, slot 2 averaged weights. `latents_state`: slot 0 first moments, slot 1 positive roots of second moments, slot 2 averaged weights. `in_params`: gains near 1. `in_state`: slot 0 first moments, slot 1 positive roots of second moments, slot 2 averaged parameters. `lat_params`: gains near 1. `lat_state`: slot 0 first moments, slot 1 positive roots of second moments, slot 2 averaged parameters.
All inputs are finite; a program needn't handle non-finite values. No bound on the sum of `mask_flags` on one device may be relied on, other than what follows from the above.
Results may differ from a plain program's by a relative error of at most 0.015.
The roundings to bfloat16 on the way count: a program that leaves them out, or rounds other values in their place, can miss the bound.
Values may be sent and summed in bfloat16 or wider, within the bound.
No kernel may reach another device: no remote copies, remote signals or barrier semaphores. Data moves between devices by JAX's collectives and lax.ppermute only.
A program may use at most 128 MiB of HBM per device.

v0:
```python
from functools import partial
import math

import jax
import jax.numpy as jnp
from jax import lax
from jax.sharding import PartitionSpec as P

HEADS = 8
HEAD = 160
SEQ_LEN = 2048
STEP = 10


clip_limit = 1.0
beta_one = 0.9
beta_two = 0.999
adam_eps = 1e-08
learn_rate = 0.05
decay_rate = 0.01
ema_keep = 0.9
norm_eps = 1e-05


def norm_rows(values, scale_row, shift_row):
    centre = jnp.mean(values, -1, keepdims=True)
    centred = values - centre
    inverse = lax.rsqrt(jnp.mean(centred * centred, -1, keepdims=True) + norm_eps)
    unit_rows = centred * inverse
    return (unit_rows * scale_row + shift_row, unit_rows, inverse)


def norm_back(upstream, unit_rows, inverse, scale_row):
    scaled = upstream * scale_row
    inner_mean = jnp.mean(scaled, -1, keepdims=True)
    along_mean = jnp.mean(scaled * unit_rows, -1, keepdims=True)
    return inverse * (scaled - inner_mean - unit_rows * along_mean)


def adamw(weight, states, gradient):
    moment_one = beta_one * states[0] + (1.0 - beta_one) * gradient
    root_two = jnp.sqrt(beta_two * states[1] * states[1] + (1.0 - beta_two) * gradient * gradient)
    corrected_one = moment_one / (1.0 - beta_one**STEP)
    denominator = root_two / math.sqrt(1.0 - beta_two**STEP) + adam_eps
    new_weight = weight - learn_rate * (corrected_one / denominator + decay_rate * weight)
    ema_new = ema_keep * states[2] + (1.0 - ema_keep) * new_weight
    return (jnp.stack([new_weight, ema_new]), jnp.stack([moment_one, root_two]))


def on_device(
    inputs,
    mask_flags,
    out_grad,
    square,
    square_state,
    kv_weights,
    kv_state,
    latents,
    latents_state,
    in_params,
    in_state,
    lat_params,
    lat_state,
):
    f32 = jnp.float32
    bf16 = jnp.bfloat16
    hid_count = lax.axis_size("hid")
    heads_here = HEADS // hid_count
    width_here = heads_here * HEAD
    group_rows = inputs.shape[0] * hid_count
    seq_here = group_rows // SEQ_LEN
    score_scale = 1.0 / math.sqrt(HEAD)
    w_sq = square.astype(bf16)
    w_kv = kv_weights.astype(bf16)
    mask_f = mask_flags.astype(f32)[:, None]
    masked = inputs * (1.0 - mask_f) + mask_f * in_params[2]
    normed, in_unit, in_inverse = norm_rows(masked, in_params[0], in_params[1])
    in_low = normed.astype(bf16)
    lat_normed, lat_unit, lat_inverse = norm_rows(latents, lat_params[0], lat_params[1])
    lat_low = lat_normed.astype(bf16)
    in_all, lat_all = (
        lax.all_gather(in_low, "hid", axis=0, tiled=True),
        lax.all_gather(lat_low, "hid", axis=0, tiled=True),
    )
    both_kv = jnp.einsum("td,kdc->tkc", in_all, w_kv, preferred_element_type=f32).astype(bf16)
    lat_total = lat_all.shape[0]
    query_rows = jnp.dot(lat_all, w_sq[0], preferred_element_type=f32).astype(bf16)
    query_heads = query_rows.reshape(lat_total, heads_here, HEAD)
    key_rows = both_kv[:, 0].reshape(seq_here, SEQ_LEN, heads_here, HEAD)
    value_rows = both_kv[:, 1].reshape(seq_here, SEQ_LEN, heads_here, HEAD)
    raw_scores = (
        jnp.einsum("lhe,bshe->bhls", query_heads, key_rows, preferred_element_type=f32)
        * score_scale
    )
    row_max = jnp.max(raw_scores, -1, keepdims=True)
    log_total = jnp.log(jnp.sum(jnp.exp(raw_scores - row_max), -1, keepdims=True)) + row_max
    attn_probs = jnp.exp(raw_scores - log_total)
    attended = jnp.einsum(
        "bhls,bshe->blhe", attn_probs.astype(bf16), value_rows, preferred_element_type=f32
    )
    attended = attended.astype(bf16).reshape(seq_here, lat_total, width_here)
    branch_term = jnp.einsum("blc,dc->bld", attended, w_sq[1], preferred_element_type=f32)
    branch = lax.psum_scatter(branch_term, "hid", scatter_dimension=1, tiled=True)
    residual = latents[None] + branch
    mid_normed, mid_unit, mid_inverse = norm_rows(residual, lat_params[2], lat_params[3])
    mid_all = lax.all_gather(mid_normed.astype(bf16), "hid", axis=1, tiled=True)
    up_proj = jnp.einsum("bld,dc->blc", mid_all, w_sq[2], preferred_element_type=f32)
    hidden = jax.nn.gelu(up_proj, approximate=False).astype(bf16)
    ffn_term = jnp.einsum("blc,dc->bld", hidden, w_sq[3], preferred_element_type=f32)
    latents_out = residual + lax.psum_scatter(
        ffn_term.astype(jnp.bfloat16), "hid", scatter_dimension=1, tiled=True
    ).astype(jnp.float32)
    grad_all = lax.all_gather(out_grad.astype(bf16), "hid", axis=1, tiled=True)
    grad_w2 = jnp.einsum("bld,blc->dc", grad_all, hidden, preferred_element_type=f32)
    grad_hidden = jnp.einsum("bld,dc->blc", grad_all, w_sq[3], preferred_element_type=f32)
    gelu_exact = partial(jax.nn.gelu, approximate=False)
    up_grad = jax.vjp(gelu_exact, up_proj)[1](grad_hidden)[0].astype(bf16)
    grad_w1 = jnp.einsum("bld,blc->dc", mid_all, up_grad, preferred_element_type=f32)
    mid_term = jnp.einsum("blc,dc->bld", up_grad, w_sq[2], preferred_element_type=f32)
    grad_mid = lax.psum_scatter(mid_term, "hid", scatter_dimension=1, tiled=True)
    grad_residual = out_grad + norm_back(grad_mid, mid_unit, mid_inverse, lat_params[2])
    mid_gain = jnp.sum(grad_mid * mid_unit, (0, 1))
    mid_shift = jnp.sum(grad_mid, (0, 1))
    branch_all = lax.all_gather(grad_residual.astype(bf16), "hid", axis=1, tiled=True)
    grad_wo = jnp.einsum("bld,blc->dc", branch_all, attended, preferred_element_type=f32)
    grad_att = jnp.einsum("bld,dc->blc", branch_all, w_sq[1], preferred_element_type=f32)
    grad_att = grad_att.astype(bf16).reshape(seq_here, lat_total, heads_here, HEAD)
    raw_again = (
        jnp.einsum("lhe,bshe->bhls", query_heads, key_rows, preferred_element_type=f32)
        * score_scale
    )
    probs_again = jnp.exp(raw_again - log_total)
    grad_values = jnp.einsum(
        "bhls,blhe->bshe", probs_again.astype(bf16), grad_att, preferred_element_type=f32
    ).astype(bf16)
    grad_probs = jnp.einsum("blhe,bshe->bhls", grad_att, value_rows, preferred_element_type=f32)
    grad_scores = probs_again * (grad_probs - jnp.sum(probs_again * grad_probs, -1, keepdims=True))
    grad_scores = grad_scores.astype(bf16)
    grad_query = (
        jnp.einsum("bhls,bshe->blhe", grad_scores, key_rows, preferred_element_type=f32)
        * score_scale
    ).astype(bf16)
    grad_keys = (
        jnp.einsum("bhls,lhe->bshe", grad_scores, query_heads, preferred_element_type=f32)
        * score_scale
    ).astype(bf16)
    grad_query = grad_query.reshape(seq_here, lat_total, width_here)
    grad_wq = jnp.einsum("ld,blc->dc", lat_all, grad_query, preferred_element_type=f32)
    lat_term = jnp.einsum("blc,dc->ld", grad_query, w_sq[0], preferred_element_type=f32)
    grad_kv = jnp.stack(
        [grad_keys.reshape(group_rows, width_here), grad_values.reshape(group_rows, width_here)], 1
    )
    grad_kvw = jnp.einsum("td,tkc->kdc", in_all, grad_kv, preferred_element_type=f32)
    input_term = jnp.einsum("tkc,kdc->td", grad_kv, w_kv, preferred_element_type=f32)
    grad_normed, grad_lat_low = (
        lax.psum_scatter(
            input_term.astype(jnp.bfloat16), "hid", scatter_dimension=0, tiled=True
        ).astype(jnp.float32),
        lax.psum_scatter(
            lat_term.astype(jnp.bfloat16), "hid", scatter_dimension=0, tiled=True
        ).astype(jnp.float32),
    )
    grad_masked = norm_back(grad_normed, in_unit, in_inverse, in_params[0])
    inputs_grad = grad_masked * (1.0 - mask_f)
    in_small = jnp.stack(
        [
            jnp.sum(grad_normed * in_unit, 0),
            jnp.sum(grad_normed, 0),
            jnp.sum(grad_masked * mask_f, 0),
        ]
    )
    grad_lat = jnp.sum(grad_residual, 0) + norm_back(
        grad_lat_low, lat_unit, lat_inverse, lat_params[0]
    )
    lat_small = jnp.stack(
        [jnp.sum(grad_lat_low * lat_unit, 0), jnp.sum(grad_lat_low, 0), mid_gain, mid_shift]
    )
    grad_square = jnp.stack([grad_wq, grad_wo, grad_w1, grad_w2])
    sq_part, kv_part, lat_part = (
        lax.psum_scatter(
            grad_square.astype(jnp.bfloat16), "seq", scatter_dimension=1, tiled=True
        ).astype(jnp.float32),
        lax.psum_scatter(
            grad_kvw.astype(jnp.bfloat16), "seq", scatter_dimension=1, tiled=True
        ).astype(jnp.float32),
        lax.psum_scatter(
            grad_lat.astype(jnp.bfloat16), "seq", scatter_dimension=1, tiled=True
        ).astype(jnp.float32),
    )
    big_sum = jnp.sum(sq_part * sq_part) + jnp.sum(kv_part * kv_part) + jnp.sum(lat_part * lat_part)
    big_sum, in_small, lat_small = lax.psum((big_sum, in_small, lat_small), ("seq", "hid"))
    grad_norm = jnp.sqrt(big_sum + jnp.sum(in_small * in_small) + jnp.sum(lat_small * lat_small))
    factor = jnp.minimum(1.0, clip_limit / (grad_norm + 1e-06))
    seq_index = lax.axis_index("seq")
    sq_rows = sq_part.shape[1]
    kv_rows = kv_part.shape[1]
    lat_cols = lat_part.shape[1]
    sq_old = lax.dynamic_slice_in_dim(square, seq_index * sq_rows, sq_rows, 1)
    kv_old = lax.dynamic_slice_in_dim(kv_weights, seq_index * kv_rows, kv_rows, 1)
    lat_old = lax.dynamic_slice_in_dim(latents, seq_index * lat_cols, lat_cols, 1)
    square_new, square_moments = adamw(sq_old, square_state, sq_part * factor)
    kv_new, kv_moments = adamw(kv_old, kv_state, kv_part * factor)
    latents_new, latents_moments = adamw(lat_old, latents_state, lat_part * factor)
    in_clipped = in_small * factor
    lat_clipped = lat_small * factor
    in_new, in_moments = adamw(in_params, in_state, in_clipped)
    lat_new, lat_moments = adamw(lat_params, lat_state, lat_clipped)
    return (
        latents_out,
        inputs_grad,
        grad_norm,
        square_new,
        square_moments,
        kv_new,
        kv_moments,
        latents_new,
        latents_moments,
        in_new,
        in_moments,
        lat_new,
        lat_moments,
        in_clipped,
        lat_clipped,
    )


def solution(mesh):
    return jax.shard_map(
        on_device,
        mesh=mesh,
        in_specs=(
            P(("seq", "hid"), None),
            P(("seq", "hid")),
            P("seq", "hid", None),
            P(None, None, "hid"),
            P(None, None, "seq", "hid"),
            P(None, None, "hid"),
            P(None, None, "seq", "hid"),
            P("hid", None),
            P(None, "hid", "seq"),
            P(),
            P(),
            P(),
            P(),
        ),
        out_specs=(
            P("seq", "hid", None),
            P(("seq", "hid"), None),
            P(),
            P(None, None, "seq", "hid"),
            P(None, None, "seq", "hid"),
            P(None, None, "seq", "hid"),
            P(None, None, "seq", "hid"),
            P(None, "hid", "seq"),
            P(None, "hid", "seq"),
            P(),
            P(),
            P(),
            P(),
            P(),
            P(),
        ),
        check_vma=False,
    )
```

profile of v0, /device:TPU:0, one launch (start us, length us, event | category | flops | bytes accessed | tf_op | source)
XLA Modules:
  0.0 718.0 jit_solution(14368689304800054956)
XLA Ops:
  16.0 4.9 convert_element_type.116
  21.8 17.6 %all_gather.16 = bf16[256,1280]{1,0:T(8,128)(2,1)S(1)} all-gather(bf16[64,1280]{1,0:T(8,128)(2,1)S(1)} %add_convert_fusion.3), channel_id=1, replica_groups=mesh['seq'=8,'hid'=4] {'hid'}, dimensions={0}, use_global_device_ids=true | all-gather | bytes 819200 | tf_op jit(solution)/shard_map/all_gather | solution.py:83
  42.5 50.0 %all-gather.5.cloned.1.call-done = bf16[4096,768]{1,0:T(8,128)(2,1)} async-done(((bf16[1024,768]{1,0:T(8,128)(2,1)}), bf16[4096,768]{1,0:T(8,128)(2,1)}) %all-gather.5.cloned.1.call-update) | async-done | bytes 6291472 | tf_op jit(solution)/shard_map/all_gather | solution.py:82
  92.5 7.6 %convolution_convert_fusion = bf16[4096,2,320]{0,2,1:T(8,128)(2,1)S(1)} fusion(bf16[4096,768]{1,0:T(8,128)(2,1)} %all-gather.5.cloned.1.call-done, f32[2,768,320]{1,2,0:T(8,128)} %param.18), kind=kOutput, calls=%fused_computation.9 | convolution fusion | flops 4029644800 | bytes 13500416 | tf_op jit(solution)/shard_map/td,kdc->tkc/dot_general | solution.py:85
  102.9 5.5 reshape_squeeze.7
  108.3 3.8 bitcast_reduce_fusion
  115.4 5.5 reshape_squeeze.6
  120.9 6.8 fusion.51
  128.4 3.5 fusion.78
  132.4 39.3 %reduce-scatter.9.cloned.1.call-done = f32[2,64,1280]{2,1,0:T(8,128)} async-done(((f32[2,256,1280]{2,1,0:T(8,128)}), f32[2,64,1280]{2,1,0:T(8,128)}) %reduce-scatter.9.cloned.1.call-update) | async-done | bytes 655376 | tf_op jit(solution)/shard_map/reduce_scatter | solution.py:103
  178.2 27.0 %all-gather.7.cloned.1.call-done = bf16[2,256,1280]{2,1,0:T(8,128)(2,1)} async-done(((bf16[2,64,1280]{2,1,0:T(8,128)(2,1)}), bf16[2,256,1280]{2,1,0:T(8,128)(2,1)}) %all-gather.7.cloned.1.call-update) | async-done | bytes 1310736 | tf_op jit(solution)/shard_map/all_gather | solution.py:106
  210.8 25.5 %all-gather.9.cloned.1.call-done = bf16[2,256,1280]{2,1,0:T(8,128)(2,1)} async-done(((bf16[2,64,1280]{2,1,0:T(8,128)(2,1)}), bf16[2,256,1280]{2,1,0:T(8,128)(2,1)}) %all-gather.9.cloned.1.call-update) | async-done | bytes 1310736 | tf_op jit(solution)/shard_map/all_gather | solution.py:113
  239.8 3.5 fusion.79
  246.6 36.4 %reduce-scatter.13.cloned.1.call-done = f32[2,64,1280]{2,1,0:T(8,128)} async-done(((f32[2,256,1280]{2,1,0:T(8,128)}), f32[2,64,1280]{2,1,0:T(8,128)}) %reduce-scatter.13.cloned.1.call-update) | async-done | bytes 655376 | tf_op jit(solution)/shard_map/reduce_scatter | solution.py:120
  285.8 29.9 %reduce-scatter.11.cloned.1.call-done = bf16[2,64,1280]{2,1,0:T(8,128)(2,1)} async-done(((bf16[2,256,1280]{2,1,0:T(8,128)(2,1)}), bf16[2,64,1280]{2,1,0:T(8,128)(2,1)}) %reduce-scatter.11.cloned.1.call-update) | async-done | bytes 327696 | tf_op jit(solution)/shard_map/reduce_scatter | solution.py:110
  315.7 3.6 fusion.133
  325.2 23.1 %all-gather.11.cloned.1.call-done = bf16[2,256,1280]{2,1,0:T(8,128)(2,1)} async-done(((bf16[2,64,1280]{2,1,0:T(8,128)(2,1)}), bf16[2,256,1280]{2,1,0:T(8,128)(2,1)}) %all-gather.11.cloned.1.call-update) | async-done | bytes 1310736 | tf_op jit(solution)/shard_map/all_gather | solution.py:124
  350.6 8.6 %multiply_reduce_fusion = (f32[2,2,256]{2,0,1:T(2,128)S(1)}, f32[2,2,256,2048]{2,3,0,1:T(8,128)S(1)}) fusion(f32[2,2,2048,256]{3,2,1,0:T(8,128)} %copy-done, f32[2,2,256]{2,0,1:T(2,128)S(1)} %log_add_fusion, bf16[2,2048,2,160]{1,0,3,2:T(2,128)(2,1)} %reshape_squeeze.6, bf16[2,256,2,160]{1,3,2,0:T(8,128)(2,1)S(1)} %bitcast.276), kind=kOutput, calls=%fused_computation.8 | convolution fusion | flops 679476224 | bytes 19734528 | tf_op jit(solution)/shard_map/blhe,bshe->bhls/dot_general | solution.py:136
  359.2 3.4 fusion.23
  372.3 6.0 copy.83
  378.2 5.5 stack_reshape.7
  383.7 6.0 copy.81
  389.7 5.5 stack_reshape.6
  402.3 8.0 %fusion.43 = bf16[2,768,320]{1,2,0:T(8,128)(2,1)} fusion(bf16[4096,2,320]{0,2,1:T(8,128)(2,1)S(1)} %constant_dynamic-update-slice_fusion, bf16[4096,768]{1,0:T(8,128)(2,1)} %all-gather.5.cloned.1.call-done), kind=kOutput, calls=%fused_computation.65 | convolution fusion | flops 4027023360 | bytes 12517376 | tf_op jit(solution)/shard_map/td,tkc->kdc/dot_general | solution.py:153
  416.0 3.3 pad_maximum_fusion
  419.2 7.8 %copy.86 = bf16[4,1280,320]{2,0,1:T(4,128)(2,1)} copy(bf16[4,1280,320]{1,2,0:T(8,128)(2,1)} %pad_maximum_fusion) | data formatting | bytes 6553600 | tf_op jit(solution)/shard_map/stack | solution.py:178
  427.1 4.7 copy.87
  431.8 9.4 %bitcast_convert_fusion = bf16[4096,768]{1,0:T(8,128)(2,1)} fusion(bf16[4096,2,320]{0,2,1:T(8,128)(2,1)} %copy-done.17, f32[2,768,320]{1,2,0:T(8,128)} %param.18), kind=kOutput, calls=%fused_computation | convolution fusion | flops 4030169088 | bytes 13500416 | tf_op jit(solution)/shard_map/tkc,kdc->td/dot_general | solution.py:154
  456.7 105.0 %all-reduce.6.cloned.1.call-done = (bf16[4,1280,320]{2,0,1:T(4,128)(2,1)}, bf16[2,768,320]{2,0,1:T(2,128)(2,1)}) async-done(((bf16[4,1280,320]{2,0,1:T(4,128)(2,1)}, bf16[2,768,320]{2,0,1:T(2,128)(2,1)}), (bf16[4,1280,320]{2,0,1:T(4,128)(2,1)}, bf16[2,768,320]{2,0,1:T(2,128)(2,1)})) %all-reduce.6.cloned.1.call-update) | async-done | bytes 4259856
  567.6 67.7 %reduce-scatter.15.cloned.1.call-done = bf16[1024,768]{1,0:T(8,128)(2,1)} async-done(((bf16[4096,768]{1,0:T(8,128)(2,1)}), bf16[1024,768]{1,0:T(8,128)(2,1)}) %reduce-scatter.15.cloned.1.call-update) | async-done | bytes 1572880 | tf_op jit(solution)/shard_map/reduce_scatter | solution.py:156
  644.0 40.2 %all-reduce.2 = (f32[]{:T(128)}, f32[3,768]{1,0:T(4,128)S(1)}, f32[4,1280]{1,0:T(4,128)S(1)}) all-reduce(f32[]{:T(128)S(6)} %add.248, f32[3,768]{1,0:T(4,128)S(1)} %pad_maximum_fusion.12, f32[4,1280]{1,0:T(4,128)} %pad_maximum_fusion.11), channel_id=1, replica_groups=mesh['seq'=8,'hid'=4] {'seq','hid'}, use_global_device_ids=true, to_apply=%region_28.0 | all-reduce | flops 7425 | bytes 59400 | tf_op jit(solution)/shard_map/psum | solution.py:191
  697.0 4.1 fusion.77
  (198 shorter events, 118.3 us)
Async XLA Ops:
  7.2 5.0 copy-start.1
  7.2 85.3 %all-gather.5.cloned.1.call-start = ((), (), s32[]{:S(2)}) async-start(), calls=%async_computation.6 | async-start | bytes 7864320 | tf_op jit(solution)/shard_map/all_gather | solution.py:82
  15.9 5.0 copy-start.2
  15.9 5.1 copy-start.26
  15.9 155.8 %reduce-scatter.9.cloned.1.call-start = ((), (), s32[]{:S(2)}) async-start(), calls=%async_computation.7 | async-start | bytes 3276800 | tf_op jit(solution)/shard_map/reduce_scatter | solution.py:103
  132.0 73.3 %all-gather.7.cloned.1.call-start = ((), (), s32[]{:S(2)}) async-start(), calls=%async_computation.8 | async-start | bytes 1638400 | tf_op jit(solution)/shard_map/all_gather | solution.py:106
  174.2 33.3 %copy-start.30 = (f32[2,64]{1,0:T(2,128)}, f32[2,64]{1,0:T(2,128)S(1)}, u32[]{:S(2)}) copy-start(f32[2,64]{1,0:T(2,128)S(1)} %add_rsqrt_fusion.1) | copy-start | bytes 1540
  176.3 60.1 %all-gather.9.cloned.1.call-start = ((), (), s32[]{:S(2)}) async-start(), calls=%async_computation.10 | async-start | bytes 1638400 | tf_op jit(solution)/shard_map/all_gather | solution.py:113
  178.2 104.8 %reduce-scatter.13.cloned.1.call-start = ((), (), s32[]{:S(2)}) async-start(), calls=%async_computation.11 | async-start | bytes 3276800 | tf_op jit(solution)/shard_map/reduce_scatter | solution.py:120
  243.3 39.8 %copy-start.31 = (f32[2,64]{1,0:T(2,128)S(1)}, f32[2,64]{1,0:T(2,128)}, u32[]{:S(2)}) copy-start(f32[2,64]{1,0:T(2,128)} %copy-done.30) | copy-start | bytes 1540
  243.3 72.4 %reduce-scatter.11.cloned.1.call-start = ((), (), s32[]{:S(2)}) async-start(), calls=%async_computation.9 | async-start | bytes 1638400 | tf_op jit(solution)/shard_map/reduce_scatter | solution.py:110
  246.6 101.7 %all-gather.11.cloned.1.call-start = ((), (), s32[]{:S(2)}) async-start(), calls=%async_computation.12 | async-start | bytes 1638400 | tf_op jit(solution)/shard_map/all_gather | solution.py:124
  319.3 91.0 %reduce-scatter.17.cloned.1.call-start = ((), (), s32[]{:S(2)}) async-start(), calls=%async_computation.14 | async-start | bytes 819200 | tf_op jit(solution)/shard_map/reduce_scatter | solution.py:159
  348.3 10.9 %slice-start = ((s8[8388608]{0:T(1024)(128)(4,1)}), s8[4194304]{0:T(1024)(128)(4,1)S(1)}, s32[]{:S(2)}) async-start(s8[8388608]{0:T(1024)(128)(4,1)} %bitcast.270), calls=%async_computation.17 | async-start | bytes 8388608
  350.6 8.6 %slice-start.1 = ((s8[8388608]{0:T(1024)(128)(4,1)}), s8[4194304]{0:T(1024)(128)(4,1)S(1)}, s32[]{:S(2)}) async-start(s8[8388608]{0:T(1024)(128)(4,1)} %bitcast.270), calls=%async_computation.18 | async-start | bytes 8388608
  372.0 83.1 %reduce-scatter.19.cloned.1.call-start = ((), (), s32[]{:S(2)}) async-start(), calls=%async_computation.15 | async-start | bytes 368640
  397.7 3.3 copy-start.13
  397.8 3.3 copy-start.24
  402.3 8.0 %copy-start.33 = (f32[64]{0:T(128)S(1)}, f32[64]{0:T(128)}, u32[]{:S(2)}) copy-start(f32[64]{0:T(128)} %copy-done.32) | copy-start | bytes 772
  402.3 8.0 %copy-start.35 = (f32[64]{0:T(128)S(1)}, f32[64]{0:T(128)}, u32[]{:S(2)}) copy-start(f32[64]{0:T(128)} %copy-done.34) | copy-start | bytes 772
  415.7 145.9 %all-reduce.6.cloned.1.call-start = ((), (), s32[]{:S(2)}) async-start(), calls=%async_computation.16 | async-start | bytes 10223616
  431.8 203.4 %reduce-scatter.15.cloned.1.call-start = ((), (), s32[]{:S(2)}) async-start(), calls=%async_computation.13 | async-start | bytes 7864320 | tf_op jit(solution)/shard_map/reduce_scatter | solution.py:156
  447.6 5.2 copy-start.11
  635.2 3.2 copy-start.6
  641.6 50.2 %copy-start.22 = (f32[3,64,160]{2,1,0:T(8,128)S(1)}, f32[3,64,160]{2,1,0:T(8,128)}, u32[]{:S(2)}) copy-start(f32[3,64,160]{2,1,0:T(8,128)} %param.21) | copy-start | bytes 368644
  641.6 50.3 %copy-start.19 = (f32[1,2,96,320]{3,2,1,0:T(8,128)S(1)}, f32[1,2,96,320]{3,2,1,0:T(8,128)}, u32[]{:S(2)}) copy-start(f32[1,2,96,320]{3,2,1,0:T(8,128)} %get-tuple-element.116) | copy-start | bytes 737284
  688.2 7.9 %copy-start.25 = (f32[4,1280]{1,0:T(4,128)}, f32[4,1280]{1,0:T(4,128)S(1)}, u32[]{:S(2)}) copy-start(f32[4,1280]{1,0:T(4,128)S(1)} %get-tuple-element.87) | copy-start | bytes 61444
  689.7 6.3 copy-start.27
  691.9 5.0 copy-start.7
  691.9 5.0 copy-start.8
  691.9 5.0 copy-start.9
  691.9 5.0 copy-start.10
  (18 other events, 29.0 us)
Sparse Core Ops, SparseCore 0:
  16.0 76.4 all-gather.4
  132.1 39.5 reduce-scatter.8
  176.4 28.7 all-gather.6
  207.5 28.7 all-gather.8
  243.4 39.5 reduce-scatter.12
  286.4 29.2 reduce-scatter.10
  319.5 28.7 all-gather.10
  372.2 25.4 reduce-scatter.16
  415.8 30.5 reduce-scatter.18
  449.3 112.3 all-reduce.5
  564.9 70.2 reduce-scatter.14
where the time goes:
time: 723 us; the launch traced here: 718 us
  waiting for transfers between devices  404 us (56%)
  matrix products  83.7 us (12%)
  local copies, waits for them, and re-layouts  79.2 us (11%)
  other arithmetic  70.8 us (10%)
  blocking collectives  57.8 us (8%)
  between operations  21.1 us (3%)
    unnamed x13, waiting for transfers between devices  105 us
    reduce_scatter x1, waiting for transfers between devices, on_device(): lax.psum_scatter(input_term.astype(jnp.bfloat16), 'hid', scatter_dimensio...  67.7 us
    all_gather x1, waiting for transfers between devices, on_device(): lax.all_gather(in_low, 'hid', axis=0, tiled=True)  50 us
    psum x1, blocking collectives, on_device(): lax.psum((big_sum, in_small, lat_small), ('seq', 'hid'))  40.2 us
    reduce_scatter x1, waiting for transfers between devices, on_device(): lax.psum_scatter(branch_term, 'hid', scatter_dimension=1, tiled=True)  39.3 us
    reduce_scatter x1, waiting for transfers between devices, on_device(): lax.psum_scatter(mid_term, 'hid', scatter_dimension=1, tiled=True)  36.4 us
    reduce_scatter x1, waiting for transfers between devices, on_device(): lax.psum_scatter(ffn_term.astype(jnp.bfloat16), 'hid', scatter_dimension=...  29.9 us
    all_gather x1, waiting for transfers between devices, on_device(): mid_all = lax.all_gather(mid_normed.astype(bf16), 'hid', axis=1, tiled=True)  27 us
  transfers between devices with their start and end apart: 11, of which 9 were waited for; matrix products, arithmetic and copies ran while one was open for 15% of the time, Pallas kernels for 0%

commit v1 on v0

v1 whole, which is shorter than its diff:
```python
from functools import partial as fix
import math

import jax
import jax.numpy as jnp
from jax import lax
from jax.experimental import pallas as pl
from jax.experimental.pallas import tpu as pltpu
from jax.sharding import PartitionSpec as P

HEADS = 8
HEAD = 160
SEQ_LEN = 2048
STEP = 10
SIDE = 128


clip_limit = 1.0
beta_one = 0.9
beta_two = 0.999
adam_eps = 1e-08
learn_rate = 0.05
decay_rate = 0.01
ema_keep = 0.9
norm_eps = 1e-05
score_scale = 1.0 / math.sqrt(HEAD)
score_two = score_scale * math.log2(math.e)

f32 = jnp.float32
bf16 = jnp.bfloat16


def unit_norm(values):
    centre = jnp.mean(values, -1, keepdims=True)
    centred = values - centre
    inverse = lax.rsqrt(jnp.mean(centred * centred, -1, keepdims=True) + norm_eps)
    return centred * inverse, inverse


def norm_back(upstream, unit_rows, inverse, scale_row):
    scaled = upstream * scale_row
    inner_mean = jnp.mean(scaled, -1, keepdims=True)
    along_mean = jnp.mean(scaled * unit_rows, -1, keepdims=True)
    return inverse * (scaled - inner_mean - unit_rows * along_mean)


def adam_step(weight, first, root, average, gradient):
    moment_one = beta_one * first + (1.0 - beta_one) * gradient
    root_two = jnp.sqrt(beta_two * root * root + (1.0 - beta_two) * gradient * gradient)
    corrected_one = moment_one / (1.0 - beta_one**STEP)
    denominator = root_two / math.sqrt(1.0 - beta_two**STEP) + adam_eps
    new_weight = weight - learn_rate * (corrected_one / denominator + decay_rate * weight)
    ema_new = ema_keep * average + (1.0 - ema_keep) * new_weight
    return new_weight, ema_new, moment_one, root_two


def dot(a, b, over_a, over_b):
    return lax.dot_general(a, b, (((over_a,), (over_b,)), ((), ())), preferred_element_type=f32)


def flip(value, bits):
    out = 0
    for i in range(bits):
        out = out + ((value >> i) & 1) * (1 << (bits - 1 - i))
    return out


class Links:
    def __init__(self):
        self.S = lax.axis_size("seq")
        self.H = lax.axis_size("hid")
        self.hb = self.H.bit_length() - 1
        self.sb = self.S.bit_length() - 1
        self.s = lax.axis_index("seq")
        self.j = lax.axis_index("hid")
        self.core = self.s & 1

    def swap(self, x, dest):
        pairs = []
        for s in range(self.S):
            for j in range(self.H):
                ds, dj = dest(s, j)
                pairs.append((s * self.H + j, ds * self.H + dj))
        return lax.ppermute(x, ("seq", "hid"), pairs)

    def swap_core(self, x):
        return self.swap(x, lambda s, j: (s ^ 1, j))

    def swap_hid(self, x, mask):
        return self.swap(x, lambda s, j: (s, j ^ mask))

    def swap_seq(self, x, mask):
        return self.swap(x, lambda s, j: (s ^ mask, j))

    def swap_step(self, x, i):
        even, odd = 1 << i, 1 << (self.hb - 1 - i)
        return self.swap(x, lambda s, j: (s, j ^ (odd if s & 1 else even)))

    def spread(self, first):
        blocks = [None]
        for i, x in enumerate(first):
            blocks += [x] + [self.swap_step(y, i) for y in blocks[1:]]
        return blocks[1:]

    def near(self, x):
        return [self.swap_hid(x, m) for m in range(1, self.H)]

    def sum_all(self, x):
        x = x + self.swap_core(x)
        for i in range(self.hb):
            x = x + self.swap_hid(x, 1 << i)
        for i in range(1, self.sb):
            x = x + self.swap_seq(x, 1 << i)
        return x


class Place:
    def __init__(self, where, H):
        self.H = H
        self.hb = H.bit_length() - 1
        self.s = where[0]
        self.j = where[1]
        self.core = self.s & 1

    def block(self, r, core):
        return self.j ^ jnp.where(core == 0, r, flip(r, self.hb))

    def halves(self):
        mine = [(self.block(r, self.core), self.core) for r in range(self.H)]
        return mine + [(self.block(r, 1 - self.core), 1 - self.core) for r in range(self.H)]


def after(x, *others):
    return lax.optimization_barrier((x, others))[0]


def rows_at(index, size):
    return pl.ds(pl.multiple_of(index * size, size), size)


VMEM = pl.BlockSpec(memory_space=pltpu.VMEM)
SMEM = pl.BlockSpec(memory_space=pltpu.SMEM)
ANY = pl.BlockSpec(memory_space=pl.ANY)


spent = {
    "kv_weight": 2.6,
    "token_norm": 5.0,
    "other_weights": 4.7,
    "kv": 10.0,
    "attention": 8.0,
    "latent": 11.0,
    "square_send": 5.0,
    "square_keep": 5.0,
    "square_top": 6.0,
    "square_step": 4.0,
    "square_turn": 4.0,
    "attention_back": 12.0,
    "kv_send": 6.5,
    "kv_keep": 6.5,
    "token_grad": 4.0,
    "update": 7.0,
}


class Order:
    def __init__(self, where):
        self.where = where
        self.last = []

    def __call__(
        self, kernel, args, outs, scratch=(), name=None, grid=(), in_specs=None, out_specs=None, after=(), onto=None
    ):
        n = len(args)
        waits = self.last + list(after)
        if onto is not None:
            waits = [onto] + waits

        def body(where, *refs):
            kernel(where, *refs[:n], *refs[n + len(waits) :])

        results = pl.pallas_call(
            body,
            out_shape=outs,
            grid=grid,
            in_specs=[SMEM] + (in_specs or [VMEM] * n) + [ANY] * len(waits),
            out_specs=out_specs or [VMEM] * len(outs),
            scratch_shapes=list(scratch),
            compiler_params=pltpu.CompilerParams(vmem_limit_bytes=56 * 1024 * 1024),
            cost_estimate=pl.CostEstimate(
                flops=int(spent.get(name, 2.0) * 3e9), bytes_accessed=0, transcendentals=0
            ),
            name=name,
            input_output_aliases={} if onto is None else {1 + n: 0},
        )(self.where, *args, *waits)
        self.last = [results[0]]
        return results

    def add(self, terms, block, count, name):
        shape = terms[0].shape[1:]
        parts = shape[0] if len(shape) == 3 else 1
        terms = [x.reshape((x.shape[0], parts) + shape[-2:]) for x in terms]

        def kernel(where, *refs):
            out = refs[-1]
            acc = refs[0][...].astype(f32)
            for x in refs[1:-1]:
                acc = acc + x[...].astype(f32)
            out[...] = acc.astype(bf16)

        size = (1, 1) + shape[-2:]
        (out,) = self(
            kernel,
            terms,
            [like((count, parts) + shape[-2:], bf16)],
            name=name,
            grid=(count, parts),
            in_specs=[pl.BlockSpec(size, lambda i, m: (block * count + i, m, 0, 0))] * len(terms),
            out_specs=[pl.BlockSpec(size, lambda i, m: (i, m, 0, 0))],
        )
        return out.reshape((count,) + shape)


def like(shape, dtype):
    return jax.ShapeDtypeStruct(tuple(shape), dtype)


class Halving:
    def __init__(self, go, top, low, bits, swap, name):
        self.go, self.top, self.terms, self.bits, self.swap, self.name = go, top, low, bits, swap, name

    def start(self):
        i = self.bits - 1
        sending = self.top[0] if len(self.top) == 1 else self.go.add(self.top, 0, 1 << i, self.name + "_top")
        self.terms = self.terms + [self.swap(sending, i)]
        self.at = i

    def step(self):
        n = 1 << (self.at - 1)
        sending = self.go.add(self.terms, 1, n, self.name + "_step")
        self.at -= 1
        self.terms = self.terms + [self.swap(sending, self.at)]


def lat_kernel(where, latents, lat_params, out):
    unit, _ = unit_norm(latents[...])
    out[...] = (unit * lat_params[0:1, :] + lat_params[1:2, :]).astype(bf16)


def kv_weight_kernel(H, where, kv, mine, other):
    at = Place(where, H)
    mine[...] = kv[at.core].astype(bf16)
    other[...] = kv[1 - at.core].astype(bf16)


def first_weight_kernel(where, weight, out):
    out[...] = weight[0].astype(bf16)


def other_weight_kernel(H, where, weight, mine, other):
    at = Place(where, H)
    n = mine.shape[1]
    mine[0] = weight[0, rows_at(at.core, n), :].astype(bf16)
    other[0] = weight[0, rows_at(1 - at.core, n), :].astype(bf16)


def query_kernel(H, where, *refs):
    near, (w0, lat_all, mine, other, turned) = refs[:H], refs[H:]
    at = Place(where, H)
    n = near[0].shape[0]
    for m, x in enumerate(near):
        lat_all[rows_at(at.j ^ m, n), :] = x[...]
    turned[...] = dot(w0[...], lat_all[...], 1, 1).astype(bf16)
    half_wide = mine.shape[0]
    mine[...] = turned[rows_at(at.core, half_wide), :]
    other[...] = turned[rows_at(1 - at.core, half_wide), :]


def token_kernel(where, inputs, mask, in_params, out, turned):
    masked = jnp.where(mask[...] > 0, in_params[2:3, :], inputs[...])
    unit, _ = unit_norm(masked)
    low = (unit * in_params[0:1, :] + in_params[1:2, :]).astype(bf16)
    out[...] = low
    turned[...] = low.T


def kv_kernel(H, where, in_turned, *refs):
    halves, (kv, weights, sems) = refs[: 2 * H], refs[2 * H :]
    at = Place(where, H)
    wide = halves[0].shape[0]
    d_lat = wide * H
    copies = []
    for i, (block, which) in enumerate(at.halves()):
        copies.append(pltpu.make_async_copy(halves[i], weights.at[which, rows_at(block, wide), :], sems.at[i]))
        copies[-1].start()
    for copy in copies:
        copy.wait()
    for which in range(2):
        kv[which] = dot(weights[which], in_turned[...], 1, 0).astype(bf16)


def three_way(x, lane):
    a = x.astype(bf16).astype(f32)
    b = (x - a).astype(bf16).astype(f32)
    part = (lane // HEADS) % 3
    return jnp.where(part == 0, a, jnp.where(part == 1, b, x - a - b)).astype(bf16)


def three_sum(x):
    return x + pltpu.roll(x, SIDE - HEADS, 1) + pltpu.roll(x, SIDE - 2 * HEADS, 1)


def attention_kernel(H, where, *refs):
    halves, kv, query = refs[: 2 * H], refs[2 * H], refs[2 * H + 1]
    packs, mix, packed = refs[2 * H + 2 : -2], refs[-2], refs[-1]
    at = Place(where, H)
    n = halves[0].shape[0]
    for i, x in enumerate(halves):
        half = at.core if i < H else 1 - at.core
        query[rows_at((at.j ^ (i % H)) * 2 + half, n), :] = x[...]
    d_lat, nlat = query.shape
    lane = lax.broadcasted_iota(jnp.int32, (nlat, SIDE), 1)
    logs = jnp.zeros((nlat, SIDE), f32)
    for h in range(HEADS):
        span = slice(h * HEAD, (h + 1) * HEAD)
        scores = dot(query[span, :], kv[0, span, :], 0, 0)
        peak = jnp.max(scores, -1, keepdims=True)
        weight = jnp.exp2((scores - peak) * score_two)
        total = jnp.sum(weight, -1, keepdims=True)
        probs = (weight * (1.0 / total)).astype(bf16)
        mix[span, :] = dot(kv[1, span, :], probs, 1, 1)
        log_part = peak * score_two + jnp.log2(total)
        logs = jnp.where((lane % HEADS == h) & (lane < 3 * HEADS), log_part, logs)
    packed[:, :d_lat] = mix[...].T.astype(bf16)
    packed[:, d_lat:] = three_way(logs, lane)
    lat_rows = nlat // H
    for m, out in enumerate(packs):
        out[...] = packed[rows_at(at.j ^ m, lat_rows), :]


def head_lanes(shape):
    return lax.broadcasted_iota(jnp.int32, shape, 1) // HEAD


def latent_kernel(H, parts, where, *refs):
    seqs = H // parts
    got, refs = refs[:H], refs[H:]
    latents, out_grad, lat_params, refs = refs[0], refs[1], refs[2], refs[3:]
    pieces, refs = refs[: 2 * H], refs[2 * H :]
    (latents_out, attended, branch_grad, up_grad, mid_low, hidden, grad_y, small, res_sum), refs = refs[:9], refs[9:]
    backs, (weights, sems, gathered, att, packed) = refs[:H], refs[H:]
    at = Place(where, H)
    lat_rows, d_lat = latents.shape
    half_wide = pieces[0].shape[1]
    copies = []
    for m in range(3):
        group = []
        for i, (block, half) in enumerate(at.halves()):
            group.append(
                pltpu.make_async_copy(
                    pieces[i].at[m],
                    weights.at[m, rows_at(block * 2 + half, half_wide), :],
                    sems.at[m, i],
                )
            )
            group[-1].start()
        copies.append(group)

    def arrived(m):
        for copy in copies[m]:
            copy.wait()

    for m in range(H):
        gathered[at.j ^ m] = got[m][...]
    heads = head_lanes((lat_rows, d_lat))
    log_totals = []
    for b in range(seqs):
        logs = [three_sum(gathered[b * parts + p, :, d_lat:].astype(f32)) for p in range(parts)]
        peak = logs[0]
        for x in logs[1:]:
            peak = jnp.maximum(peak, x)
        log_total = peak + jnp.log2(sum(jnp.exp2(x - peak) for x in logs))
        log_totals.append(log_total)
        mixed = jnp.zeros((lat_rows, d_lat), f32)
        for p in range(parts):
            share = jnp.exp2(logs[p] - log_total)
            spread = jnp.zeros((lat_rows, d_lat), f32)
            for h in range(HEADS):
                spread = jnp.where(heads == h, share[:, h : h + 1], spread)
            mixed = mixed + spread * gathered[b * parts + p, :, :d_lat].astype(f32)
        att[b * lat_rows : (b + 1) * lat_rows, :] = mixed
    attended[...] = att[...].astype(bf16)
    grad_y[...] = jnp.concatenate([out_grad[b] for b in range(seqs)], 0).astype(bf16)

    arrived(0)
    branch = dot(attended[...], weights[0], 1, 0)
    residual = jnp.concatenate([latents[...]] * seqs, 0) + branch
    unit, inverse = unit_norm(residual)
    mid_low[...] = (unit * lat_params[2:3, :] + lat_params[3:4, :]).astype(bf16)
    arrived(1)
    up_proj = dot(mid_low[...], weights[1], 1, 1)
    below = 0.5 + 0.5 * lax.erf(up_proj * math.sqrt(0.5))
    hidden[...] = (up_proj * below).astype(bf16)
    slope = below + up_proj * jnp.exp(-0.5 * up_proj * up_proj) * (1.0 / math.sqrt(2.0 * math.pi))
    arrived(2)
    latents_out[...] = residual + dot(hidden[...], weights[2], 1, 0)
    up_grad[...] = (dot(grad_y[...], weights[2], 1, 1) * slope).astype(bf16)
    grad_mid = dot(up_grad[...], weights[1], 1, 0)
    small[0:1, :] = jnp.sum(grad_mid * unit, 0, keepdims=True)
    small[1:2, :] = jnp.sum(grad_mid, 0, keepdims=True)
    grad_residual = jnp.concatenate([out_grad[b] for b in range(seqs)], 0) + norm_back(
        grad_mid, unit, inverse, lat_params[2:3, :]
    )
    branch_grad[...] = grad_residual.astype(bf16)
    folded = grad_residual[0:lat_rows]
    for b in range(1, seqs):
        folded = folded + grad_residual[b * lat_rows : (b + 1) * lat_rows]
    res_sum[...] = folded.astype(bf16)
    grad_att = dot(branch_grad[...], weights[0], 1, 1).astype(bf16)
    along = grad_att.astype(f32) * att[...]
    heads = head_lanes((seqs * lat_rows, d_lat))
    lane = lax.broadcasted_iota(jnp.int32, (lat_rows, SIDE), 1)
    inner = []
    for h in range(HEADS):
        lo, hi = h * HEAD // 128 * 128, -(-(h + 1) * HEAD // 128) * 128
        inner.append(jnp.sum(jnp.where(heads[:, lo:hi] == h, along[:, lo:hi], 0.0), -1, keepdims=True))
    for b in range(seqs):
        t = log_totals[b]
        side = jnp.where(lane < HEADS, t, jnp.where(lane < 2 * HEADS, pltpu.roll(t, HEADS, 1), pltpu.roll(t, 2 * HEADS, 1)))
        for h in range(HEADS):
            own = (lane % HEADS == h) & (lane >= 3 * HEADS)
            side = jnp.where(own, inner[h][b * lat_rows : (b + 1) * lat_rows], side)
        side = jnp.where(lane < 6 * HEADS, side, 0.0)
        packed[b, :, :d_lat] = grad_att[b * lat_rows : (b + 1) * lat_rows]
        packed[b, :, d_lat:] = three_way(side, lane)
    for m, out in enumerate(backs):
        out[...] = packed[(at.j ^ m) // parts]


def square_grad_kernel(H, keep, where, *refs):
    lefts, rights = refs[:3], refs[3:6]
    top, low, turned = refs[6:]
    at = Place(where, H)
    core = at.core if keep else 1 - at.core
    for m in range(3):
        turned[m] = lefts[m][...].T
    half_wide = top.shape[2]
    for r in range(H):
        out = low if r < H // 2 else top
        at_row = rows_at(at.block(r, core) * 2 + core, half_wide)
        for m in range(3):
            out[r % (H // 2), m] = dot(turned[m, at_row, :], rights[m][...], 1, 0).astype(bf16)


def attention_back_kernel(H, where, query, kv, *refs):
    backs, refs = refs[:H], refs[H:]
    grad_kv, send_top, send_low, keep_top, keep_low, packed, turned, grad_q = refs
    at = Place(where, H)
    d_lat, nlat = query.shape
    lat_rows = nlat // H
    for m in range(H):
        packed[rows_at(at.j ^ m, lat_rows), :] = backs[m][...]
    turned[...] = packed[:, :d_lat].T
    side = three_sum(packed[:, d_lat:].astype(f32))
    for h in range(HEADS):
        span = slice(h * HEAD, (h + 1) * HEAD)
        scores = dot(query[span, :], kv[0, span, :], 0, 0)
        probs = jnp.exp2(scores * score_two - side[:, h : h + 1])
        grad_kv[1, span, :] = dot(turned[span, :], probs.astype(bf16), 1, 0).astype(bf16)
        grad_probs = dot(turned[span, :], kv[1, span, :], 0, 0)
        grad_scores = (probs * (grad_probs - side[:, 3 * HEADS + h : 3 * HEADS + h + 1])).astype(bf16)
        grad_q[span, :] = (dot(kv[0, span, :], grad_scores, 1, 1) * score_scale).astype(bf16)
        grad_kv[0, span, :] = (dot(query[span, :], grad_scores, 1, 0) * score_scale).astype(bf16)
    slots_out(at, 1 - at.core, grad_q, send_top, send_low)
    slots_out(at, at.core, grad_q, keep_top, keep_low)


def slots_out(at, core, whole, top, low):
    n = top.shape[1]
    per = whole.shape[0] // (at.H * n)
    for r in range(at.H):
        out = low if r < at.H // 2 else top
        block = at.block(r, core)
        out[r % (at.H // 2)] = whole[rows_at(block * 2 + core if per == 2 else block, n), :]


def kv_grad_kernel(H, keep, where, grad_kv, in_low, top, low, whole):
    at = Place(where, H)
    core = at.core if keep else 1 - at.core
    whole[...] = dot(grad_kv[core], in_low[...], 1, 0).astype(bf16)
    slots_out(at, core, whole, top, low)


def token_grad_kernel(where, inputs, mask, in_params, grad_kv, weights, inputs_grad, small, normed):
    normed[...] = dot(grad_kv[0], weights[0], 0, 0) + dot(grad_kv[1], weights[1], 0, 0)
    rows, d_in = inputs.shape
    step = min(rows, 128)
    small[...] = jnp.zeros_like(small)
    for i in range(rows // step):
        span = slice(i * step, (i + 1) * step)
        masked_row = mask[span, :] > 0
        unit, inverse = unit_norm(jnp.where(masked_row, in_params[2:3, :], inputs[span, :]))
        upstream = normed[span, :]
        grad = norm_back(upstream, unit, inverse, in_params[0:1, :])
        inputs_grad[span, :] = jnp.where(masked_row, 0.0, grad)
        for r, term in enumerate((upstream * unit, upstream, jnp.where(masked_row, grad, 0.0))):
            small[0, r : r + 1, :] += jnp.sum(term, 0, keepdims=True)


def turn(where, total, turned, top, low):
    turned[...] = total[...].T.astype(bf16)
    chip = where[0] >> 1
    half, rows, lanes = top.shape
    for r in range(2 * half):
        out = low if r < half else top
        out[r % half] = turned[rows_at(chip ^ flip(r, half.bit_length()), rows), 0:lanes]


def square_turn_kernel(where, *refs):
    terms, (lat_mine, lat_other, top, low, total, turned) = refs[:-6], refs[-6:]
    half = terms[0].shape[2]
    for m in range(3):
        acc = terms[0][0, m].astype(f32)
        for x in terms[1:]:
            acc = acc + x[0, m].astype(f32)
        total[m * half : (m + 1) * half, :] = acc
    n = lat_mine.shape[0]
    total[3 * half : 3 * half + n, :] = lat_mine[...].astype(f32) + lat_other[...].astype(f32)
    if 3 * half + n < total.shape[0]:
        total[3 * half + n :, :] = jnp.zeros((total.shape[0] - 3 * half - n, total.shape[1]), f32)
    turn(where, total, turned, top, low)


def kv_turn_kernel(where, *refs):
    terms, (top, low, total, turned) = refs[:-4], refs[-4:]
    acc = terms[0][0].astype(f32)
    for x in terms[1:]:
        acc = acc + x[0].astype(f32)
    total[...] = acc
    turn(where, total, turned, top, low)


def first_blocks(terms):
    return [pl.BlockSpec((1,) + x.shape[1:], lambda i, z=(0,) * x.ndim: z) for x in terms]


def whole_blocks(arrays):
    return [pl.BlockSpec(x.shape, lambda i, z=(0,) * len(x.shape): z) for x in arrays]


def halve_end_kernel(where, *refs):
    terms, (mine, other, total) = refs[:-3], refs[-3:]
    core = where[0] & 1
    acc = terms[0][0].astype(f32)
    for x in terms[1:]:
        acc = acc + x[0].astype(f32)
    total[...] = acc
    n = mine.shape[0]
    mine[...] = total[rows_at(core, n), :]
    other[...] = total[rows_at(1 - core, n), :].astype(bf16)


def latent_end_kernel(where, mine, other, latents, lat_params, extra, small, turned):
    core = where[0] & 1
    first, second = mine[...].astype(f32), other[...].astype(f32)
    low = jnp.concatenate([jnp.where(core == 0, first, second), jnp.where(core == 0, second, first)], 0)
    unit, inverse = unit_norm(latents[...])
    once = jnp.where(where[0] == 0, 1.0, 0.0)
    small[0:1, :] = jnp.sum(low * unit, 0, keepdims=True) * once
    small[1:2, :] = jnp.sum(low, 0, keepdims=True) * once
    turned[...] = norm_back(low, unit, inverse, lat_params[0:1, :]).T
    extra[...] = turned[rows_at(where[0], extra.shape[0]), :]


def core_rows_kernel(where, pair, mine, other):
    core = where[0] & 1
    n = mine.shape[0]
    mine[...] = pair[rows_at(core, n), :]
    other[...] = pair[rows_at(1 - core, n), :]


def update_kernel(count, where, sums, *refs):
    ins, outs = refs[: 3 * (count - 2) + 4], refs[3 * (count - 2) + 4 :]
    small = sums[0:7, :]
    squares = jnp.sum(jnp.sum(small * small, 1, keepdims=True), 0, keepdims=True) + sums[7:8, 0:1]
    norm = jnp.sqrt(squares)
    outs[0][...] = norm
    factor = jnp.minimum(1.0, clip_limit / (norm + 1e-06))
    for i in range(count - 2):
        weight, state, gradient = ins[3 * i : 3 * i + 3]
        new, moments = outs[1 + 2 * i : 3 + 2 * i]
        scale = factor if gradient.ndim == 2 else factor[None]
        new[0], new[1], moments[0], moments[1] = adam_step(
            weight[...], state[0], state[1], state[2], gradient[...] * scale
        )
    lat_params, lat_state, in_params, in_state = ins[-4:]
    lat_new, lat_moments, in_new, in_moments, lat_clipped, in_clipped = outs[1 + 2 * (count - 2) :]
    lat_clipped[...] = sums[0:4, :] * factor
    lat_new[0], lat_new[1], lat_moments[0], lat_moments[1] = adam_step(
        lat_params[...], lat_state[0], lat_state[1], lat_state[2], lat_clipped[...]
    )
    in_clipped[...] = sums[4:7, 0 : in_params.shape[1]] * factor
    results = adam_step(in_params[...], in_state[0], in_state[1], in_state[2], in_clipped[...])
    for i in range(3):
        row = slice(i, i + 1)
        in_new[i, 0:1], in_new[i, 1:2], in_moments[i, 0:1], in_moments[i, 1:2] = (x[row] for x in results)


def query_back_kernel(H, where, lat_all, w0, mine, other, wq, top, low, grad_q, whole, term):
    at = Place(where, H)
    half_wide = mine.shape[0]
    grad_q[rows_at(at.core, half_wide), :] = mine[...]
    grad_q[rows_at(1 - at.core, half_wide), :] = other[...]
    term[...] = dot(grad_q[...], w0[...], 0, 0).astype(bf16)
    slots_out(at, at.core, term, top, low)
    whole[...] = dot(lat_all[...], grad_q[...], 0, 1)
    wq[...] = whole[rows_at(at.s, wq.shape[0]), :]


def finish_kernel(
    where, wq, sq_mine, sq_other, kv_mine, kv_other, lat_extra, lat_small, mid_small, in_sums_a, in_sums_b, in_sums_c, in_sums_d,
    square_grad, kv_grad, lat_grad, sums,
):
    core = where[0] & 1
    half = wq.shape[1] // 2
    mine, other = sq_mine[...], sq_other[...].astype(f32)
    low, high = jnp.where(core == 0, mine, other), jnp.where(core == 0, other, mine)
    square_grad[0] = wq[...]
    for m in range(3):
        square_grad[1 + m, :, 0:half] = low[:, m * half : (m + 1) * half]
        square_grad[1 + m, :, half:] = high[:, m * half : (m + 1) * half]
    kv_grad[core] = kv_mine[...]
    kv_grad[1 - core] = kv_other[...].astype(f32)
    n = lat_extra.shape[1] // 2
    ends = slice(3 * half, 3 * half + n)
    lat_grad[...] = (lat_extra[...] + jnp.concatenate([low[:, ends], high[:, ends]], 1)).T

    def squares(x):
        return jnp.sum(jnp.sum(x * x, 0, keepdims=True), 1, keepdims=True)

    own = slice(0, 3 * half)
    out = squares(wq[...]) + squares(mine[:, own]) + squares(other[:, own]) + squares(lat_grad[...])
    out = out + squares(kv_mine[...]) + squares(kv_other[...].astype(f32))
    sums[...] = jnp.zeros_like(sums)
    sums[0:2, :] = lat_small[...]
    sums[2:4, :] = mid_small[...]
    d_in = in_sums_a.shape[2]
    sums[4:7, 0:d_in] = (in_sums_a[0] + in_sums_b[0]) + (in_sums_c[0] + in_sums_d[0])
    sums[7:8, :] = jnp.broadcast_to(out, (1, sums.shape[1]))


def on_device(
    inputs,
    mask_flags,
    out_grad,
    square,
    square_state,
    kv_weights,
    kv_state,
    latents,
    latents_state,
    in_params,
    in_state,
    lat_params,
    lat_state,
):
    L = Links()
    S, H = L.S, L.H
    go = Order(jnp.stack([L.s, L.j]).astype(jnp.int32))
    rows, d_in = inputs.shape
    parts = SEQ_LEN // rows
    seqs = H // parts
    lat_rows, d_lat = latents.shape
    nlat = lat_rows * H
    wide = square.shape[2]
    half_wide = wide // 2
    d_part, in_part = d_lat // S, d_in // S
    chips = S // 2
    mine_rows = seqs * lat_rows

    def low(*shape):
        return like(shape, bf16)

    def full(*shape):
        return like(shape, f32)

    square_t, kv_t = jnp.swapaxes(square, 1, 2), jnp.swapaxes(kv_weights, 1, 2)
    (lat_low,) = go(lat_kernel, [latents, lat_params], [low(lat_rows, d_lat)], name="lat_norm")
    kv_pair = go(fix(kv_weight_kernel, H), [kv_t], [low(wide, d_in)] * 2, name="kv_weight")
    kv_first = [L.swap_step(kv_pair[0], i) for i in range(L.hb)]
    lat_near = L.near(lat_low)
    mask = mask_flags.reshape(rows, 1)
    step = min(rows, 256)
    in_low, in_turned = go(
        token_kernel,
        [inputs, mask, in_params],
        [low(rows, d_in), low(d_in, rows)],
        name="token_norm",
        grid=(rows // step,),
        in_specs=[
            pl.BlockSpec((step, d_in), lambda i: (i, 0)),
            pl.BlockSpec((step, 1), lambda i: (i, 0)),
            pl.BlockSpec(in_params.shape, lambda i: (0, 0)),
        ],
        out_specs=[pl.BlockSpec((step, d_in), lambda i: (i, 0)), pl.BlockSpec((d_in, step), lambda i: (0, i))],
    )
    (w0,) = go(
        first_weight_kernel,
        [square_t],
        [low(wide, d_lat)],
        name="first_weight",
        grid=(1,),
        in_specs=[pl.BlockSpec((1, wide, d_lat), lambda i: (0, 0, 0))],
        out_specs=[pl.BlockSpec((wide, d_lat), lambda i: (0, 0))],
    )
    kv_first = [after(x, w0) for x in kv_first]
    kv_mine = [kv_pair[0]] + L.spread(kv_first)
    kv_halves = kv_mine + [kv_pair[1]] + [L.swap_core(x) for x in kv_mine[1:]]
    lat_near = [lat_low] + [after(x, *kv_first) for x in lat_near]
    lat_all, query_mine, query_other = go(
        fix(query_kernel, H),
        [*lat_near, w0],
        [low(nlat, d_lat)] + [low(half_wide, nlat)] * 2,
        [pltpu.VMEM((wide, nlat), bf16)],
        name="query",
    )
    query_near = L.near(query_mine)
    sq_mine, sq_other = go(
        fix(other_weight_kernel, H),
        [square_t],
        [low(3, half_wide, d_lat)] * 2,
        name="other_weights",
        grid=(3,),
        in_specs=[pl.BlockSpec((1, wide, d_lat), lambda i: (1 + i, 0, 0))],
        out_specs=[pl.BlockSpec((1, half_wide, d_lat), lambda i: (i, 0, 0))] * 2,
    )
    sq_sent = after(sq_mine, kv_mine[-1])
    sq_near = [L.swap_step(sq_sent, i) for i in range(L.hb)]

    kv, kv_all = go(
        fix(kv_kernel, H),
        [in_turned, *kv_halves],
        [low(2, d_lat, rows), low(2, d_lat, d_in)],
        [pltpu.SemaphoreType.DMA((2 * H,))],
        name="kv",
        in_specs=[VMEM] + [ANY] * (2 * H),
        after=[sq_sent],
    )
    query_near = [after(x, kv) for x in query_near]
    query_halves = [query_mine] + query_near + [query_other] + [L.swap_core(x) for x in query_near]
    query, *packs = go(
        fix(attention_kernel, H),
        [*query_halves, kv],
        [low(d_lat, nlat)] + [low(lat_rows, d_lat + SIDE)] * H,
        [pltpu.VMEM((d_lat, nlat), f32), pltpu.VMEM((nlat, d_lat + SIDE), bf16)],
        name="attention",
    )
    got = [packs[0]] + [L.swap_hid(packs[m], m) for m in range(1, H)]
    sq_near = [after(x, *got) for x in sq_near]
    sq_all = [sq_mine] + L.spread(sq_near)
    sq_halves = sq_all + [sq_other] + [L.swap_core(x) for x in sq_all[1:]]

    latents_out, attended, branch_grad, up_grad, mid_low, hidden, grad_y, mid_small, res_sum, *backs = go(
        fix(latent_kernel, H, parts),
        [*got, latents, out_grad, lat_params, *sq_halves],
        [full(mine_rows, d_lat)]
        + [low(mine_rows, d_lat)] * 6
        + [full(2, d_lat), low(lat_rows, d_lat)]
        + [low(lat_rows, d_lat + SIDE)] * H,
        [
            pltpu.VMEM((3, d_lat, d_lat), bf16),
            pltpu.SemaphoreType.DMA((3, 2 * H)),
            pltpu.VMEM((H, lat_rows, d_lat + SIDE), bf16),
            pltpu.VMEM((mine_rows, d_lat), f32),
            pltpu.VMEM((seqs, lat_rows, d_lat + SIDE), bf16),
        ],
        name="latent",
        in_specs=[VMEM] * (H + 3) + [ANY] * (2 * H),
    )
    back = [backs[0]] + [L.swap_hid(backs[m], m) for m in range(1, H)]

    sq_args = [attended, up_grad, hidden, branch_grad, mid_low, grad_y]
    sq_scratch = [pltpu.VMEM((3, d_lat, mine_rows), bf16)]
    sq_like = [low(H // 2, 3, half_wide, d_lat)] * 2
    sq_send = go(fix(square_grad_kernel, H, False), sq_args, sq_like, sq_scratch, name="square_send")
    sq_got = [L.swap_core(x) for x in sq_send]
    sq_keep = go(fix(square_grad_kernel, H, True), sq_args, sq_like, sq_scratch, name="square_keep")
    sq = Halving(go, [sq_keep[0], sq_got[0]], [sq_keep[1], sq_got[1]], L.hb, L.swap_step, "square")
    sq.start()

    grad_kv, *gq = go(
        fix(attention_back_kernel, H),
        [query, kv, *back],
        [low(2, d_lat, rows)] + [low(H // 2, half_wide, nlat)] * 4,
        [
            pltpu.VMEM((nlat, d_lat + SIDE), bf16),
            pltpu.VMEM((d_lat, nlat), bf16),
            pltpu.VMEM((d_lat, nlat), bf16),
        ],
        name="attention_back",
    )
    gq_got = [L.swap_core(x) for x in gq[:2]]
    kv_scratch = [pltpu.VMEM((d_lat, d_in), bf16)]
    kv_like = [low(H // 2, wide, d_in)] * 2
    kv_send = go(fix(kv_grad_kernel, H, False), [grad_kv, in_low], kv_like, kv_scratch, name="kv_send")
    kv_got = [L.swap_core(x) for x in kv_send]
    gq_sums = Halving(go, [gq[2], gq_got[0]], [gq[3], gq_got[1]], L.hb, L.swap_step, "query")
    gq_sums.start()
    kv_keep = go(fix(kv_grad_kernel, H, True), [grad_kv, in_low], kv_like, kv_scratch, name="kv_keep")
    kv_sums = Halving(go, [kv_keep[0], kv_got[0]], [kv_keep[1], kv_got[1]], L.hb, L.swap_step, "kv")
    kv_sums.start()

    quarter = rows // 4
    in_sums = []
    inputs_grad = None

    def token_grad():
        nonlocal inputs_grad
        i = len(in_sums)
        outs = [full(rows, d_in), full(1, 3, d_in)]
        inputs_grad, sums = go(
            token_grad_kernel,
            [inputs, mask, in_params, grad_kv, kv_all],
            outs,
            [pltpu.VMEM((quarter, d_in), f32)],
            name="token_grad",
            grid=(1,),
            in_specs=[
                pl.BlockSpec((quarter, d_in), lambda g: (i, 0)),
                pl.BlockSpec((quarter, 1), lambda g: (i, 0)),
                pl.BlockSpec(in_params.shape, lambda g: (0, 0)),
                pl.BlockSpec((2, d_lat, quarter), lambda g: (0, 0, i)),
                pl.BlockSpec(kv_all.shape, lambda g: (0, 0, 0)),
            ],
            out_specs=[pl.BlockSpec((quarter, d_in), lambda g: (i, 0)), pl.BlockSpec((1, 3, d_in), lambda g: (0, 0, 0))],
            onto=inputs_grad,
        )
        in_sums.append(sums)

    lanes = 3 * half_wide + lat_rows // 2
    padded = -(-lanes // 128) * 128

    def turn_to_chips(kernel, terms, extra, n, lanes, padded, name):
        d = terms[0].shape[-1]
        out = [low(chips // 2, n, lanes)] * 2
        return go(
            kernel,
            [*terms, *extra],
            out,
            [pltpu.VMEM((padded, d), f32), pltpu.VMEM((d, padded), bf16)],
            name=name,
            grid=(1,),
            in_specs=first_blocks(terms) + whole_blocks(extra),
            out_specs=whole_blocks(out),
        )

    n = L.sb - 1

    def chip_step(x, i):
        return L.swap_seq(x, 2 << (n - 1 - i))

    def end(terms, n, lanes, name):
        return go(
            halve_end_kernel,
            terms,
            [full(n, lanes), low(n, lanes)],
            [pltpu.VMEM((2 * n, lanes), f32)],
            name=name,
            grid=(1,),
            in_specs=first_blocks(terms),
            out_specs=[pl.BlockSpec((n, lanes), lambda i: (0, 0))] * 2,
        )

    sq.step()
    gq_sums.step()
    token_grad()
    kv_sums.step()
    for _ in range(L.hb - 2):
        gq_sums.step()
        kv_sums.step()
        sq.step()
    gq_mine = go.add(gq_sums.terms, 0, 1, "query_sum")
    gq_near = L.swap_seq(gq_mine, 2)
    res_mine, res_send = go(core_rows_kernel, [res_sum], [low(lat_rows // 2, d_lat)] * 2, name="latent_rows")
    res_other = L.swap_core(res_send)
    token_grad()
    kv_top, kv_low = turn_to_chips(kv_turn_kernel, kv_sums.terms, [], 2 * in_part, wide, wide, "kv_turn")
    kv_chips = Halving(go, [kv_top], [kv_low], n, chip_step, "kv_chip")
    kv_chips.start()
    gq_mine = go.add([gq_mine, gq_near], 0, 1, "query_chip")
    gq_near = L.swap_seq(gq_mine, 4)
    token_grad()
    sq_top, sq_low = turn_to_chips(
        square_turn_kernel, sq.terms, [res_mine, res_other], 2 * d_part, lanes, padded, "square_turn"
    )
    sq_chips = Halving(go, [sq_top], [sq_low], n, chip_step, "square_chip")
    sq_chips.start()
    for i in range(2, L.sb):
        gq_mine = go.add([gq_mine, gq_near], 0, 1, "query_chip")
        if i + 1 < L.sb:
            gq_near = L.swap_seq(gq_mine, 2 << i)
    gq_mine = gq_mine[0]
    gq_other = L.swap_core(gq_mine)
    kv_chips.step()
    wq_part, lat_top, lat_low_half = go(
        fix(query_back_kernel, H),
        [lat_all, w0, gq_mine, gq_other],
        [full(d_part, wide)] + [low(H // 2, lat_rows // 2, d_lat)] * 2,
        [pltpu.VMEM((wide, nlat), bf16), pltpu.VMEM((d_lat, wide), f32), pltpu.VMEM((nlat, d_lat), bf16)],
        name="query_back",
    )
    lat_sums = Halving(go, [lat_top], [lat_low_half], L.hb, L.swap_step, "latent")
    lat_sums.start()
    token_grad()
    sq_chips.step()
    for _ in range(L.hb - 1):
        lat_sums.step()
    for _ in range(n - 2):
        kv_chips.step()
        sq_chips.step()
    kv_mine, kv_send = end(kv_chips.terms, in_part, wide, "kv_end")
    kv_other = L.swap_core(kv_send)
    low_mine = go.add(lat_sums.terms, 0, 1, "latent_sum")[0]
    low_other = L.swap_core(low_mine)
    lat_extra, lat_small = go(
        latent_end_kernel,
        [low_mine, low_other, latents, lat_params],
        [full(d_part, lat_rows), full(2, d_lat)],
        [pltpu.VMEM((d_lat, lat_rows), f32)],
        name="latent_end",
    )
    sq_mine, sq_send = end(sq_chips.terms, d_part, lanes, "square_end")
    sq_other = L.swap_core(sq_send)

    square_grad, kv_grad, lat_grad, sums = go(
        finish_kernel,
        [wq_part, sq_mine, sq_other, kv_mine, kv_other, lat_extra, lat_small, mid_small, *in_sums],
        [full(4, d_part, wide), full(2, in_part, wide), full(lat_rows, d_part), full(8, d_lat)],
        name="finish",
    )
    sums = L.sum_all(sums)
    sq_old = lax.dynamic_slice_in_dim(square, L.s * d_part, d_part, 1)
    kv_old = lax.dynamic_slice_in_dim(kv_weights, L.s * in_part, in_part, 1)
    lat_old = lax.dynamic_slice_in_dim(latents, L.s * d_part, d_part, 1)
    pair = [full(3, 2, d_in)] * 2
    outs = [full(1, 1)]
    for x in (sq_old, kv_old, lat_old, lat_params):
        outs += [full(2, *x.shape)] * 2
    results = go(
        fix(update_kernel, 5),
        [sums, sq_old, square_state, square_grad, kv_old, kv_state, kv_grad, lat_old, latents_state, lat_grad]
        + [lat_params, lat_state, in_params, in_state],
        outs + pair + [full(*lat_params.shape), full(*in_params.shape)],
        name="update",
    )
    (grad_norm, square_new, square_moments, kv_new, kv_moments, latents_new, latents_moments) = results[:7]
    (lat_new, lat_moments, in_new, in_moments, lat_clipped, in_clipped) = results[7:]
    grad_norm = grad_norm[0, 0]
    in_new, in_moments = jnp.swapaxes(in_new, 0, 1), jnp.swapaxes(in_moments, 0, 1)
    return (
        latents_out.reshape(seqs, lat_rows, d_lat),
        inputs_grad,
        grad_norm,
        square_new,
        square_moments,
        kv_new,
        kv_moments,
        latents_new,
        latents_moments,
        in_new,
        in_moments,
        lat_new,
        lat_moments,
        in_clipped,
        lat_clipped,
    )


def solution(mesh):
    return jax.shard_map(
        on_device,
        mesh=mesh,
        in_specs=(
            P(("seq", "hid"), None),
            P(("seq", "hid")),
            P("seq", "hid", None),
            P(None, None, "hid"),
            P(None, None, "seq", "hid"),
            P(None, None, "hid"),
            P(None, None, "seq", "hid"),
            P("hid", None),
            P(None, "hid", "seq"),
            P(),
            P(),
            P(),
            P(),
        ),
        out_specs=(
            P("seq", "hid", None),
            P(("seq", "hid"), None),
            P(),
            P(None, None, "seq", "hid"),
            P(None, None, "seq", "hid"),
            P(None, None, "seq", "hid"),
            P(None, None, "seq", "hid"),
            P(None, "hid", "seq"),
            P(None, "hid", "seq"),
            P(),
            P(),
            P(),
            P(),
            P(),
            P(),
        ),
        check_vma=False,
    )
```

time: 723 us -> 319 us (0.44)
  waiting for transfers between devices: 404 us -> 78.1 us
  Pallas kernels: 0 us -> 161 us
  matrix products: 83.7 us -> 0 us
  other arithmetic: 70.8 us -> 2.04 us
  blocking collectives: 57.8 us -> 0 us
  local copies, waits for them, and re-layouts: 79.2 us -> 27.5 us
  starting transfers between devices: 1.25 us -> 44.8 us
  between operations: 21.1 us -> 1.36 us
    reduce_scatter x5 -> x0, waiting for transfers between devices: 173 us -> none  [the longest x1 67.7 us: on_device(): lax.psum_scatter(input_term.astype(jnp.bfloat16), 'hid', scatter_dimensio...]
    pallas_call x0 -> x40, Pallas kernels: none -> 161 us  [__call__(): pl.pallas_call(body, out_shape=outs, grid=grid, in_specs=[SMEM] + (in_spe...]
    all_gather x4 -> x0, waiting for transfers between devices: 126 us -> none  [the longest x1 50 us: on_device(): lax.all_gather(in_low, 'hid', axis=0, tiled=True)]
    unnamed x13 -> x0, waiting for transfers between devices: 105 us -> none
    dot_general x21 -> x0, matrix products: 83.7 us -> none  [the longest x1 9.41 us: on_device(): jnp.einsum('tkc,kdc->td', grad_kv, w_kv, preferred_element_type=f32)]
    ppermute x0 -> x57, waiting for transfers between devices: none -> 78.1 us  [swap(): return lax.ppermute(x, ('seq', 'hid'), pairs)]
    ppermute x0 -> x57, starting transfers between devices: none -> 44.8 us  [swap(): return lax.ppermute(x, ('seq', 'hid'), pairs)]
    psum x1 -> x0, blocking collectives: 40.2 us -> none  [on_device(): lax.psum((big_sum, in_small, lat_small), ('seq', 'hid'))]
  transfers between devices with their start and end apart: 11 -> 57, of which waited for: 9 -> 22; matrix products, arithmetic and copies ran while one was open for 15% -> 3% of each run, Pallas kernels for 0% -> 40%
where the time goes in v1:
time: 319 us; the launch traced here: 315 us
  Pallas kernels  161 us (50%)
  waiting for transfers between devices  78.1 us (24%)
  starting transfers between devices  44.8 us (14%)
  local copies, waits for them, and re-layouts  27.5 us (9%)
    pallas_call x40, Pallas kernels, __call__(): pl.pallas_call(body, out_shape=outs, grid=grid, in_specs=[SMEM] + (in_spe...  161 us
    ppermute x57, waiting for transfers between devices, swap(): return lax.ppermute(x, ('seq', 'hid'), pairs)  78.1 us
    ppermute x57, starting transfers between devices, swap(): return lax.ppermute(x, ('seq', 'hid'), pairs)  44.8 us
    unnamed x134, local copies, waits for them, and re-layouts  21.5 us
  transfers between devices with their start and end apart: 57, of which 22 were waited for; matrix products, arithmetic and copies ran while one was open for 3% of the time, Pallas kernels for 40%

profile of v1, /device:TPU:0, one launch (start us, length us, event | category | flops | bytes accessed | tf_op | source)
XLA Modules:
  0.0 315.1 jit_solution(6562738879678159281)
XLA Ops:
  5.8 2.9 collective-permute-start.1
  14.8 4.9 %token_norm.1 = (bf16[1024,768]{1,0:T(8,128)(2,1)}, bf16[768,1024]{1,0:T(8,128)(2,1)}) custom-call(s32[2]{0:T(128)} %pad_add_fusion.where, f32[1024,768]{1,0:T(8,128)} %refs_0_.11, s32[1024,1]{1,0:T(8,128)} %copy.37.refs_1_, f32[3,768]{1,0:T(4,128)} %refs_12_.1, bf16[320,768]{1,0:T(8,128)(2,1)} %get-tuple-element.108.refs_3_.refs_1_), custom_call_target="tpu_custom_call" | custom-call | flops 15000000512 | tf_op jit(solution)/shard_map/token_norm/pallas_call | solution.py:182
  31.2 3.2 %collective-permute-start.11 = (bf16[160,256]{1,0:T(8,128)(2,1)}, bf16[160,256]{1,0:T(8,128)(2,1)S(1)}, u32[]{:S(2)}, u32[]{:S(2)}) collective-permute-start(bf16[160,256]{1,0:T(8,128)(2,1)} %get-tuple-element.115.refs_0_), channel_id=1, source_target_pairs={{0,3},{1,2},{2,1},{3,0},{4,7},{5,6},{6,5},{7,4},{8,11},{9,10},{10,... | collective-permute-start | bytes 245768 | tf_op jit(solution)/shard_map/ppermute | solution.py:84
  34.8 5.1 %other_weights.1 = (bf16[3,160,1280]{2,1,0:T(8,128)(2,1)}, bf16[3,160,1280]{2,1,0:T(8,128)(2,1)}) custom-call(s32[2]{0:T(128)} %pad_add_fusion.where, f32[4,320,1280]{2,1,0:T(8,128)} %bitcast.49, bf16[256,1280]{1,0:T(8,128)(2,1)} %get-tuple-element.118.refs_1_.refs_0_), custom_call_target="tpu_custom_call" | custom-call | flops 14099999744 | tf_op jit(solution)/shard_map/other_weights/pallas_call | solution.py:182
  41.2 10.2 %kv.1 = (bf16[2,1280,1024]{2,1,0:T(8,128)(2,1)}, bf16[2,1280,768]{2,1,0:T(8,128)(2,1)}) custom-call(s32[2]{0:T(128)} %pad_add_fusion.where, bf16[768,1024]{1,0:T(8,128)(2,1)} %get-tuple-element.116.refs_0_, bf16[320,768]{1,0:T(8,128)(2,1)} %get-tuple-element.108.refs_3_.refs_1_, bf16[320,768]{1,0:T(8,128)(2,1)} %copy-done.16, bf16[320,768]{1,0:T(8,128)(2,1)} %copy-done.17, ...), custom_call_target="tpu_custom_call" | custom-call | flops 30000001024 | tf_op jit(solution)/shard_map/kv/pallas_call | solution.py:182
  54.7 7.7 %attention.1 = (bf16[1280,256]{1,0:T(8,128)(2,1)}, bf16[64,1408]{1,0:T(8,128)(2,1)}, bf16[64,1408]{1,0:T(8,128)(2,1)}, bf16[64,1408]{1,0:T(8,128)(2,1)}, bf16[64,1408]{1,0:T(8,128)(2,1)}) custom-call(s32[2]{0:T(128)} %pad_add_fusion.where, bf16[160,256]{1,0:T(8,128)(2,1)} %get-tuple-element.115.refs_0_, bf16[160,256]{1,0:T(8,128)(2,1)} %copy-done.50, ...), custom_call_target="tpu_custom_call" | custom-call | flops 24000000000 | tf_op jit(solution)/shard_map/attention/pallas_call | solution.py:182
  67.5 8.7 %collective-permute-done.15.refs_1_ = bf16[64,1408]{1,0:T(8,128)(2,1)S(1)} collective-permute-done((bf16[64,1408]{1,0:T(8,128)(2,1)}, bf16[64,1408]{1,0:T(8,128)(2,1)S(1)}, u32[]{:S(2)}, u32[]{:S(2)}) %collective-permute-start.15) | collective-permute-done | bytes 180256 | tf_op jit(solution)/shard_map/ppermute | solution.py:84
  76.2 5.9 %collective-permute-done.17.refs_3_ = bf16[64,1408]{1,0:T(8,128)(2,1)S(1)} collective-permute-done((bf16[64,1408]{1,0:T(8,128)(2,1)}, bf16[64,1408]{1,0:T(8,128)(2,1)S(1)}, u32[]{:S(2)}, u32[]{:S(2)}) %collective-permute-start.17) | collective-permute-done | bytes 180256 | tf_op jit(solution)/shard_map/ppermute | solution.py:84
  82.3 7.1 %collective-permute-done.19.refs_9_ = bf16[3,160,1280]{2,1,0:T(8,128)(2,1)S(1)} collective-permute-done((bf16[3,160,1280]{2,1,0:T(8,128)(2,1)S(1)}, bf16[3,160,1280]{2,1,0:T(8,128)(2,1)S(1)}, u32[]{:S(2)}, u32[]{:S(2)}) %collective-permute-start.19) | collective-permute-done | bytes 1228832 | tf_op jit(solution)/shard_map/ppermute | solution.py:84
  90.0 12.6 %collective-permute-done.20.refs_10_ = bf16[3,160,1280]{2,1,0:T(8,128)(2,1)S(1)} collective-permute-done((bf16[3,160,1280]{2,1,0:T(8,128)(2,1)S(1)}, bf16[3,160,1280]{2,1,0:T(8,128)(2,1)S(1)}, u32[]{:S(2)}, u32[]{:S(2)}) %collective-permute-start.20) | collective-permute-done | bytes 1228832 | tf_op jit(solution)/shard_map/ppermute | solution.py:84
  106.6 11.1 %latent.1 = (f32[128,1280]{1,0:T(8,128)}, bf16[128,1280]{1,0:T(8,128)(2,1)}, bf16[128,1280]{1,0:T(8,128)(2,1)}, bf16[128,1280]{1,0:T(8,128)(2,1)}, bf16[128,1280...) custom-call(s32[2]{0:T(128)} %pad_add_fusion.where, ...), custom_call_target="tpu_custom_call" | custom-call | flops 32999999488 | tf_op jit(solution)/shard_map/latent/pallas_call | solution.py:182
  117.7 4.9 %square_send.1 = (bf16[2,3,160,1280]{3,2,1,0:T(8,128)(2,1)}, bf16[2,3,160,1280]{3,2,1,0:T(8,128)(2,1)}) custom-call(s32[2]{0:T(128)} %pad_add_fusion.where, bf16[128,1280]{1,0:T(8,128)(2,1)} %get-tuple-element.139.refs_0_, bf16[128,1280]{1,0:T(8,128)(2,1)} %get-tuple-element.140.refs_1_, bf16[128,1280]{1,0:T(8,128)(2,1)} %get-tuple-element.141.refs_2_, ...), custom_call_target="tpu_custom_call" | custom-call | flops 15000000512 | tf_op jit(solution)/shard_map/square_send/pallas_call | solution.py:182
  126.3 4.8 %square_keep.1 = (bf16[2,3,160,1280]{3,2,1,0:T(8,128)(2,1)}, bf16[2,3,160,1280]{3,2,1,0:T(8,128)(2,1)}) custom-call(s32[2]{0:T(128)} %pad_add_fusion.where, bf16[128,1280]{1,0:T(8,128)(2,1)} %get-tuple-element.139.refs_0_, bf16[128,1280]{1,0:T(8,128)(2,1)} %get-tuple-element.140.refs_1_, bf16[128,1280]{1,0:T(8,128)(2,1)} %get-tuple-element.141.refs_2_, ...), custom_call_target="tpu_custom_call" | custom-call | flops 15000000512 | tf_op jit(solution)/shard_map/square_keep/pallas_call | solution.py:182
  132.5 5.6 %square_top.1.refs_6_ = bf16[2,3,160,1280]{3,2,1,0:T(8,128)(2,1)} custom-call(s32[2]{0:T(128)} %pad_add_fusion.where, bf16[2,3,160,1280]{3,2,1,0:T(8,128)(2,1)} %get-tuple-element.146.refs_0_.refs_2_, bf16[2,3,160,1280]{3,2,1,0:T(8,128)(2,1)} %copy-done.3, bf16[2,3,160,1280]{3,2,1,0:T(8,128)(2,1)} %get-tuple-element.146.refs_0_.refs_2_), custom_call_target="tpu_custom_call" | custom-call | flops 17999998976 | tf_op jit(solution)/shard_map/square_top/pallas_call | solution.py:182
  140.8 11.6 %attention_back.1 = (bf16[2,1280,1024]{2,1,0:T(8,128)(2,1)}, bf16[2,160,256]{2,1,0:T(8,128)(2,1)}, bf16[2,160,256]{2,1,0:T(8,128)(2,1)}, bf16[2,160,256]{2,1,0:T(8,128)(2,1)}, bf16[2,160,256]{2,1,0:T(8,128)(2,1)}) custom-call(s32[2]{0:T(128)} %pad_add_fusion.where, bf16[1280,256]{1,0:T(8,128)(2,1)} %get-tuple-element.133.refs_15_.refs_0_, ...), custom_call_target="tpu_custom_call" | custom-call | flops 35999997952 | tf_op jit(solution)/shard_map/attention_back/pallas_call | solution.py:182
  152.4 6.6 %kv_send.1 = (bf16[2,320,768]{2,1,0:T(8,128)(2,1)}, bf16[2,320,768]{2,1,0:T(8,128)(2,1)}) custom-call(s32[2]{0:T(128)} %pad_add_fusion.where, bf16[2,1280,1024]{2,1,0:T(8,128)(2,1)} %get-tuple-element.147.refs_0_.refs_2_.refs_3_, bf16[1024,768]{1,0:T(8,128)(2,1)} %get-tuple-element.109.refs_1_, bf16[2,1280,1024]{2,1,0:T(8,128)(2,1)} %get-tuple-element.147.refs_0_.refs_2_.refs_3_), custom_call_target="tpu_custom_call" | custom-call | flops 19499999232 | tf_op jit(solution)/shard_map/kv_send/pallas_call | solution.py:182
  161.9 6.6 %kv_keep.1 = (bf16[2,320,768]{2,1,0:T(8,128)(2,1)}, bf16[2,320,768]{2,1,0:T(8,128)(2,1)}) custom-call(s32[2]{0:T(128)} %pad_add_fusion.where, bf16[2,1280,1024]{2,1,0:T(8,128)(2,1)} %get-tuple-element.147.refs_0_.refs_2_.refs_3_, bf16[1024,768]{1,0:T(8,128)(2,1)} %get-tuple-element.109.refs_1_, bf16[2,1,160,256]{3,2,1,0:T(8,128)(2,1)} %query_top.1.refs_2_), custom_call_target="tpu_custom_call" | custom-call | flops 19499999232 | tf_op jit(solution)/shard_map/kv_keep/pallas_call | solution.py:182
  175.0 4.1 %square_step.1.refs_3_ = bf16[1,3,160,1280]{3,2,1,0:T(8,128)(2,1)} custom-call(s32[2]{0:T(128)} %pad_add_fusion.where, bf16[2,3,160,1280]{3,2,1,0:T(8,128)(2,1)} %get-tuple-element.154.refs_0_, bf16[2,3,160,1280]{3,2,1,0:T(8,128)(2,1)} %copy-done.1, bf16[2,3,160,1280]{3,2,1,0:T(8,128)(2,1)} %copy-done.2, bf16[2,1,320,768]{3,2,1,0:T(8,128)(2,1)} %kv_top.1.refs_3_), custom_call_target="tpu_custom_call" | custom-call | flops 12000000000 | tf_op jit(solution)/shard_map/square_step/pallas_call | solution.py:182
  183.5 5.3 %token_grad.4 = (f32[1024,768]{1,0:T(8,128)}, f32[1,3,768]{2,1,0:T(4,128)}) custom-call(s32[2]{0:T(128)} %pad_add_fusion.where, f32[1024,768]{1,0:T(8,128)} %refs_0_.11, s32[1024,1]{1,0:T(8,128)} %copy.37.refs_1_, f32[3,768]{1,0:T(4,128)} %refs_12_.1, bf16[2,1280,1024]{2,1,0:T(8,128)(2,1)} %get-tuple-element.147.refs_0_.refs_2_.refs_3_, ...), custom_call_target="tpu_custom_call" | custom-call | flops 12000000000 | tf_op jit(solution)/shard_map/token_grad/pallas_call | solution.py:182
  188.8 3.0 collective-permute-done.36.refs_2_
  195.5 4.5 %collective-permute-done.34 = bf16[1,160,256]{2,1,0:T(8,128)(2,1)S(1)} collective-permute-done((bf16[1,160,256]{2,1,0:T(8,128)(2,1)}, bf16[1,160,256]{2,1,0:T(8,128)(2,1)S(1)}, u32[]{:S(2)}, u32[]{:S(2)}) %collective-permute-start.34) | collective-permute-done | bytes 81952 | tf_op jit(solution)/shard_map/ppermute | solution.py:84
  203.9 5.3 %token_grad.5 = (f32[1024,768]{1,0:T(8,128)}, f32[1,3,768]{2,1,0:T(4,128)}) custom-call(s32[2]{0:T(128)} %pad_add_fusion.where, f32[1024,768]{1,0:T(8,128)} %refs_0_.11, s32[1024,1]{1,0:T(8,128)} %copy.37.refs_1_, f32[3,768]{1,0:T(4,128)} %refs_12_.1, ...), custom_call_target="tpu_custom_call", output_to_operand_aliasing={{0}: (6, {})} | custom-call | flops 12000000000 | tf_op jit(solution)/shard_map/token_grad/pallas_call | solution.py:182
  217.8 5.3 %token_grad.6 = (f32[1024,768]{1,0:T(8,128)}, f32[1,3,768]{2,1,0:T(4,128)}) custom-call(s32[2]{0:T(128)} %pad_add_fusion.where, f32[1024,768]{1,0:T(8,128)} %refs_0_.11, s32[1024,1]{1,0:T(8,128)} %copy.37.refs_1_, f32[3,768]{1,0:T(4,128)} %refs_12_.1, ...), custom_call_target="tpu_custom_call", output_to_operand_aliasing={{0}: (6, {})} | custom-call | flops 12000000000 | tf_op jit(solution)/shard_map/token_grad/pallas_call | solution.py:182
  226.8 4.3 %square_turn.1 = (bf16[2,320,512]{2,1,0:T(8,128)(2,1)}, bf16[2,320,512]{2,1,0:T(8,128)(2,1)}) custom-call(s32[2]{0:T(128)} %pad_add_fusion.where, bf16[2,3,160,1280]{3,2,1,0:T(8,128)(2,1)} %get-tuple-element.154.refs_0_, bf16[2,3,160,1280]{3,2,1,0:T(8,128)(2,1)} %copy-done.1, bf16[2,3,160,1280]{3,2,1,0:T(8,128)(2,1)} %copy-done.2, ...), custom_call_target="tpu_custom_call" | custom-call | flops 12000000000 | tf_op jit(solution)/shard_map/square_turn/pallas_call | solution.py:182
  238.3 3.0 query_back.1
  242.1 5.3 %token_grad.7 = (f32[1024,768]{1,0:T(8,128)}, f32[1,3,768]{2,1,0:T(4,128)}) custom-call(s32[2]{0:T(128)} %pad_add_fusion.where, f32[1024,768]{1,0:T(8,128)} %refs_0_.11, s32[1024,1]{1,0:T(8,128)} %copy.37.refs_1_, f32[3,768]{1,0:T(4,128)} %refs_12_.1, ...), custom_call_target="tpu_custom_call", output_to_operand_aliasing={{0}: (6, {})} | custom-call | flops 12000000000 | tf_op jit(solution)/shard_map/token_grad/pallas_call | solution.py:182
  247.4 3.1 collective-permute-done.44.refs_1_
  266.9 13.1 %collective-permute-done.45.refs_2_ = bf16[1,320,512]{2,1,0:T(8,128)(2,1)S(1)} collective-permute-done((bf16[1,320,512]{2,1,0:T(8,128)(2,1)S(1)}, bf16[1,320,512]{2,1,0:T(8,128)(2,1)S(1)}, u32[]{:S(2)}, u32[]{:S(2)}) %collective-permute-start.45) | collective-permute-done | bytes 327712 | tf_op jit(solution)/shard_map/ppermute | solution.py:84
  285.2 2.7 finish.1
  290.9 3.3 %collective-permute-done.53 = f32[8,1280]{1,0:T(8,128)S(1)} collective-permute-done((f32[8,1280]{1,0:T(8,128)S(1)}, f32[8,1280]{1,0:T(8,128)S(1)}, u32[]{:S(2)}, u32[]{:S(2)}) %collective-permute-start.53) | collective-permute-done | bytes 40992 | tf_op jit(solution)/shard_map/ppermute | solution.py:84
  299.4 2.7 collective-permute-done.55
  307.7 7.1 %update.1 = (f32[1,1]{1,0:T(1,128)}, f32[2,4,160,320]{3,2,1,0:T(8,128)}, f32[2,4,160,320]{3,2,1,0:T(8,128)}, f32[2,2,96,320]{3,2,1,0:T(8,128)}, f32[2,2,96,320]{...) custom-call(s32[2]{0:T(128)} %pad_add_fusion.where, ...), custom_call_target="tpu_custom_call" | custom-call | flops 20999999488 | tf_op jit(solution)/shard_map/update/pallas_call | solution.py:182
  (266 shorter events, 121.9 us)
Async XLA Ops:
  5.8 16.3 %collective-permute-start.1 = (bf16[320,768]{1,0:T(8,128)(2,1)}, bf16[320,768]{1,0:T(8,128)(2,1)S(1)}, u32[]{:S(2)}, u32[]{:S(2)}) collective-permute-start(bf16[320,768]{1,0:T(8,128)(2,1)} %get-tuple-element.108.refs_3_.refs_1_), channel_id=1, source_target_pairs={{0,1},{1,0},{2,3},{3,2},{4,6},{5,7},{6,4},{7,5},{8,9},{9,8},{10,11... | collective-permute-start | bytes 1474568 | tf_op jit(solution)/shard_map/ppermute | solution.py:84
  8.7 16.1 %collective-permute-start.2 = (bf16[320,768]{1,0:T(8,128)(2,1)}, bf16[320,768]{1,0:T(8,128)(2,1)S(1)}, u32[]{:S(2)}, u32[]{:S(2)}) collective-permute-start(bf16[320,768]{1,0:T(8,128)(2,1)} %get-tuple-element.108.refs_3_.refs_1_), channel_id=1, source_target_pairs={{0,2},{1,3},{2,0},{3,1},{4,5},{5,4},{6,7},{7,6},{8,10},{9,11},{10,... | collective-permute-start | bytes 1474568 | tf_op jit(solution)/shard_map/ppermute | solution.py:84
  10.2 15.8 %collective-permute-start.4 = (bf16[64,1280]{1,0:T(8,128)(2,1)S(1)}, bf16[64,1280]{1,0:T(8,128)(2,1)S(1)}, u32[]{:S(2)}, u32[]{:S(2)}) collective-permute-start(bf16[64,1280]{1,0:T(8,128)(2,1)S(1)} %copy-done.38), channel_id=1, source_target_pairs={{0,3},{1,2},{2,1},{3,0},{4,7},{5,6},{6,5},{7,4},{8,11},{9,10},{10,... | collective-permute-start | bytes 491528 | tf_op jit(solution)/shard_map/ppermute | solution.py:84
  10.2 17.0 %collective-permute-start.3 = (bf16[64,1280]{1,0:T(8,128)(2,1)S(1)}, bf16[64,1280]{1,0:T(8,128)(2,1)S(1)}, u32[]{:S(2)}, u32[]{:S(2)}) collective-permute-start(bf16[64,1280]{1,0:T(8,128)(2,1)S(1)} %copy-done.38), channel_id=1, source_target_pairs={{0,2},{1,3},{2,0},{3,1},{4,6},{5,7},{6,4},{7,5},{8,10},{9,11},{10,... | collective-permute-start | bytes 491528 | tf_op jit(solution)/shard_map/ppermute | solution.py:84
  12.2 15.3 %collective-permute-start = (bf16[64,1280]{1,0:T(8,128)(2,1)S(1)}, bf16[64,1280]{1,0:T(8,128)(2,1)S(1)}, u32[]{:S(2)}, u32[]{:S(2)}) collective-permute-start(bf16[64,1280]{1,0:T(8,128)(2,1)S(1)} %copy-done.38), channel_id=1, source_target_pairs={{0,1},{1,0},{2,3},{3,2},{4,5},{5,4},{6,7},{7,6},{8,9},{9,8},{10,11... | collective-permute-start | bytes 491528 | tf_op jit(solution)/shard_map/ppermute | solution.py:84
  24.8 15.1 %collective-permute-start.7 = (bf16[320,768]{1,0:T(8,128)(2,1)S(1)}, bf16[320,768]{1,0:T(8,128)(2,1)S(1)}, u32[]{:S(2)}, u32[]{:S(2)}) collective-permute-start(bf16[320,768]{1,0:T(8,128)(2,1)S(1)} %collective-permute-done.1.refs_2_), channel_id=1, source_target_pairs={{0,4},{1,5},{2,6},{3,7},{4,0},{5,1},{6,2},{7,3},{8,12},{9,13},{10,... | collective-permute-start | bytes 1474568 | tf_op jit(solution)/shard_map/ppermute | solution.py:84
  26.1 14.2 %collective-permute-start.8 = (bf16[320,768]{1,0:T(8,128)(2,1)S(1)}, bf16[320,768]{1,0:T(8,128)(2,1)S(1)}, u32[]{:S(2)}, u32[]{:S(2)}) collective-permute-start(bf16[320,768]{1,0:T(8,128)(2,1)S(1)} %collective-permute-done.2.refs_3_), channel_id=1, source_target_pairs={{0,4},{1,5},{2,6},{3,7},{4,0},{5,1},{6,2},{7,3},{8,12},{9,13},{10,... | collective-permute-start | bytes 1474568 | tf_op jit(solution)/shard_map/ppermute | solution.py:84
  31.2 20.2 %collective-permute-start.11 = (bf16[160,256]{1,0:T(8,128)(2,1)}, bf16[160,256]{1,0:T(8,128)(2,1)S(1)}, u32[]{:S(2)}, u32[]{:S(2)}) collective-permute-start(bf16[160,256]{1,0:T(8,128)(2,1)} %get-tuple-element.115.refs_0_), channel_id=1, source_target_pairs={{0,3},{1,2},{2,1},{3,0},{4,7},{5,6},{6,5},{7,4},{8,11},{9,10},{10,... | collective-permute-start | bytes 245768 | tf_op jit(solution)/shard_map/ppermute | solution.py:84
  34.4 17.3 %collective-permute-start.10 = (bf16[160,256]{1,0:T(8,128)(2,1)}, bf16[160,256]{1,0:T(8,128)(2,1)S(1)}, u32[]{:S(2)}, u32[]{:S(2)}) collective-permute-start(bf16[160,256]{1,0:T(8,128)(2,1)} %get-tuple-element.115.refs_0_), channel_id=1, source_target_pairs={{0,2},{1,3},{2,0},{3,1},{4,6},{5,7},{6,4},{7,5},{8,10},{9,11},{10,... | collective-permute-start | bytes 245768 | tf_op jit(solution)/shard_map/ppermute | solution.py:84
  52.2 29.9 %collective-permute-start.18 = (bf16[3,160,1280]{2,1,0:T(8,128)(2,1)S(1)}, bf16[3,160,1280]{2,1,0:T(8,128)(2,1)S(1)}, u32[]{:S(2)}, u32[]{:S(2)}) collective-permute-start(bf16[3,160,1280]{2,1,0:T(8,128)(2,1)S(1)} %copy-done.4), channel_id=1, source_target_pairs={{0,1},{1,0},{2,3},{3,2},{4,6},{5,7},{6,4},{7,5},{8,9},{9,8},{10,11... | collective-permute-start | bytes 3686408 | tf_op jit(solution)/shard_map/ppermute | solution.py:84
  62.4 13.8 %collective-permute-start.15 = (bf16[64,1408]{1,0:T(8,128)(2,1)}, bf16[64,1408]{1,0:T(8,128)(2,1)S(1)}, u32[]{:S(2)}, u32[]{:S(2)}) collective-permute-start(bf16[64,1408]{1,0:T(8,128)(2,1)} %get-tuple-element.127), channel_id=1, source_target_pairs={{0,1},{1,0},{2,3},{3,2},{4,5},{5,4},{6,7},{7,6},{8,9},{9,8},{10,11... | collective-permute-start | bytes 540680 | tf_op jit(solution)/shard_map/ppermute | solution.py:84
  65.1 17.0 %collective-permute-start.17 = (bf16[64,1408]{1,0:T(8,128)(2,1)}, bf16[64,1408]{1,0:T(8,128)(2,1)S(1)}, u32[]{:S(2)}, u32[]{:S(2)}) collective-permute-start(bf16[64,1408]{1,0:T(8,128)(2,1)} %get-tuple-element.129), channel_id=1, source_target_pairs={{0,3},{1,2},{2,1},{3,0},{4,7},{5,6},{6,5},{7,4},{8,11},{9,10},{10,... | collective-permute-start | bytes 540680 | tf_op jit(solution)/shard_map/ppermute | solution.py:84
  65.9 23.5 %collective-permute-start.19 = (bf16[3,160,1280]{2,1,0:T(8,128)(2,1)S(1)}, bf16[3,160,1280]{2,1,0:T(8,128)(2,1)S(1)}, u32[]{:S(2)}, u32[]{:S(2)}) collective-permute-start(bf16[3,160,1280]{2,1,0:T(8,128)(2,1)S(1)} %copy-done.4), channel_id=1, source_target_pairs={{0,2},{1,3},{2,0},{3,1},{4,5},{5,4},{6,7},{7,6},{8,10},{9,11},{10,... | collective-permute-start | bytes 3686408 | tf_op jit(solution)/shard_map/ppermute | solution.py:84
  82.1 20.5 %collective-permute-start.20 = (bf16[3,160,1280]{2,1,0:T(8,128)(2,1)S(1)}, bf16[3,160,1280]{2,1,0:T(8,128)(2,1)S(1)}, u32[]{:S(2)}, u32[]{:S(2)}) collective-permute-start(bf16[3,160,1280]{2,1,0:T(8,128)(2,1)S(1)} %collective-permute-done.18.refs_8_), channel_id=1, source_target_pairs={{0,2},{1,3},{2,0},{3,1},{4,5},{5,4},{6,7},{7,6},{8,10},{9,11},{10,... | collective-permute-start | bytes 3686408 | tf_op jit(solution)/shard_map/ppermute | solution.py:84
  82.2 20.6 %collective-permute-start.21 = (bf16[3,160,1280]{2,1,0:T(8,128)(2,1)S(1)}, bf16[3,160,1280]{2,1,0:T(8,128)(2,1)S(1)}, u32[]{:S(2)}, u32[]{:S(2)}) collective-permute-start(bf16[3,160,1280]{2,1,0:T(8,128)(2,1)S(1)} %collective-permute-done.18.refs_8_), channel_id=1, source_target_pairs={{0,4},{1,5},{2,6},{3,7},{4,0},{5,1},{6,2},{7,3},{8,12},{9,13},{10,... | collective-permute-start | bytes 3686408 | tf_op jit(solution)/shard_map/ppermute | solution.py:84
  89.4 13.4 %collective-permute-start.22 = (bf16[3,160,1280]{2,1,0:T(8,128)(2,1)S(1)}, bf16[3,160,1280]{2,1,0:T(8,128)(2,1)S(1)}, u32[]{:S(2)}, u32[]{:S(2)}) collective-permute-start(bf16[3,160,1280]{2,1,0:T(8,128)(2,1)S(1)} %collective-permute-done.19.refs_9_), channel_id=1, source_target_pairs={{0,4},{1,5},{2,6},{3,7},{4,0},{5,1},{6,2},{7,3},{8,12},{9,13},{10,... | collective-permute-start | bytes 3686408 | tf_op jit(solution)/shard_map/ppermute | solution.py:84
  122.8 17.2 %collective-permute-start.24 = (bf16[64,1408]{1,0:T(8,128)(2,1)S(1)}, bf16[64,1408]{1,0:T(8,128)(2,1)S(1)}, u32[]{:S(2)}, u32[]{:S(2)}) collective-permute-start(bf16[64,1408]{1,0:T(8,128)(2,1)S(1)} %copy-done.31), channel_id=1, source_target_pairs={{0,1},{1,0},{2,3},{3,2},{4,5},{5,4},{6,7},{7,6},{8,9},{9,8},{10,11... | collective-permute-start | bytes 540680 | tf_op jit(solution)/shard_map/ppermute | solution.py:84
  124.5 15.5 %collective-permute-start.25 = (bf16[64,1408]{1,0:T(8,128)(2,1)S(1)}, bf16[64,1408]{1,0:T(8,128)(2,1)S(1)}, u32[]{:S(2)}, u32[]{:S(2)}) collective-permute-start(bf16[64,1408]{1,0:T(8,128)(2,1)S(1)} %copy-done.30), channel_id=1, source_target_pairs={{0,2},{1,3},{2,0},{3,1},{4,6},{5,7},{6,4},{7,5},{8,10},{9,11},{10,... | collective-permute-start | bytes 540680 | tf_op jit(solution)/shard_map/ppermute | solution.py:84
  126.1 13.9 %collective-permute-start.26 = (bf16[64,1408]{1,0:T(8,128)(2,1)S(1)}, bf16[64,1408]{1,0:T(8,128)(2,1)S(1)}, u32[]{:S(2)}, u32[]{:S(2)}) collective-permute-start(bf16[64,1408]{1,0:T(8,128)(2,1)S(1)} %copy-done.29), channel_id=1, source_target_pairs={{0,3},{1,2},{2,1},{3,0},{4,7},{5,6},{6,5},{7,4},{8,11},{9,10},{10,... | collective-permute-start | bytes 540680 | tf_op jit(solution)/shard_map/ppermute | solution.py:84
  126.3 46.3 %collective-permute-start.31 = (bf16[2,3,160,1280]{3,2,1,0:T(8,128)(2,1)}, bf16[2,3,160,1280]{3,2,1,0:T(8,128)(2,1)S(1)}, u32[]{:S(2)}, u32[]{:S(2)}) collective-permute-start(bf16[2,3,160,1280]{3,2,1,0:T(8,128)(2,1)} %get-tuple-element.155), channel_id=1, source_target_pairs={{0,4},{1,5},{2,6},{3,7},{4,0},{5,1},{6,2},{7,3},{8,12},{9,13},{10,... | collective-permute-start | bytes 7372808 | tf_op jit(solution)/shard_map/ppermute | solution.py:84
  138.1 35.3 %collective-permute-start.32 = (bf16[2,3,160,1280]{3,2,1,0:T(8,128)(2,1)}, bf16[2,3,160,1280]{3,2,1,0:T(8,128)(2,1)S(1)}, u32[]{:S(2)}, u32[]{:S(2)}) collective-permute-start(bf16[2,3,160,1280]{3,2,1,0:T(8,128)(2,1)} %square_top.1.refs_6_), channel_id=1, source_target_pairs={{0,2},{1,3},{2,0},{3,1},{4,5},{5,4},{6,7},{7,6},{8,10},{9,11},{10,... | collective-permute-start | bytes 7372808 | tf_op jit(solution)/shard_map/ppermute | solution.py:84
  159.5 20.6 %collective-permute-start.28 = (bf16[2,160,256]{2,1,0:T(8,128)(2,1)S(1)}, bf16[2,160,256]{2,1,0:T(8,128)(2,1)S(1)}, u32[]{:S(2)}, u32[]{:S(2)}) collective-permute-start(bf16[2,160,256]{2,1,0:T(8,128)(2,1)S(1)} %copy-done.36), channel_id=1, source_target_pairs={{0,4},{1,5},{2,6},{3,7},{4,0},{5,1},{6,2},{7,3},{8,12},{9,13},{10,... | collective-permute-start | bytes 491528 | tf_op jit(solution)/shard_map/ppermute | solution.py:84
  159.6 29.2 %collective-permute-start.35 = (bf16[2,320,768]{2,1,0:T(8,128)(2,1)}, bf16[2,320,768]{2,1,0:T(8,128)(2,1)S(1)}, u32[]{:S(2)}, u32[]{:S(2)}) collective-permute-start(bf16[2,320,768]{2,1,0:T(8,128)(2,1)} %get-tuple-element.160), channel_id=1, source_target_pairs={{0,4},{1,5},{2,6},{3,7},{4,0},{5,1},{6,2},{7,3},{8,12},{9,13},{10,... | collective-permute-start | bytes 2949128 | tf_op jit(solution)/shard_map/ppermute | solution.py:84
  172.5 19.3 %collective-permute-start.36 = (bf16[2,320,768]{2,1,0:T(8,128)(2,1)}, bf16[2,320,768]{2,1,0:T(8,128)(2,1)S(1)}, u32[]{:S(2)}, u32[]{:S(2)}) collective-permute-start(bf16[2,320,768]{2,1,0:T(8,128)(2,1)} %bitcast.54), channel_id=1, source_target_pairs={{0,2},{1,3},{2,0},{3,1},{4,5},{5,4},{6,7},{7,6},{8,10},{9,11},{10,... | collective-permute-start | bytes 2949128 | tf_op jit(solution)/shard_map/ppermute | solution.py:84
  179.0 46.7 %collective-permute-start.40 = (bf16[1,3,160,1280]{3,2,1,0:T(8,128)(2,1)}, bf16[1,3,160,1280]{3,2,1,0:T(8,128)(2,1)S(1)}, u32[]{:S(2)}, u32[]{:S(2)}) collective-permute-start(bf16[1,3,160,1280]{3,2,1,0:T(8,128)(2,1)} %square_step.1.refs_3_), channel_id=1, source_target_pairs={{0,1},{1,0},{2,3},{3,2},{4,6},{5,7},{6,4},{7,5},{8,9},{9,8},{10,11... | collective-permute-start | bytes 3686408 | tf_op jit(solution)/shard_map/ppermute | solution.py:84
  182.5 17.5 %collective-permute-start.34 = (bf16[1,160,256]{2,1,0:T(8,128)(2,1)}, bf16[1,160,256]{2,1,0:T(8,128)(2,1)S(1)}, u32[]{:S(2)}, u32[]{:S(2)}) collective-permute-start(bf16[1,160,256]{2,1,0:T(8,128)(2,1)} %bitcast.76), channel_id=1, source_target_pairs={{0,1},{1,0},{2,3},{3,2},{4,6},{5,7},{6,4},{7,5},{8,9},{9,8},{10,11... | collective-permute-start | bytes 245768 | tf_op jit(solution)/shard_map/ppermute | solution.py:84
  195.1 16.6 %collective-permute-start.38 = (bf16[1,320,768]{2,1,0:T(8,128)(2,1)}, bf16[1,320,768]{2,1,0:T(8,128)(2,1)S(1)}, u32[]{:S(2)}, u32[]{:S(2)}) collective-permute-start(bf16[1,320,768]{2,1,0:T(8,128)(2,1)} %bitcast.57), channel_id=1, source_target_pairs={{0,1},{1,0},{2,3},{3,2},{4,6},{5,7},{6,4},{7,5},{8,9},{9,8},{10,11... | collective-permute-start | bytes 1474568 | tf_op jit(solution)/shard_map/ppermute | solution.py:84
  210.9 14.9 %collective-permute-start.41 = (bf16[32,1280]{1,0:T(8,128)(2,1)S(1)}, bf16[32,1280]{1,0:T(8,128)(2,1)S(1)}, u32[]{:S(2)}, u32[]{:S(2)}) collective-permute-start(bf16[32,1280]{1,0:T(8,128)(2,1)S(1)} %copy-done.52), channel_id=1, source_target_pairs={{0,4},{1,5},{2,6},{3,7},{4,0},{5,1},{6,2},{7,3},{8,12},{9,13},{10,... | collective-permute-start | bytes 245768 | tf_op jit(solution)/shard_map/ppermute | solution.py:84
  215.1 19.8 %collective-permute-start.43 = (bf16[2,192,320]{2,1,0:T(8,128)(2,1)}, bf16[2,192,320]{2,1,0:T(8,128)(2,1)S(1)}, u32[]{:S(2)}, u32[]{:S(2)}) collective-permute-start(bf16[2,192,320]{2,1,0:T(8,128)(2,1)} %get-tuple-element.163.refs_2_), channel_id=1, source_target_pairs={{0,8},{1,9},{2,10},{3,11},{4,12},{5,13},{6,14},{7,15},{8,0},{9,1},... | collective-permute-start | bytes 737288 | tf_op jit(solution)/shard_map/ppermute | solution.py:84
  231.1 19.5 %collective-permute-start.44 = (bf16[2,320,512]{2,1,0:T(8,128)(2,1)}, bf16[2,320,512]{2,1,0:T(8,128)(2,1)S(1)}, u32[]{:S(2)}, u32[]{:S(2)}) collective-permute-start(bf16[2,320,512]{2,1,0:T(8,128)(2,1)} %get-tuple-element.166.refs_2_), channel_id=1, source_target_pairs={{0,8},{1,9},{2,10},{3,11},{4,12},{5,13},{6,14},{7,15},{8,0},{9,1},... | collective-permute-start | bytes 1966088 | tf_op jit(solution)/shard_map/ppermute | solution.py:84
  237.3 19.1 %collective-permute-start.48 = (bf16[1,192,320]{2,1,0:T(8,128)(2,1)}, bf16[1,192,320]{2,1,0:T(8,128)(2,1)S(1)}, u32[]{:S(2)}, u32[]{:S(2)}) collective-permute-start(bf16[1,192,320]{2,1,0:T(8,128)(2,1)} %bitcast.68), channel_id=1, source_target_pairs={{0,16},{1,17},{2,18},{3,19},{4,20},{5,21},{6,22},{7,23},{8,24},{9,... | collective-permute-start | bytes 368648 | tf_op jit(solution)/shard_map/ppermute | solution.py:84
  262.5 17.5 %collective-permute-start.45 = (bf16[1,320,512]{2,1,0:T(8,128)(2,1)S(1)}, bf16[1,320,512]{2,1,0:T(8,128)(2,1)S(1)}, u32[]{:S(2)}, u32[]{:S(2)}) collective-permute-start(bf16[1,320,512]{2,1,0:T(8,128)(2,1)S(1)} %bitcast.58), channel_id=1, source_target_pairs={{0,16},{1,17},{2,18},{3,19},{4,20},{5,21},{6,22},{7,23},{8,24},{9,... | collective-permute-start | bytes 983048 | tf_op jit(solution)/shard_map/ppermute | solution.py:84
  (91 other events, 427.9 us)

commit v2 on v1

--- a/solution.py
+++ b/solution.py
@@ -47,9 +47,9 @@
 def adam_step(weight, first, root, average, gradient):
     moment_one = beta_one * first + (1.0 - beta_one) * gradient
     root_two = jnp.sqrt(beta_two * root * root + (1.0 - beta_two) * gradient * gradient)
-    corrected_one = moment_one / (1.0 - beta_one**STEP)
-    denominator = root_two / math.sqrt(1.0 - beta_two**STEP) + adam_eps
-    new_weight = weight - learn_rate * (corrected_one / denominator + decay_rate * weight)
+    corrected_one = moment_one * (learn_rate / (1.0 - beta_one**STEP))
+    denominator = root_two * (1.0 / math.sqrt(1.0 - beta_two**STEP)) + adam_eps
+    new_weight = weight * (1.0 - learn_rate * decay_rate) - corrected_one / denominator
     ema_new = ema_keep * average + (1.0 - ema_keep) * new_weight
     return new_weight, ema_new, moment_one, root_two
 
@@ -105,13 +105,19 @@
     def near(self, x):
         return [self.swap_hid(x, m) for m in range(1, self.H)]
 
-    def sum_all(self, x):
+    def near_chips(self, x):
+        return [self.swap_seq(x, 2 * m) for m in range(1, self.S // 2)]
+
+    def sum_all(self, x, last):
         x = x + self.swap_core(x)
-        for i in range(self.hb):
-            x = x + self.swap_hid(x, 1 << i)
-        for i in range(1, self.sb):
-            x = x + self.swap_seq(x, 1 << i)
-        return x
+        x = tree_sum([x] + self.near(x))
+        return tree_sum([x] + after(self.near_chips(x), last))
+
+
+def tree_sum(terms):
+    while len(terms) > 1:
+        terms = [a + b for a, b in zip(terms[::2], terms[1::2])]
+    return terms[0]
 
 
 class Place:
@@ -144,21 +150,32 @@
 
 
 spent = {
-    "kv_weight": 2.6,
-    "token_norm": 5.0,
-    "other_weights": 4.7,
-    "kv": 10.0,
-    "attention": 8.0,
+    "kv_weight": 5.0,
+    "first_weight": 0.1,
+    "query": 4.0,
+    "token_norm": 10.0,
+    "other_weights": 0.1,
+    "kv": 0.1,
+    "attention": 0.1,
+    "kv_turned": 0.1,
     "latent": 11.0,
-    "square_send": 5.0,
-    "square_keep": 5.0,
-    "square_top": 6.0,
+    "square_grad": 5.0,
+    "attention_back": 12.0,
+    "token_grad_0": 0.1,
+    "query_core": 0.1,
     "square_step": 4.0,
-    "square_turn": 4.0,
-    "attention_back": 12.0,
-    "kv_send": 6.5,
-    "kv_keep": 6.5,
-    "token_grad": 4.0,
+    "query_hid": 0.1,
+    "kv_grad": 1.0,
+    "query_chips": 10.0,
+    "square_turn": 0.1,
+    "query_back": 0.1,
+    "kv_step": 0.1,
+    "square_chip_step": 0.1,
+    "kv_turn": 0.1,
+    "latent_end": 3.0,
+    "token_grad_1": 0.1,
+    "kv_chip_step": 0.1,
+    "square_end": 3.0,
     "update": 7.0,
 }
 
@@ -188,13 +205,19 @@
             scratch_shapes=list(scratch),
             compiler_params=pltpu.CompilerParams(vmem_limit_bytes=56 * 1024 * 1024),
             cost_estimate=pl.CostEstimate(
-                flops=int(spent.get(name, 2.0) * 3e9), bytes_accessed=0, transcendentals=0
+                flops=int(spent.get(name, 2.0) * 1e9), bytes_accessed=0, transcendentals=0
             ),
             name=name,
             input_output_aliases={} if onto is None else {1 + n: 0},
         )(self.where, *args, *waits)
-        self.last = [results[0]]
+        self.last = [results[-1]]
         return results
+
+    def tree(self, terms, name):
+        def kernel(where, *refs):
+            refs[-1][...] = tree_sum([x[...].astype(f32) for x in refs[:-1]]).astype(bf16)
+
+        return self(kernel, terms, [like(terms[0].shape, bf16)], name=name)[0]
 
     def add(self, terms, block, count, name):
         shape = terms[0].shape[1:]
@@ -265,15 +288,12 @@
 
 
 def query_kernel(H, where, *refs):
-    near, (w0, lat_all, mine, other, turned) = refs[:H], refs[H:]
+    near, (w0, lat_all, query) = refs[:H], refs[H:]
     at = Place(where, H)
     n = near[0].shape[0]
     for m, x in enumerate(near):
         lat_all[rows_at(at.j ^ m, n), :] = x[...]
-    turned[...] = dot(w0[...], lat_all[...], 1, 1).astype(bf16)
-    half_wide = mine.shape[0]
-    mine[...] = turned[rows_at(at.core, half_wide), :]
-    other[...] = turned[rows_at(1 - at.core, half_wide), :]
+    query[...] = dot(w0[...], lat_all[...], 1, 1).astype(bf16)
 
 
 def token_kernel(where, inputs, mask, in_params, out, turned):
@@ -284,19 +304,43 @@
     turned[...] = low.T
 
 
+def started(copies):
+    for copy in copies:
+        copy.start()
+    return copies
+
+
+def waited(copies):
+    for copy in copies:
+        copy.wait()
+
+
 def kv_kernel(H, where, in_turned, *refs):
-    halves, (kv, weights, sems) = refs[: 2 * H], refs[2 * H :]
+    halves, (kv, kv_all, weights, product, sems, out_sems) = refs[: 2 * H], refs[2 * H :]
     at = Place(where, H)
     wide = halves[0].shape[0]
     d_lat = wide * H
-    copies = []
-    for i, (block, which) in enumerate(at.halves()):
-        copies.append(pltpu.make_async_copy(halves[i], weights.at[which, rows_at(block, wide), :], sems.at[i]))
-        copies[-1].start()
-    for copy in copies:
-        copy.wait()
+    copies = started(
+        [
+            pltpu.make_async_copy(halves[i], weights.at[which, rows_at(block, wide), :], sems.at[i])
+            for i, (block, which) in enumerate(at.halves())
+        ]
+    )
+    waited(copies)
+    outs = started([pltpu.make_async_copy(weights, kv_all, out_sems.at[4])])
     for which in range(2):
-        kv[which] = dot(weights[which], in_turned[...], 1, 0).astype(bf16)
+        for part in range(2):
+            span = slice(part * d_lat // 2, (part + 1) * d_lat // 2)
+            product[which, span, :] = dot(weights[which, span, :], in_turned[...], 1, 0).astype(bf16)
+            copy = pltpu.make_async_copy(
+                product.at[which, span, :], kv.at[which, span, :], out_sems.at[2 * which + part]
+            )
+            outs += started([copy])
+    waited(outs)
+
+
+def kv_turned_kernel(where, kv_all, out):
+    out[0] = kv_all[0].T
 
 
 def three_way(x, lane):
@@ -311,13 +355,12 @@
 
 
 def attention_kernel(H, where, *refs):
-    halves, kv, query = refs[: 2 * H], refs[2 * H], refs[2 * H + 1]
-    packs, mix, packed = refs[2 * H + 2 : -2], refs[-2], refs[-1]
+    near, kv, query = refs[:H], refs[H], refs[H + 1]
+    packs, (mix, packed) = refs[H + 2 : -2], refs[-2:]
     at = Place(where, H)
-    n = halves[0].shape[0]
-    for i, x in enumerate(halves):
-        half = at.core if i < H else 1 - at.core
-        query[rows_at((at.j ^ (i % H)) * 2 + half, n), :] = x[...]
+    n = near[0].shape[0]
+    for m, x in enumerate(near):
+        query[rows_at(at.j ^ m, n), :] = x[...]
     d_lat, nlat = query.shape
     lane = lax.broadcasted_iota(jnp.int32, (nlat, SIDE), 1)
     logs = jnp.zeros((nlat, SIDE), f32)
@@ -347,8 +390,9 @@
     got, refs = refs[:H], refs[H:]
     latents, out_grad, lat_params, refs = refs[0], refs[1], refs[2], refs[3:]
     pieces, refs = refs[: 2 * H], refs[2 * H :]
-    (latents_out, attended, branch_grad, up_grad, mid_low, hidden, grad_y, small, res_sum), refs = refs[:9], refs[9:]
-    backs, (weights, sems, gathered, att, packed) = refs[:H], refs[H:]
+    (latents_out, acts, small, res_mine, res_send), refs = refs[:5], refs[5:]
+    attended, up_grad, hidden, branch_grad, mid_low, grad_y = (acts.at[i] for i in range(6))
+    backs, (weights, sems, gathered, att, packed, res) = refs[:H], refs[H:]
     at = Place(where, H)
     lat_rows, d_lat = latents.shape
     half_wide = pieces[0].shape[1]
@@ -415,7 +459,9 @@
     folded = grad_residual[0:lat_rows]
     for b in range(1, seqs):
         folded = folded + grad_residual[b * lat_rows : (b + 1) * lat_rows]
-    res_sum[...] = folded.astype(bf16)
+    res[...] = folded.astype(bf16)
+    res_mine[...] = res[rows_at(at.core, lat_rows // 2), :]
+    res_send[...] = res[rows_at(1 - at.core, lat_rows // 2), :]
     grad_att = dot(branch_grad[...], weights[0], 1, 1).astype(bf16)
     along = grad_att.astype(f32) * att[...]
     heads = head_lanes((seqs * lat_rows, d_lat))
@@ -437,24 +483,25 @@
         out[...] = packed[(at.j ^ m) // parts]
 
 
-def square_grad_kernel(H, keep, where, *refs):
-    lefts, rights = refs[:3], refs[3:6]
-    top, low, turned = refs[6:]
+def square_grad_kernel(H, where, acts, others, top, low, turned, rights):
     at = Place(where, H)
-    core = at.core if keep else 1 - at.core
+    rows = acts.shape[1]
     for m in range(3):
-        turned[m] = lefts[m][...].T
+        turned[m, :, 0:rows] = acts[m].T
+        turned[m, :, rows:] = others[m].T
+        rights[m, 0:rows, :] = acts[3 + m]
+        rights[m, rows:, :] = others[3 + m]
     half_wide = top.shape[2]
     for r in range(H):
         out = low if r < H // 2 else top
-        at_row = rows_at(at.block(r, core) * 2 + core, half_wide)
+        at_row = rows_at(at.block(r, at.core) * 2 + at.core, half_wide)
         for m in range(3):
-            out[r % (H // 2), m] = dot(turned[m, at_row, :], rights[m][...], 1, 0).astype(bf16)
-
-
-def attention_back_kernel(H, where, query, kv, *refs):
+            out[r % (H // 2), m] = dot(turned[m, at_row, :], rights[m], 1, 0).astype(bf16)
+
+
+def attention_back_kernel(H, where, query, *refs):
     backs, refs = refs[:H], refs[H:]
-    grad_kv, send_top, send_low, keep_top, keep_low, packed, turned, grad_q = refs
+    kv, mine, send, q_keep, q_send, packed, turned, grad_q, grad_kv = refs
     at = Place(where, H)
     d_lat, nlat = query.shape
     lat_rows = nlat // H
@@ -471,8 +518,18 @@
         grad_scores = (probs * (grad_probs - side[:, 3 * HEADS + h : 3 * HEADS + h + 1])).astype(bf16)
         grad_q[span, :] = (dot(kv[0, span, :], grad_scores, 1, 1) * score_scale).astype(bf16)
         grad_kv[0, span, :] = (dot(query[span, :], grad_scores, 1, 0) * score_scale).astype(bf16)
-    slots_out(at, 1 - at.core, grad_q, send_top, send_low)
-    slots_out(at, at.core, grad_q, keep_top, keep_low)
+    n = q_keep.shape[1]
+    for m in range(H):
+        block = (at.j ^ m) * 2
+        q_keep[m] = grad_q[rows_at(block + at.core, n), :]
+        q_send[m] = grad_q[rows_at(block + 1 - at.core, n), :]
+    mine[...] = grad_kv[at.core]
+    send[...] = grad_kv[1 - at.core]
+
+
+def query_core_kernel(where, keep, got, *outs):
+    for m, out in enumerate(outs):
+        out[...] = (keep[m].astype(f32) + got[m].astype(f32)).astype(bf16)
 
 
 def slots_out(at, core, whole, top, low):
@@ -484,27 +541,26 @@
         out[r % (at.H // 2)] = whole[rows_at(block * 2 + core if per == 2 else block, n), :]
 
 
-def kv_grad_kernel(H, keep, where, grad_kv, in_low, top, low, whole):
+def kv_grad_kernel(H, where, mine, got, in_low, in_other, top, low, whole):
     at = Place(where, H)
-    core = at.core if keep else 1 - at.core
-    whole[...] = dot(grad_kv[core], in_low[...], 1, 0).astype(bf16)
-    slots_out(at, core, whole, top, low)
-
-
-def token_grad_kernel(where, inputs, mask, in_params, grad_kv, weights, inputs_grad, small, normed):
-    normed[...] = dot(grad_kv[0], weights[0], 0, 0) + dot(grad_kv[1], weights[1], 0, 0)
-    rows, d_in = inputs.shape
-    step = min(rows, 128)
-    small[...] = jnp.zeros_like(small)
-    for i in range(rows // step):
-        span = slice(i * step, (i + 1) * step)
-        masked_row = mask[span, :] > 0
-        unit, inverse = unit_norm(jnp.where(masked_row, in_params[2:3, :], inputs[span, :]))
-        upstream = normed[span, :]
-        grad = norm_back(upstream, unit, inverse, in_params[0:1, :])
-        inputs_grad[span, :] = jnp.where(masked_row, 0.0, grad)
-        for r, term in enumerate((upstream * unit, upstream, jnp.where(masked_row, grad, 0.0))):
-            small[0, r : r + 1, :] += jnp.sum(term, 0, keepdims=True)
+    whole[...] = (dot(mine[...], in_low[...], 1, 0) + dot(got[...], in_other[...], 1, 0)).astype(bf16)
+    slots_out(at, at.core, whole, top, low)
+
+
+def token_grad_kernel(where, inputs, mask, in_params, mine, send, weights, inputs_grad, small):
+    core = where[0] & 1
+    upstream = (dot(weights[core], mine[...], 1, 0) + dot(weights[1 - core], send[...], 1, 0)).T
+    masked_row = mask[...] > 0
+    unit, inverse = unit_norm(jnp.where(masked_row, in_params[2:3, :], inputs[...]))
+    grad = norm_back(upstream, unit, inverse, in_params[0:1, :])
+    inputs_grad[...] = jnp.where(masked_row, 0.0, grad)
+
+    @pl.when(pl.program_id(0) == 0)
+    def _():
+        small[...] = jnp.zeros_like(small)
+
+    for r, term in enumerate((upstream * unit, upstream, jnp.where(masked_row, grad, 0.0))):
+        small[0, r : r + 1, :] += jnp.sum(term, 0, keepdims=True)
 
 
 def turn(where, total, turned, top, low):
@@ -548,8 +604,28 @@
     return [pl.BlockSpec(x.shape, lambda i, z=(0,) * len(x.shape): z) for x in arrays]
 
 
-def halve_end_kernel(where, *refs):
-    terms, (mine, other, total) = refs[:-3], refs[-3:]
+def squares(x):
+    return jnp.sum(jnp.sum(x * x, 0, keepdims=True), 1, keepdims=True)
+
+
+def square_end_kernel(where, *refs):
+    terms, (extra, wq_squares, mine, other, total_squares, total) = refs[:-6], refs[-6:]
+    core = where[0] & 1
+    acc = terms[0][0].astype(f32)
+    for x in terms[1:]:
+        acc = acc + x[0].astype(f32)
+    total[...] = acc
+    lanes = extra.shape[1]
+    total[:, acc.shape[1] - lanes :] += extra[...]
+    total_squares[...] = squares(total[...]) + wq_squares[...]
+    n = mine.shape[0]
+    mine[...] = total[rows_at(core, n), :]
+    other[...] = total[rows_at(1 - core, n), :].astype(bf16)
+
+
+def kv_end_kernel(where, *refs):
+    terms, refs = refs[:-9], refs[-9:]
+    sq_squares, lat_small, mid_small, in_a, in_b, mine, other, sums, total = refs
     core = where[0] & 1
     acc = terms[0][0].astype(f32)
     for x in terms[1:]:
@@ -558,69 +634,71 @@
     n = mine.shape[0]
     mine[...] = total[rows_at(core, n), :]
     other[...] = total[rows_at(1 - core, n), :].astype(bf16)
-
-
-def latent_end_kernel(where, mine, other, latents, lat_params, extra, small, turned):
-    core = where[0] & 1
-    first, second = mine[...].astype(f32), other[...].astype(f32)
-    low = jnp.concatenate([jnp.where(core == 0, first, second), jnp.where(core == 0, second, first)], 0)
+    sums[...] = jnp.zeros_like(sums)
+    sums[0:2, :] = lat_small[...]
+    sums[2:4, :] = mid_small[...]
+    sums[4:7, 0 : in_a.shape[2]] = in_a[0] + in_b[0]
+    sums[7:8, :] = jnp.broadcast_to(squares(acc) + sq_squares[...], (1, sums.shape[1]))
+
+
+def latent_end_kernel(H, where, *refs):
+    terms, (latents, lat_params, extra, small, turned) = refs[:H], refs[H:]
+    low = tree_sum([x[...].astype(f32) for x in terms])
     unit, inverse = unit_norm(latents[...])
     once = jnp.where(where[0] == 0, 1.0, 0.0)
     small[0:1, :] = jnp.sum(low * unit, 0, keepdims=True) * once
     small[1:2, :] = jnp.sum(low, 0, keepdims=True) * once
     turned[...] = norm_back(low, unit, inverse, lat_params[0:1, :]).T
-    extra[...] = turned[rows_at(where[0], extra.shape[0]), :]
-
-
-def core_rows_kernel(where, pair, mine, other):
-    core = where[0] & 1
-    n = mine.shape[0]
-    mine[...] = pair[rows_at(core, n), :]
-    other[...] = pair[rows_at(1 - core, n), :]
-
-
-def update_kernel(count, where, sums, *refs):
-    ins, outs = refs[: 3 * (count - 2) + 4], refs[3 * (count - 2) + 4 :]
+    both = turned[rows_at(where[0] >> 1, extra.shape[0]), :]
+    n = extra.shape[1]
+    extra[...] = jnp.where((where[0] & 1) == 0, both[:, 0:n], both[:, n:])
+
+
+def update_kernel(where, sums, *refs):
+    square, kv, refs = refs[:3], refs[3:6], refs[6:]
+    rest, (norm_out, sq_new, sq_moments, kv_new, kv_moments), outs = refs[:7], refs[7:12], refs[12:]
     small = sums[0:7, :]
-    squares = jnp.sum(jnp.sum(small * small, 1, keepdims=True), 0, keepdims=True) + sums[7:8, 0:1]
-    norm = jnp.sqrt(squares)
-    outs[0][...] = norm
+    norm = jnp.sqrt(jnp.sum(jnp.sum(small * small, 1, keepdims=True), 0, keepdims=True) + sums[7:8, 0:1])
     factor = jnp.minimum(1.0, clip_limit / (norm + 1e-06))
-    for i in range(count - 2):
-        weight, state, gradient = ins[3 * i : 3 * i + 3]
-        new, moments = outs[1 + 2 * i : 3 + 2 * i]
-        scale = factor if gradient.ndim == 2 else factor[None]
-        new[0], new[1], moments[0], moments[1] = adam_step(
-            weight[...], state[0], state[1], state[2], gradient[...] * scale
+    for (weight, state, gradient), new, moments in ((square, sq_new, sq_moments), (kv, kv_new, kv_moments)):
+        new[0, 0], new[1, 0], moments[0, 0], moments[1, 0] = adam_step(
+            weight[0], state[0, 0], state[1, 0], state[2, 0], gradient[0] * factor
         )
-    lat_params, lat_state, in_params, in_state = ins[-4:]
-    lat_new, lat_moments, in_new, in_moments, lat_clipped, in_clipped = outs[1 + 2 * (count - 2) :]
-    lat_clipped[...] = sums[0:4, :] * factor
-    lat_new[0], lat_new[1], lat_moments[0], lat_moments[1] = adam_step(
-        lat_params[...], lat_state[0], lat_state[1], lat_state[2], lat_clipped[...]
-    )
-    in_clipped[...] = sums[4:7, 0 : in_params.shape[1]] * factor
-    results = adam_step(in_params[...], in_state[0], in_state[1], in_state[2], in_clipped[...])
-    for i in range(3):
-        row = slice(i, i + 1)
-        in_new[i, 0:1], in_new[i, 1:2], in_moments[i, 0:1], in_moments[i, 1:2] = (x[row] for x in results)
-
-
-def query_back_kernel(H, where, lat_all, w0, mine, other, wq, top, low, grad_q, whole, term):
+
+    @pl.when(pl.program_id(0) == 0)
+    def _():
+        latents, latents_state, lat_grad, lat_params, lat_state, in_params, in_state = rest
+        (latents_new, latents_moments, lat_new, lat_moments, in_new, in_moments, lat_clipped, in_clipped) = outs
+        norm_out[...] = norm
+        latents_new[0], latents_new[1], latents_moments[0], latents_moments[1] = adam_step(
+            latents[...], latents_state[0], latents_state[1], latents_state[2], lat_grad[...] * factor
+        )
+        lat_clipped[...] = sums[0:4, :] * factor
+        lat_new[0], lat_new[1], lat_moments[0], lat_moments[1] = adam_step(
+            lat_params[...], lat_state[0], lat_state[1], lat_state[2], lat_clipped[...]
+        )
+        in_clipped[...] = sums[4:7, 0 : in_params.shape[1]] * factor
+        results = adam_step(in_params[...], in_state[0], in_state[1], in_state[2], in_clipped[...])
+        for i in range(3):
+            row = slice(i, i + 1)
+            in_new[i, 0:1], in_new[i, 1:2], in_moments[i, 0:1], in_moments[i, 1:2] = (x[row] for x in results)
+
+
+def query_back_kernel(H, where, lat_all, w0, mine, other, wq, wq_squares, *refs):
+    outs, (grad_q, whole, term) = refs[:H], refs[H:]
     at = Place(where, H)
     half_wide = mine.shape[0]
     grad_q[rows_at(at.core, half_wide), :] = mine[...]
     grad_q[rows_at(1 - at.core, half_wide), :] = other[...]
     term[...] = dot(grad_q[...], w0[...], 0, 0).astype(bf16)
-    slots_out(at, at.core, term, top, low)
+    for m, out in enumerate(outs):
+        out[...] = term[rows_at(at.j ^ m, out.shape[0]), :]
     whole[...] = dot(lat_all[...], grad_q[...], 0, 1)
     wq[...] = whole[rows_at(at.s, wq.shape[0]), :]
-
-
-def finish_kernel(
-    where, wq, sq_mine, sq_other, kv_mine, kv_other, lat_extra, lat_small, mid_small, in_sums_a, in_sums_b, in_sums_c, in_sums_d,
-    square_grad, kv_grad, lat_grad, sums,
-):
+    wq_squares[...] = squares(wq[...])
+
+
+def finish_kernel(where, wq, sq_mine, sq_other, kv_mine, kv_other, square_grad, kv_grad, lat_grad):
     core = where[0] & 1
     half = wq.shape[1] // 2
     mine, other = sq_mine[...], sq_other[...].astype(f32)
@@ -631,22 +709,9 @@
         square_grad[1 + m, :, half:] = high[:, m * half : (m + 1) * half]
     kv_grad[core] = kv_mine[...]
     kv_grad[1 - core] = kv_other[...].astype(f32)
-    n = lat_extra.shape[1] // 2
+    n = lat_grad.shape[0] // 2
     ends = slice(3 * half, 3 * half + n)
-    lat_grad[...] = (lat_extra[...] + jnp.concatenate([low[:, ends], high[:, ends]], 1)).T
-
-    def squares(x):
-        return jnp.sum(jnp.sum(x * x, 0, keepdims=True), 1, keepdims=True)
-
-    own = slice(0, 3 * half)
-    out = squares(wq[...]) + squares(mine[:, own]) + squares(other[:, own]) + squares(lat_grad[...])
-    out = out + squares(kv_mine[...]) + squares(kv_other[...].astype(f32))
-    sums[...] = jnp.zeros_like(sums)
-    sums[0:2, :] = lat_small[...]
-    sums[2:4, :] = mid_small[...]
-    d_in = in_sums_a.shape[2]
-    sums[4:7, 0:d_in] = (in_sums_a[0] + in_sums_b[0]) + (in_sums_c[0] + in_sums_d[0])
-    sums[7:8, :] = jnp.broadcast_to(out, (1, sums.shape[1]))
+    lat_grad[...] = jnp.concatenate([low[:, ends], high[:, ends]], 1).T
 
 
 def on_device(
@@ -689,6 +754,20 @@
     kv_pair = go(fix(kv_weight_kernel, H), [kv_t], [low(wide, d_in)] * 2, name="kv_weight")
     kv_first = [L.swap_step(kv_pair[0], i) for i in range(L.hb)]
     lat_near = L.near(lat_low)
+    (w0,) = go(
+        first_weight_kernel,
+        [square_t],
+        [low(wide, d_lat)],
+        name="first_weight",
+        grid=(1,),
+        in_specs=[pl.BlockSpec((1, wide, d_lat), lambda i: (0, 0, 0))],
+        out_specs=[pl.BlockSpec((wide, d_lat), lambda i: (0, 0))],
+    )
+    lat_near = [lat_low] + lat_near
+    lat_all, query_mine = go(
+        fix(query_kernel, H), [*lat_near, w0], [low(nlat, d_lat), low(wide, nlat)], name="query"
+    )
+    query_near = [query_mine] + L.near(query_mine)
     mask = mask_flags.reshape(rows, 1)
     step = min(rows, 256)
     in_low, in_turned = go(
@@ -704,27 +783,9 @@
         ],
         out_specs=[pl.BlockSpec((step, d_in), lambda i: (i, 0)), pl.BlockSpec((d_in, step), lambda i: (0, i))],
     )
-    (w0,) = go(
-        first_weight_kernel,
-        [square_t],
-        [low(wide, d_lat)],
-        name="first_weight",
-        grid=(1,),
-        in_specs=[pl.BlockSpec((1, wide, d_lat), lambda i: (0, 0, 0))],
-        out_specs=[pl.BlockSpec((wide, d_lat), lambda i: (0, 0))],
-    )
-    kv_first = [after(x, w0) for x in kv_first]
+    kv_first = after(kv_first, query_mine)
     kv_mine = [kv_pair[0]] + L.spread(kv_first)
     kv_halves = kv_mine + [kv_pair[1]] + [L.swap_core(x) for x in kv_mine[1:]]
-    lat_near = [lat_low] + [after(x, *kv_first) for x in lat_near]
-    lat_all, query_mine, query_other = go(
-        fix(query_kernel, H),
-        [*lat_near, w0],
-        [low(nlat, d_lat)] + [low(half_wide, nlat)] * 2,
-        [pltpu.VMEM((wide, nlat), bf16)],
-        name="query",
-    )
-    query_near = L.near(query_mine)
     sq_mine, sq_other = go(
         fix(other_weight_kernel, H),
         [square_t],
@@ -734,38 +795,58 @@
         in_specs=[pl.BlockSpec((1, wide, d_lat), lambda i: (1 + i, 0, 0))],
         out_specs=[pl.BlockSpec((1, half_wide, d_lat), lambda i: (i, 0, 0))] * 2,
     )
-    sq_sent = after(sq_mine, kv_mine[-1])
+    sq_sent = after(sq_mine, kv_mine[-1], *query_near)
     sq_near = [L.swap_step(sq_sent, i) for i in range(L.hb)]
 
     kv, kv_all = go(
         fix(kv_kernel, H),
         [in_turned, *kv_halves],
         [low(2, d_lat, rows), low(2, d_lat, d_in)],
-        [pltpu.SemaphoreType.DMA((2 * H,))],
+        [
+            pltpu.VMEM((2, d_lat, d_in), bf16),
+            pltpu.VMEM((2, d_lat, rows), bf16),
+            pltpu.SemaphoreType.DMA((2 * H,)),
+            pltpu.SemaphoreType.DMA((5,)),
+        ],
         name="kv",
         in_specs=[VMEM] + [ANY] * (2 * H),
+        out_specs=[ANY] * 2,
         after=[sq_sent],
     )
-    query_near = [after(x, kv) for x in query_near]
-    query_halves = [query_mine] + query_near + [query_other] + [L.swap_core(x) for x in query_near]
     query, *packs = go(
         fix(attention_kernel, H),
-        [*query_halves, kv],
+        [*query_near, kv],
         [low(d_lat, nlat)] + [low(lat_rows, d_lat + SIDE)] * H,
-        [pltpu.VMEM((d_lat, nlat), f32), pltpu.VMEM((nlat, d_lat + SIDE), bf16)],
+        [
+            pltpu.VMEM((d_lat, nlat), f32),
+            pltpu.VMEM((nlat, d_lat + SIDE), bf16),
+        ],
         name="attention",
     )
     got = [packs[0]] + [L.swap_hid(packs[m], m) for m in range(1, H)]
-    sq_near = [after(x, *got) for x in sq_near]
+    sq_old = lax.dynamic_slice_in_dim(square, L.s * d_part, d_part, 1)
+    kv_old = lax.dynamic_slice_in_dim(kv_weights, L.s * in_part, in_part, 1)
+    lat_old = lax.dynamic_slice_in_dim(latents, L.s * d_part, d_part, 1)
+    (kv_turned,) = go(
+        kv_turned_kernel,
+        [kv_all],
+        [low(2, d_in, d_lat)],
+        name="kv_turned",
+        grid=(2,),
+        in_specs=[pl.BlockSpec((1, d_lat, d_in), lambda i: (i, 0, 0))],
+        out_specs=[pl.BlockSpec((1, d_in, d_lat), lambda i: (i, 0, 0))],
+        after=[sq_old, kv_old, lat_old],
+    )
+    in_other = L.swap_core(in_low)
+    sq_near = after(sq_near, *got, kv_turned)
     sq_all = [sq_mine] + L.spread(sq_near)
     sq_halves = sq_all + [sq_other] + [L.swap_core(x) for x in sq_all[1:]]
 
-    latents_out, attended, branch_grad, up_grad, mid_low, hidden, grad_y, mid_small, res_sum, *backs = go(
+    latents_out, acts, mid_small, res_mine, res_send, *backs = go(
         fix(latent_kernel, H, parts),
         [*got, latents, out_grad, lat_params, *sq_halves],
-        [full(mine_rows, d_lat)]
-        + [low(mine_rows, d_lat)] * 6
-        + [full(2, d_lat), low(lat_rows, d_lat)]
+        [full(mine_rows, d_lat), low(6, mine_rows, d_lat), full(2, d_lat)]
+        + [low(lat_rows // 2, d_lat)] * 2
         + [low(lat_rows, d_lat + SIDE)] * H,
         [
             pltpu.VMEM((3, d_lat, d_lat), bf16),
@@ -773,69 +854,86 @@
             pltpu.VMEM((H, lat_rows, d_lat + SIDE), bf16),
             pltpu.VMEM((mine_rows, d_lat), f32),
             pltpu.VMEM((seqs, lat_rows, d_lat + SIDE), bf16),
+            pltpu.VMEM((lat_rows, d_lat), bf16),
         ],
         name="latent",
         in_specs=[VMEM] * (H + 3) + [ANY] * (2 * H),
+        after=[in_other],
     )
     back = [backs[0]] + [L.swap_hid(backs[m], m) for m in range(1, H)]
 
-    sq_args = [attended, up_grad, hidden, branch_grad, mid_low, grad_y]
-    sq_scratch = [pltpu.VMEM((3, d_lat, mine_rows), bf16)]
-    sq_like = [low(H // 2, 3, half_wide, d_lat)] * 2
-    sq_send = go(fix(square_grad_kernel, H, False), sq_args, sq_like, sq_scratch, name="square_send")
-    sq_got = [L.swap_core(x) for x in sq_send]
-    sq_keep = go(fix(square_grad_kernel, H, True), sq_args, sq_like, sq_scratch, name="square_keep")
-    sq = Halving(go, [sq_keep[0], sq_got[0]], [sq_keep[1], sq_got[1]], L.hb, L.swap_step, "square")
+    sq_top, sq_low = go(
+        fix(square_grad_kernel, H),
+        [acts, L.swap_core(acts)],
+        [low(H // 2, 3, half_wide, d_lat)] * 2,
+        [pltpu.VMEM((3, d_lat, 2 * mine_rows), bf16), pltpu.VMEM((3, 2 * mine_rows, d_lat), bf16)],
+        name="square_grad",
+    )
+    sq = Halving(go, [sq_top], [sq_low], L.hb, L.swap_step, "square")
     sq.start()
-
-    grad_kv, *gq = go(
+    res_other = L.swap_core(res_send)
+
+    gkv_mine, gkv_send, gq_keep, gq_send = go(
         fix(attention_back_kernel, H),
-        [query, kv, *back],
-        [low(2, d_lat, rows)] + [low(H // 2, half_wide, nlat)] * 4,
+        [query, *back, kv],
+        [low(d_lat, rows)] * 2 + [low(H, half_wide, nlat)] * 2,
         [
             pltpu.VMEM((nlat, d_lat + SIDE), bf16),
             pltpu.VMEM((d_lat, nlat), bf16),
             pltpu.VMEM((d_lat, nlat), bf16),
+            pltpu.VMEM((2, d_lat, rows), bf16),
         ],
         name="attention_back",
-    )
-    gq_got = [L.swap_core(x) for x in gq[:2]]
-    kv_scratch = [pltpu.VMEM((d_lat, d_in), bf16)]
-    kv_like = [low(H // 2, wide, d_in)] * 2
-    kv_send = go(fix(kv_grad_kernel, H, False), [grad_kv, in_low], kv_like, kv_scratch, name="kv_send")
-    kv_got = [L.swap_core(x) for x in kv_send]
-    gq_sums = Halving(go, [gq[2], gq_got[0]], [gq[3], gq_got[1]], L.hb, L.swap_step, "query")
-    gq_sums.start()
-    kv_keep = go(fix(kv_grad_kernel, H, True), [grad_kv, in_low], kv_like, kv_scratch, name="kv_keep")
-    kv_sums = Halving(go, [kv_keep[0], kv_got[0]], [kv_keep[1], kv_got[1]], L.hb, L.swap_step, "kv")
-    kv_sums.start()
-
-    quarter = rows // 4
+        after=[res_other],
+    )
+    gkv_got = L.swap_core(gkv_send)
+    gq_got = L.swap_core(gq_send)
+
     in_sums = []
     inputs_grad = None
+    block = min(rows // 2, 256)
 
     def token_grad():
         nonlocal inputs_grad
-        i = len(in_sums)
-        outs = [full(rows, d_in), full(1, 3, d_in)]
+        first = len(in_sums) * (rows // 2 // block)
         inputs_grad, sums = go(
             token_grad_kernel,
-            [inputs, mask, in_params, grad_kv, kv_all],
-            outs,
-            [pltpu.VMEM((quarter, d_in), f32)],
-            name="token_grad",
-            grid=(1,),
+            [inputs, mask, in_params, gkv_mine, gkv_send, kv_turned],
+            [full(rows, d_in), full(1, 3, d_in)],
+            name="token_grad_%d" % len(in_sums),
+            grid=(rows // 2 // block,),
             in_specs=[
-                pl.BlockSpec((quarter, d_in), lambda g: (i, 0)),
-                pl.BlockSpec((quarter, 1), lambda g: (i, 0)),
+                pl.BlockSpec((block, d_in), lambda g: (first + g, 0)),
+                pl.BlockSpec((block, 1), lambda g: (first + g, 0)),
                 pl.BlockSpec(in_params.shape, lambda g: (0, 0)),
-                pl.BlockSpec((2, d_lat, quarter), lambda g: (0, 0, i)),
-                pl.BlockSpec(kv_all.shape, lambda g: (0, 0, 0)),
+                pl.BlockSpec((d_lat, block), lambda g: (0, first + g)),
+                pl.BlockSpec((d_lat, block), lambda g: (0, first + g)),
+                pl.BlockSpec(kv_turned.shape, lambda g: (0, 0, 0)),
             ],
-            out_specs=[pl.BlockSpec((quarter, d_in), lambda g: (i, 0)), pl.BlockSpec((1, 3, d_in), lambda g: (0, 0, 0))],
+            out_specs=[
+                pl.BlockSpec((block, d_in), lambda g: (first + g, 0)),
+                pl.BlockSpec((1, 3, d_in), lambda g: (0, 0, 0)),
+            ],
             onto=inputs_grad,
         )
         in_sums.append(sums)
+
+    token_grad()
+    gq_all = go(query_core_kernel, [gq_keep, gq_got], [low(half_wide, nlat)] * H, name="query_core")
+    gq_near = [L.swap_hid(gq_all[m], m) for m in range(1, H)]
+    sq.terms = after(sq.terms, *gq_near)
+    sq.step()
+    gq_mine = go.tree([gq_all[0]] + gq_near, "query_hid")
+    gq_chips = L.near_chips(gq_mine)
+    kv_top, kv_low = go(
+        fix(kv_grad_kernel, H),
+        [gkv_mine, gkv_got, in_low, in_other],
+        [low(H // 2, wide, d_in)] * 2,
+        [pltpu.VMEM((d_lat, d_in), bf16)],
+        name="kv_grad",
+    )
+    kv_sums = Halving(go, [kv_top], [kv_low], L.hb, L.swap_step, "kv")
+    kv_sums.start()
 
     lanes = 3 * half_wide + lat_rows // 2
     padded = -(-lanes // 128) * 128
@@ -859,99 +957,107 @@
     def chip_step(x, i):
         return L.swap_seq(x, 2 << (n - 1 - i))
 
-    def end(terms, n, lanes, name):
+    def end(kernel, terms, extra, n, lanes, more, name, after=()):
+        outs = [full(n, lanes), low(n, lanes)] + more
         return go(
-            halve_end_kernel,
-            terms,
-            [full(n, lanes), low(n, lanes)],
+            kernel,
+            [*terms, *extra],
+            outs,
             [pltpu.VMEM((2 * n, lanes), f32)],
             name=name,
             grid=(1,),
-            in_specs=first_blocks(terms),
-            out_specs=[pl.BlockSpec((n, lanes), lambda i: (0, 0))] * 2,
+            in_specs=first_blocks(terms) + whole_blocks(extra),
+            out_specs=whole_blocks(outs),
+            after=after,
         )
 
-    sq.step()
-    gq_sums.step()
-    token_grad()
+    for _ in range(L.hb - 2):
+        sq.step()
+        kv_sums.step()
+    gq_mine = go.tree([gq_mine] + gq_chips, "query_chips")
+    gq_other = L.swap_core(gq_mine)
+    sq_top, sq_low = turn_to_chips(
+        square_turn_kernel, sq.terms, [res_mine, res_other], 2 * d_part, lanes, padded, "square_turn"
+    )
+    sq_chips = Halving(go, [sq_top], [sq_low], n, chip_step, "square_chip")
+    sq_chips.start()
+    wq_part, wq_squares, *lat_blocks = go(
+        fix(query_back_kernel, H),
+        [lat_all, w0, gq_mine, gq_other],
+        [full(d_part, wide), full(1, 1)] + [low(lat_rows, d_lat)] * H,
+        [pltpu.VMEM((wide, nlat), bf16), pltpu.VMEM((d_lat, wide), f32), pltpu.VMEM((nlat, d_lat), bf16)],
+        name="query_back",
+    )
+    lat_near = [L.swap_hid(lat_blocks[m], m) for m in range(1, H)]
     kv_sums.step()
-    for _ in range(L.hb - 2):
-        gq_sums.step()
-        kv_sums.step()
-        sq.step()
-    gq_mine = go.add(gq_sums.terms, 0, 1, "query_sum")
-    gq_near = L.swap_seq(gq_mine, 2)
-    res_mine, res_send = go(core_rows_kernel, [res_sum], [low(lat_rows // 2, d_lat)] * 2, name="latent_rows")
-    res_other = L.swap_core(res_send)
-    token_grad()
+    sq_chips.step()
     kv_top, kv_low = turn_to_chips(kv_turn_kernel, kv_sums.terms, [], 2 * in_part, wide, wide, "kv_turn")
     kv_chips = Halving(go, [kv_top], [kv_low], n, chip_step, "kv_chip")
     kv_chips.start()
-    gq_mine = go.add([gq_mine, gq_near], 0, 1, "query_chip")
-    gq_near = L.swap_seq(gq_mine, 4)
-    token_grad()
-    sq_top, sq_low = turn_to_chips(
-        square_turn_kernel, sq.terms, [res_mine, res_other], 2 * d_part, lanes, padded, "square_turn"
-    )
-    sq_chips = Halving(go, [sq_top], [sq_low], n, chip_step, "square_chip")
-    sq_chips.start()
-    for i in range(2, L.sb):
-        gq_mine = go.add([gq_mine, gq_near], 0, 1, "query_chip")
-        if i + 1 < L.sb:
-            gq_near = L.swap_seq(gq_mine, 2 << i)
-    gq_mine = gq_mine[0]
-    gq_other = L.swap_core(gq_mine)
-    kv_chips.step()
-    wq_part, lat_top, lat_low_half = go(
-        fix(query_back_kernel, H),
-        [lat_all, w0, gq_mine, gq_other],
-        [full(d_part, wide)] + [low(H // 2, lat_rows // 2, d_lat)] * 2,
-        [pltpu.VMEM((wide, nlat), bf16), pltpu.VMEM((d_lat, wide), f32), pltpu.VMEM((nlat, d_lat), bf16)],
-        name="query_back",
-    )
-    lat_sums = Halving(go, [lat_top], [lat_low_half], L.hb, L.swap_step, "latent")
-    lat_sums.start()
-    token_grad()
-    sq_chips.step()
-    for _ in range(L.hb - 1):
-        lat_sums.step()
-    for _ in range(n - 2):
-        kv_chips.step()
-        sq_chips.step()
-    kv_mine, kv_send = end(kv_chips.terms, in_part, wide, "kv_end")
-    kv_other = L.swap_core(kv_send)
-    low_mine = go.add(lat_sums.terms, 0, 1, "latent_sum")[0]
-    low_other = L.swap_core(low_mine)
     lat_extra, lat_small = go(
-        latent_end_kernel,
-        [low_mine, low_other, latents, lat_params],
-        [full(d_part, lat_rows), full(2, d_lat)],
+        fix(latent_end_kernel, H),
+        [lat_blocks[0], *lat_near, latents, lat_params],
+        [full(2 * d_part, lat_rows // 2), full(2, d_lat)],
         [pltpu.VMEM((d_lat, lat_rows), f32)],
         name="latent_end",
     )
-    sq_mine, sq_send = end(sq_chips.terms, d_part, lanes, "square_end")
+    token_grad()
+    kv_chips.step()
+    for _ in range(n - 2):
+        sq_chips.step()
+        kv_chips.step()
+    sq_mine, sq_send, sq_squares = end(
+        square_end_kernel,
+        sq_chips.terms,
+        [lat_extra, wq_squares],
+        d_part,
+        lanes,
+        [full(1, 1)],
+        "square_end",
+    )
     sq_other = L.swap_core(sq_send)
-
-    square_grad, kv_grad, lat_grad, sums = go(
+    kv_mine, kv_send, sums = end(
+        kv_end_kernel,
+        kv_chips.terms,
+        [sq_squares, lat_small, mid_small, *in_sums],
+        in_part,
+        wide,
+        [full(8, d_lat)],
+        "kv_end",
+    )
+    kv_other = L.swap_core(kv_send)
+
+    square_grad, kv_grad, lat_grad = go(
         finish_kernel,
-        [wq_part, sq_mine, sq_other, kv_mine, kv_other, lat_extra, lat_small, mid_small, *in_sums],
-        [full(4, d_part, wide), full(2, in_part, wide), full(lat_rows, d_part), full(8, d_lat)],
+        [wq_part, sq_mine, sq_other, kv_mine, kv_other],
+        [full(4, d_part, wide), full(2, in_part, wide), full(lat_rows, d_part)],
         name="finish",
     )
-    sums = L.sum_all(sums)
-    sq_old = lax.dynamic_slice_in_dim(square, L.s * d_part, d_part, 1)
-    kv_old = lax.dynamic_slice_in_dim(kv_weights, L.s * in_part, in_part, 1)
-    lat_old = lax.dynamic_slice_in_dim(latents, L.s * d_part, d_part, 1)
+    sums = L.sum_all(sums, square_grad)
     pair = [full(3, 2, d_in)] * 2
-    outs = [full(1, 1)]
-    for x in (sq_old, kv_old, lat_old, lat_params):
-        outs += [full(2, *x.shape)] * 2
+    rest = [lat_old, latents_state, lat_grad, lat_params, lat_state, in_params, in_state]
+    outs = [full(2, *lat_old.shape)] * 2 + [full(2, *lat_params.shape)] * 2 + pair
+    outs += [full(*lat_params.shape), full(*in_params.shape)]
+    half = in_part // 2
+    sq_out = pl.BlockSpec((2, 1, d_part, wide), lambda g: (0, g, 0, 0))
+    kv_out = pl.BlockSpec((2, 1, half, wide), lambda g: (0, g // 2, g % 2, 0))
     results = go(
-        fix(update_kernel, 5),
-        [sums, sq_old, square_state, square_grad, kv_old, kv_state, kv_grad, lat_old, latents_state, lat_grad]
-        + [lat_params, lat_state, in_params, in_state],
-        outs + pair + [full(*lat_params.shape), full(*in_params.shape)],
+        update_kernel,
+        [sums, sq_old, square_state, square_grad, kv_old, kv_state, kv_grad, *rest],
+        [full(1, 1)] + [full(2, *sq_old.shape)] * 2 + [full(2, *kv_old.shape)] * 2 + outs,
         name="update",
+        grid=(4,),
+        in_specs=whole_blocks([sums])
+        + [
+            pl.BlockSpec((1, d_part, wide), lambda g: (g, 0, 0)),
+            pl.BlockSpec((3, 1, d_part, wide), lambda g: (0, g, 0, 0)),
+            pl.BlockSpec((1, d_part, wide), lambda g: (g, 0, 0)),
+            pl.BlockSpec((1, half, wide), lambda g: (g // 2, g % 2, 0)),
+            pl.BlockSpec((3, 1, half, wide), lambda g: (0, g // 2, g % 2, 0)),
+            pl.BlockSpec((1, half, wide), lambda g: (g // 2, g % 2, 0)),
+        ]
+        + whole_blocks(rest),
+        out_specs=whole_blocks([full(1, 1)]) + [sq_out] * 2 + [kv_out] * 2 + whole_blocks(outs),
     )
     (grad_norm, square_new, square_moments, kv_new, kv_moments, latents_new, latents_moments) = results[:7]
     (lat_new, lat_moments, in_new, in_moments, lat_clipped, in_clipped) = results[7:]

time: 319 us -> 277 us (0.87)
  waiting for transfers between devices: 78.1 us -> 45.8 us
  Pallas kernels: 161 us -> 147 us
  starting transfers between devices: 44.8 us -> 52.6 us
    ppermute x57 -> x56, waiting for transfers between devices: 78.1 us -> 45.8 us  [swap(): return lax.ppermute(x, ('seq', 'hid'), pairs)]
    pallas_call x40 -> x30, Pallas kernels: 161 us -> 147 us  [__call__(): pl.pallas_call(body, out_shape=outs, grid=grid, in_specs=[SMEM] + (in_spe...]
    ppermute x57 -> x56, starting transfers between devices: 44.8 us -> 52.6 us  [swap(): return lax.ppermute(x, ('seq', 'hid'), pairs)]
    unnamed x134 -> x106, local copies, waits for them, and re-layouts: 21.5 us -> 19 us
  transfers between devices with their start and end apart: 57 -> 56, of which waited for: 22 -> 18; matrix products, arithmetic and copies ran while one was open for 3% -> 3% of each run, Pallas kernels for 40% -> 45%
where the time goes in v2:
time: 277 us; the launch traced here: 274 us
  Pallas kernels  147 us (53%)
  starting transfers between devices  52.6 us (19%)
  waiting for transfers between devices  45.8 us (17%)
  local copies, waits for them, and re-layouts  24.8 us (9%)
    pallas_call x30, Pallas kernels, __call__(): pl.pallas_call(body, out_shape=outs, grid=grid, in_specs=[SMEM] + (in_spe...  147 us
    ppermute x56, starting transfers between devices, swap(): return lax.ppermute(x, ('seq', 'hid'), pairs)  52.6 us
    ppermute x56, waiting for transfers between devices, swap(): return lax.ppermute(x, ('seq', 'hid'), pairs)  45.8 us
    unnamed x106, local copies, waits for them, and re-layouts  19 us
  transfers between devices with their start and end apart: 56, of which 18 were waited for; matrix products, arithmetic and copies ran while one was open for 3% of the time, Pallas kernels for 45%

profile of v2, /device:TPU:0, one launch (start us, length us, event | category | flops | bytes accessed | tf_op | source)
XLA Modules:
  0.0 273.8 jit_solution(16122560732111381530)
XLA Ops:
  3.1 3.9 %collective-permute-start.2 = (bf16[64,1280]{1,0:T(8,128)(2,1)}, bf16[64,1280]{1,0:T(8,128)(2,1)S(1)}, u32[]{:S(2)}, u32[]{:S(2)}) collective-permute-start(bf16[64,1280]{1,0:T(8,128)(2,1)} %lat_norm.1.refs_1_.refs_0_), channel_id=1, source_target_pairs={{0,3},{1,2},{2,1},{3,0},{4,7},{5,6},{6,5},{7,4},{8,11},{9,10},{10,... | collective-permute-start | bytes 491528 | tf_op jit(solution)/shard_map/ppermute | solution.py:84
  7.6 2.6 kv_weight.1
  14.7 2.5 first_weight.1.refs_4_.refs_5_.refs_1_
  18.6 2.6 query.1
  24.7 3.5 %collective-permute-done.7.refs_3_ = bf16[320,768]{1,0:T(8,128)(2,1)S(1)} collective-permute-done((bf16[320,768]{1,0:T(8,128)(2,1)}, bf16[320,768]{1,0:T(8,128)(2,1)S(1)}, u32[]{:S(2)}, u32[]{:S(2)}) %collective-permute-start.7) | collective-permute-done | bytes 491552 | tf_op jit(solution)/shard_map/ppermute | solution.py:84
  28.5 4.9 %token_norm.1 = (bf16[1024,768]{1,0:T(8,128)(2,1)}, bf16[768,1024]{1,0:T(8,128)(2,1)}) custom-call(s32[2]{0:T(128)} %pad_add_fusion.where, f32[1024,768]{1,0:T(8,128)} %refs_0_.7, s32[1024,1]{1,0:T(8,128)} %copy.34.refs_1_, f32[3,768]{1,0:T(4,128)} %refs_12_.1, bf16[320,256]{1,0:T(8,128)(2,1)} %get-tuple-element.100.refs_3_.refs_0_), custom_call_target="tpu_custom_call" | custom-call | flops 10000000000 | tf_op jit(solution)/shard_map/token_norm/pallas_call | solution.py:199
  33.4 4.7 %other_weights.1 = (bf16[3,160,1280]{2,1,0:T(8,128)(2,1)}, bf16[3,160,1280]{2,1,0:T(8,128)(2,1)}) custom-call(s32[2]{0:T(128)} %pad_add_fusion.where, f32[4,320,1280]{2,1,0:T(8,128)} %bitcast.25, bf16[768,1024]{1,0:T(8,128)(2,1)} %get-tuple-element.101.refs_1_.refs_0_), custom_call_target="tpu_custom_call" | custom-call | flops 100000000 | tf_op jit(solution)/shard_map/other_weights/pallas_call | solution.py:199
  43.6 8.9 %kv.1 = (bf16[2,1280,1024]{2,1,0:T(8,128)(2,1)}, bf16[2,1280,768]{2,1,0:T(8,128)(2,1)}) custom-call(s32[2]{0:T(128)} %pad_add_fusion.where, bf16[768,1024]{1,0:T(8,128)(2,1)} %get-tuple-element.101.refs_1_.refs_0_, bf16[320,768]{1,0:T(8,128)(2,1)} %get-tuple-element.102.refs_1_, bf16[320,768]{1,0:T(8,128)(2,1)} %copy-done.8, bf16[320,768]{1,0:T(8,128)(2,1)} %copy-done.7, ...), custom_call_target="tpu_custom_call" | custom-call | flops 100000000 | tf_op jit(solution)/shard_map/kv/pallas_call | solution.py:199
  52.6 7.8 %attention.1 = (bf16[1280,256]{1,0:T(8,128)(2,1)}, bf16[64,1408]{1,0:T(8,128)(2,1)}, bf16[64,1408]{1,0:T(8,128)(2,1)}, bf16[64,1408]{1,0:T(8,128)(2,1)}, bf16[64,1408]{1,0:T(8,128)(2,1)}) custom-call(s32[2]{0:T(128)} %pad_add_fusion.where, bf16[320,256]{1,0:T(8,128)(2,1)} %get-tuple-element.100.refs_3_.refs_0_, bf16[320,256]{1,0:T(8,128)(2,1)} %copy-done.18, ...), custom_call_target="tpu_custom_call" | custom-call | flops 100000000 | tf_op jit(solution)/shard_map/attention/pallas_call | solution.py:199
  69.0 4.4 %kv_turned.1.refs_15_.refs_5_ = bf16[2,768,1280]{2,1,0:T(8,128)(2,1)} custom-call(s32[2]{0:T(128)} %pad_add_fusion.where, bf16[2,1280,768]{2,1,0:T(8,128)(2,1)} %get-tuple-element.109.refs_5_.refs_0_, bf16[64,1408]{1,0:T(8,128)(2,1)} %get-tuple-element.113.refs_1_, f32[4,160,320]{2,1,0:T(8,128)} %copy.42.refs_2_.refs_1_, ...), custom_call_target="tpu_custom_call" | custom-call | flops 100000000 | tf_op jit(solution)/shard_map/kv_turned/pallas_call | solution.py:199
  77.4 15.6 %collective-permute-done.17.refs_10_ = bf16[3,160,1280]{2,1,0:T(8,128)(2,1)S(1)} collective-permute-done((bf16[3,160,1280]{2,1,0:T(8,128)(2,1)}, bf16[3,160,1280]{2,1,0:T(8,128)(2,1)S(1)}, u32[]{:S(2)}, u32[]{:S(2)}) %collective-permute-start.17) | collective-permute-done | bytes 1228832 | tf_op jit(solution)/shard_map/ppermute | solution.py:84
  93.1 2.9 %collective-permute-done.20.refs_14_ = bf16[3,160,1280]{2,1,0:T(8,128)(2,1)S(1)} collective-permute-done((bf16[3,160,1280]{2,1,0:T(8,128)(2,1)S(1)}, bf16[3,160,1280]{2,1,0:T(8,128)(2,1)S(1)}, u32[]{:S(2)}, u32[]{:S(2)}) %collective-permute-start.20) | collective-permute-done | bytes 1228832 | tf_op jit(solution)/shard_map/ppermute | solution.py:84
  97.0 10.8 %latent.1 = (f32[128,1280]{1,0:T(8,128)}, bf16[6,128,1280]{2,1,0:T(8,128)(2,1)}, f32[2,1280]{1,0:T(2,128)}, bf16[32,1280]{1,0:T(8,128)(2,1)}, bf16[32,1280]{1,0:...) custom-call(s32[2]{0:T(128)} %pad_add_fusion.where, ...), custom_call_target="tpu_custom_call" | custom-call | flops 11000000512 | tf_op jit(solution)/shard_map/latent/pallas_call | solution.py:199
  113.3 5.6 %square_grad.1 = (bf16[2,3,160,1280]{3,2,1,0:T(8,128)(2,1)}, bf16[2,3,160,1280]{3,2,1,0:T(8,128)(2,1)}) custom-call(s32[2]{0:T(128)} %pad_add_fusion.where, bf16[6,128,1280]{2,1,0:T(8,128)(2,1)} %get-tuple-element.123.refs_0_, bf16[6,128,1280]{2,1,0:T(8,128)(2,1)} %copy-done.25, bf16[64,1408]{1,0:T(8,128)(2,1)} %get-tuple-element.122.refs_2_), custom_call_target="tpu_custom_call" | custom-call | flops 5000000000 | tf_op jit(solution)/shard_map/square_grad/pallas_call | solution.py:199
  120.6 24.7 %attention_back.1 = (bf16[1280,1024]{1,0:T(8,128)(2,1)}, bf16[1280,1024]{1,0:T(8,128)(2,1)}, bf16[4,160,256]{2,1,0:T(8,128)(2,1)}, bf16[4,160,256]{2,1,0:T(8,128)(2,1)}) custom-call(s32[2]{0:T(128)} %pad_add_fusion.where, bf16[1280,256]{1,0:T(8,128)(2,1)} %get-tuple-element.118.refs_0_, bf16[64,1408]{1,0:T(8,128)(2,1)} %get-tuple-element.119.refs_1_, ...), custom_call_target="tpu_custom_call" | custom-call | flops 12000000000 | tf_op jit(solution)/shard_map/attention_back/pallas_call | solution.py:199
  145.8 7.2 %token_grad_0.1 = (f32[1024,768]{1,0:T(8,128)}, f32[1,3,768]{2,1,0:T(4,128)}) custom-call(s32[2]{0:T(128)} %pad_add_fusion.where, f32[1024,768]{1,0:T(8,128)} %refs_0_.7, s32[1024,1]{1,0:T(8,128)} %copy.34.refs_1_, f32[3,768]{1,0:T(4,128)} %refs_12_.1, bf16[1280,1024]{1,0:T(8,128)(2,1)} %get-tuple-element.126.refs_3_.refs_0_, ...), custom_call_target="tpu_custom_call" | custom-call | flops 100000000 | tf_op jit(solution)/shard_map/token_grad_0/pallas_call | solution.py:199
  160.2 2.9 %collective-permute-done.29.refs_2_ = bf16[160,256]{1,0:T(8,128)(2,1)S(1)} collective-permute-done((bf16[160,256]{1,0:T(8,128)(2,1)}, bf16[160,256]{1,0:T(8,128)(2,1)S(1)}, u32[]{:S(2)}, u32[]{:S(2)}) %collective-permute-start.29) | collective-permute-done | bytes 81952 | tf_op jit(solution)/shard_map/ppermute | solution.py:84
  164.5 3.6 %square_step.1.refs_4_ = bf16[1,3,160,1280]{3,2,1,0:T(8,128)(2,1)} custom-call(s32[2]{0:T(128)} %pad_add_fusion.where, bf16[2,3,160,1280]{3,2,1,0:T(8,128)(2,1)} %get-tuple-element.138.refs_6_.refs_0_, bf16[2,3,160,1280]{3,2,1,0:T(8,128)(2,1)} %copy-done.2, bf16[160,256]{1,0:T(8,128)(2,1)} %get-tuple-element.136.refs_2_), custom_call_target="tpu_custom_call" | custom-call | flops 4000000000 | tf_op jit(solution)/shard_map/square_step/pallas_call | solution.py:199
  171.1 3.6 %collective-permute-start.34 = (bf16[160,256]{1,0:T(8,128)(2,1)}, bf16[160,256]{1,0:T(8,128)(2,1)S(1)}, u32[]{:S(2)}, u32[]{:S(2)}) collective-permute-start(bf16[160,256]{1,0:T(8,128)(2,1)} %query_hid.1.refs_4_.refs_0_), channel_id=1, source_target_pairs={{0,24},{1,25},{2,26},{3,27},{4,28},{5,29},{6,30},{7,31},{8,16},{9,... | collective-permute-start | bytes 245768 | tf_op jit(solution)/shard_map/ppermute | solution.py:84
  177.0 9.0 %kv_grad.1 = (bf16[2,320,768]{2,1,0:T(8,128)(2,1)}, bf16[2,320,768]{2,1,0:T(8,128)(2,1)}) custom-call(s32[2]{0:T(128)} %pad_add_fusion.where, bf16[1280,1024]{1,0:T(8,128)(2,1)} %get-tuple-element.126.refs_3_.refs_0_, bf16[1280,1024]{1,0:T(8,128)(2,1)} %copy-done.1, bf16[1024,768]{1,0:T(8,128)(2,1)} %get-tuple-element.116.refs_2_, ...), custom_call_target="tpu_custom_call" | custom-call | flops 1000000000 | tf_op jit(solution)/shard_map/kv_grad/pallas_call | solution.py:199
  190.3 3.8 %square_turn.1 = (bf16[2,320,512]{2,1,0:T(8,128)(2,1)}, bf16[2,320,512]{2,1,0:T(8,128)(2,1)}) custom-call(s32[2]{0:T(128)} %pad_add_fusion.where, bf16[2,3,160,1280]{3,2,1,0:T(8,128)(2,1)} %get-tuple-element.138.refs_6_.refs_0_, bf16[2,3,160,1280]{3,2,1,0:T(8,128)(2,1)} %copy-done.2, bf16[1,3,160,1280]{3,2,1,0:T(8,128)(2,1)} %copy-done.5, ...), custom_call_target="tpu_custom_call" | custom-call | flops 100000000 | tf_op jit(solution)/shard_map/square_turn/pallas_call | solution.py:199
  197.3 3.1 %query_back.1 = (f32[160,320]{1,0:T(8,128)}, f32[1,1]{1,0:T(1,128)}, bf16[64,1280]{1,0:T(8,128)(2,1)}, bf16[64,1280]{1,0:T(8,128)(2,1)}, bf16[64,1280]{1,0:T(8,128)(2,1)}, /*index=5*/bf16[64,1280]{1,0:T(8,128)(2,1)}) custom-call(s32[2]{0:T(128)} %pad_add_fusion.where, bf16[256,1280]{1,0:T(8,128)(2,1)} %get-tuple-element.130.refs_0_, ...), custom_call_target="tpu_custom_call" | custom-call | flops 100000000 | tf_op jit(solution)/shard_map/query_back/pallas_call | solution.py:199
  210.8 2.9 %collective-permute-start.46 = (bf16[1,320,512]{2,1,0:T(8,128)(2,1)}, bf16[1,320,512]{2,1,0:T(8,128)(2,1)S(1)}, u32[]{:S(2)}, u32[]{:S(2)}) collective-permute-start(bf16[1,320,512]{2,1,0:T(8,128)(2,1)} %bitcast.30), channel_id=1, source_target_pairs={{0,16},{1,17},{2,18},{3,19},{4,20},{5,21},{6,22},{7,23},{8,24},{9,... | collective-permute-start | bytes 983048 | tf_op jit(solution)/shard_map/ppermute | solution.py:84
  216.6 2.5 kv_turn.1
  220.7 2.6 latent_end.1
  223.4 7.2 %token_grad_1.1 = (f32[1024,768]{1,0:T(8,128)}, f32[1,3,768]{2,1,0:T(4,128)}) custom-call(s32[2]{0:T(128)} %pad_add_fusion.where, f32[1024,768]{1,0:T(8,128)} %refs_0_.7, s32[1024,1]{1,0:T(8,128)} %copy.34.refs_1_, f32[3,768]{1,0:T(4,128)} %refs_12_.1, bf16[1280,1024]{1,0:T(8,128)(2,1)} %get-tuple-element.126.refs_3_.refs_0_, ...), custom_call_target="tpu_custom_call", output_to_operand_aliasing={{0}: (7, {})} | custom-call | flops 100000000 | tf_op jit(solution)/shard_map/token_grad_1/pallas_call | solution.py:199
  230.6 3.6 %collective-permute-done.44.refs_1_ = bf16[2,192,320]{2,1,0:T(8,128)(2,1)S(1)} collective-permute-done((bf16[2,192,320]{2,1,0:T(8,128)(2,1)}, bf16[2,192,320]{2,1,0:T(8,128)(2,1)S(1)}, u32[]{:S(2)}, u32[]{:S(2)}) %collective-permute-start.44) | collective-permute-done | bytes 245792 | tf_op jit(solution)/shard_map/ppermute | solution.py:84
  237.3 2.9 %square_end.1 = (f32[160,512]{1,0:T(8,128)}, bf16[160,512]{1,0:T(8,128)(2,1)}, f32[1,1]{1,0:T(1,128)}) custom-call(s32[2]{0:T(128)} %pad_add_fusion.where, bf16[2,320,512]{2,1,0:T(8,128)(2,1)} %get-tuple-element.142.refs_4_.refs_0_, bf16[2,320,512]{2,1,0:T(8,128)(2,1)} %copy-done.6, bf16[1,320,512]{2,1,0:T(8,128)(2,1)} %copy-done.30, ...), custom_call_target="tpu_custom_call" | custom-call | flops 3000000000 | tf_op jit(solution)/shard_map/square_end/pallas_call | solution.py:199
  240.2 5.5 %collective-permute-done.45.refs_2_ = bf16[1,192,320]{2,1,0:T(8,128)(2,1)S(1)} collective-permute-done((bf16[1,192,320]{2,1,0:T(8,128)(2,1)}, bf16[1,192,320]{2,1,0:T(8,128)(2,1)S(1)}, u32[]{:S(2)}, u32[]{:S(2)}) %collective-permute-start.45) | collective-permute-done | bytes 122912 | tf_op jit(solution)/shard_map/ppermute | solution.py:84
  246.4 3.3 %kv_end.1 = (f32[96,320]{1,0:T(8,128)}, bf16[96,320]{1,0:T(8,128)(2,1)}, f32[8,1280]{1,0:T(8,128)}) custom-call(s32[2]{0:T(128)} %pad_add_fusion.where, bf16[2,192,320]{2,1,0:T(8,128)(2,1)} %get-tuple-element.149.refs_6_.refs_0_, bf16[2,192,320]{2,1,0:T(8,128)(2,1)} %copy-done.14, bf16[1,192,320]{2,1,0:T(8,128)(2,1)} %copy-done.47, ...), custom_call_target="tpu_custom_call" | custom-call | flops 2000000000 | tf_op jit(solution)/shard_map/kv_end/pallas_call | solution.py:199
  263.3 2.6 finish.1
  266.6 7.0 %update.1 = (f32[1,1]{1,0:T(1,128)}, f32[2,4,160,320]{3,2,1,0:T(8,128)}, f32[2,4,160,320]{3,2,1,0:T(8,128)}, f32[2,2,96,320]{3,2,1,0:T(8,128)}, f32[2,2,96,320]{...) custom-call(s32[2]{0:T(128)} %pad_add_fusion.where, ...), custom_call_target="tpu_custom_call" | custom-call | flops 7000000000 | tf_op jit(solution)/shard_map/update/pallas_call | solution.py:199
  (224 shorter events, 93.7 us)
Async XLA Ops:
  3.1 14.1 %collective-permute-start.2 = (bf16[64,1280]{1,0:T(8,128)(2,1)}, bf16[64,1280]{1,0:T(8,128)(2,1)S(1)}, u32[]{:S(2)}, u32[]{:S(2)}) collective-permute-start(bf16[64,1280]{1,0:T(8,128)(2,1)} %lat_norm.1.refs_1_.refs_0_), channel_id=1, source_target_pairs={{0,3},{1,2},{2,1},{3,0},{4,7},{5,6},{6,5},{7,4},{8,11},{9,10},{10,... | collective-permute-start | bytes 491528 | tf_op jit(solution)/shard_map/ppermute | solution.py:84
  10.2 18.0 %collective-permute-start.7 = (bf16[320,768]{1,0:T(8,128)(2,1)}, bf16[320,768]{1,0:T(8,128)(2,1)S(1)}, u32[]{:S(2)}, u32[]{:S(2)}) collective-permute-start(bf16[320,768]{1,0:T(8,128)(2,1)} %get-tuple-element.102.refs_1_), channel_id=1, source_target_pairs={{0,2},{1,3},{2,0},{3,1},{4,5},{5,4},{6,7},{7,6},{8,10},{9,11},{10,... | collective-permute-start | bytes 1474568 | tf_op jit(solution)/shard_map/ppermute | solution.py:84
  12.2 16.0 %collective-permute-start.6 = (bf16[320,768]{1,0:T(8,128)(2,1)}, bf16[320,768]{1,0:T(8,128)(2,1)S(1)}, u32[]{:S(2)}, u32[]{:S(2)}) collective-permute-start(bf16[320,768]{1,0:T(8,128)(2,1)} %get-tuple-element.102.refs_1_), channel_id=1, source_target_pairs={{0,1},{1,0},{2,3},{3,2},{4,6},{5,7},{6,4},{7,5},{8,9},{9,8},{10,11... | collective-permute-start | bytes 1474568 | tf_op jit(solution)/shard_map/ppermute | solution.py:84
  21.2 16.9 %collective-permute-start.5 = (bf16[320,256]{1,0:T(8,128)(2,1)}, bf16[320,256]{1,0:T(8,128)(2,1)S(1)}, u32[]{:S(2)}, u32[]{:S(2)}) collective-permute-start(bf16[320,256]{1,0:T(8,128)(2,1)} %get-tuple-element.100.refs_3_.refs_0_), channel_id=1, source_target_pairs={{0,3},{1,2},{2,1},{3,0},{4,7},{5,6},{6,5},{7,4},{8,11},{9,10},{10,... | collective-permute-start | bytes 491528 | tf_op jit(solution)/shard_map/ppermute | solution.py:84
  21.6 16.5 %collective-permute-start.4 = (bf16[320,256]{1,0:T(8,128)(2,1)}, bf16[320,256]{1,0:T(8,128)(2,1)S(1)}, u32[]{:S(2)}, u32[]{:S(2)}) collective-permute-start(bf16[320,256]{1,0:T(8,128)(2,1)} %get-tuple-element.100.refs_3_.refs_0_), channel_id=1, source_target_pairs={{0,2},{1,3},{2,0},{3,1},{4,6},{5,7},{6,4},{7,5},{8,10},{9,11},{10,... | collective-permute-start | bytes 491528 | tf_op jit(solution)/shard_map/ppermute | solution.py:84
  23.2 14.9 %collective-permute-start.3 = (bf16[320,256]{1,0:T(8,128)(2,1)}, bf16[320,256]{1,0:T(8,128)(2,1)S(1)}, u32[]{:S(2)}, u32[]{:S(2)}) collective-permute-start(bf16[320,256]{1,0:T(8,128)(2,1)} %get-tuple-element.100.refs_3_.refs_0_), channel_id=1, source_target_pairs={{0,1},{1,0},{2,3},{3,2},{4,5},{5,4},{6,7},{7,6},{8,9},{9,8},{10,11... | collective-permute-start | bytes 491528 | tf_op jit(solution)/shard_map/ppermute | solution.py:84
  38.2 37.8 %collective-permute-start.16 = (bf16[3,160,1280]{2,1,0:T(8,128)(2,1)}, bf16[3,160,1280]{2,1,0:T(8,128)(2,1)}, u32[]{:S(2)}, u32[]{:S(2)}) collective-permute-start(bf16[3,160,1280]{2,1,0:T(8,128)(2,1)} %get-tuple-element.107.refs_10_.refs_7_), channel_id=1, source_target_pairs={{0,2},{1,3},{2,0},{3,1},{4,5},{5,4},{6,7},{7,6},{8,10},{9,11},{10,... | collective-permute-start | bytes 3686408 | tf_op jit(solution)/shard_map/ppermute | solution.py:84
  40.0 36.0 %collective-permute-start.15 = (bf16[3,160,1280]{2,1,0:T(8,128)(2,1)}, bf16[3,160,1280]{2,1,0:T(8,128)(2,1)}, u32[]{:S(2)}, u32[]{:S(2)}) collective-permute-start(bf16[3,160,1280]{2,1,0:T(8,128)(2,1)} %get-tuple-element.107.refs_10_.refs_7_), channel_id=1, source_target_pairs={{0,1},{1,0},{2,3},{3,2},{4,6},{5,7},{6,4},{7,5},{8,9},{9,8},{10,11... | collective-permute-start | bytes 3686408 | tf_op jit(solution)/shard_map/ppermute | solution.py:84
  60.3 13.1 %collective-permute-start.12 = (bf16[64,1408]{1,0:T(8,128)(2,1)}, bf16[64,1408]{1,0:T(8,128)(2,1)S(1)}, u32[]{:S(2)}, u32[]{:S(2)}) collective-permute-start(bf16[64,1408]{1,0:T(8,128)(2,1)} %get-tuple-element.111), channel_id=1, source_target_pairs={{0,1},{1,0},{2,3},{3,2},{4,5},{5,4},{6,7},{7,6},{8,9},{9,8},{10,11... | collective-permute-start | bytes 540680 | tf_op jit(solution)/shard_map/ppermute | solution.py:84
  62.2 13.8 %collective-permute-start.13 = (bf16[64,1408]{1,0:T(8,128)(2,1)}, bf16[64,1408]{1,0:T(8,128)(2,1)S(1)}, u32[]{:S(2)}, u32[]{:S(2)}) collective-permute-start(bf16[64,1408]{1,0:T(8,128)(2,1)} %get-tuple-element.112), channel_id=1, source_target_pairs={{0,2},{1,3},{2,0},{3,1},{4,6},{5,7},{6,4},{7,5},{8,10},{9,11},{10,... | collective-permute-start | bytes 540680 | tf_op jit(solution)/shard_map/ppermute | solution.py:84
  62.4 13.6 %collective-permute-start.14 = (bf16[64,1408]{1,0:T(8,128)(2,1)}, bf16[64,1408]{1,0:T(8,128)(2,1)S(1)}, u32[]{:S(2)}, u32[]{:S(2)}) collective-permute-start(bf16[64,1408]{1,0:T(8,128)(2,1)} %get-tuple-element.113.refs_1_), channel_id=1, source_target_pairs={{0,3},{1,2},{2,1},{3,0},{4,7},{5,6},{6,5},{7,4},{8,11},{9,10},{10,... | collective-permute-start | bytes 540680 | tf_op jit(solution)/shard_map/ppermute | solution.py:84
  76.0 17.0 %collective-permute-start.17 = (bf16[3,160,1280]{2,1,0:T(8,128)(2,1)}, bf16[3,160,1280]{2,1,0:T(8,128)(2,1)S(1)}, u32[]{:S(2)}, u32[]{:S(2)}) collective-permute-start(bf16[3,160,1280]{2,1,0:T(8,128)(2,1)} %collective-permute-done.15.refs_8_), channel_id=1, source_target_pairs={{0,2},{1,3},{2,0},{3,1},{4,5},{5,4},{6,7},{7,6},{8,10},{9,11},{10,... | collective-permute-start | bytes 3686408 | tf_op jit(solution)/shard_map/ppermute | solution.py:84
  76.9 16.2 %collective-permute-start.21 = (bf16[1024,768]{1,0:T(8,128)(2,1)S(1)}, bf16[1024,768]{1,0:T(8,128)(2,1)S(1)}, u32[]{:S(2)}, u32[]{:S(2)}) collective-permute-start(bf16[1024,768]{1,0:T(8,128)(2,1)S(1)} %copy-done.3), channel_id=1, source_target_pairs={{0,4},{1,5},{2,6},{3,7},{4,0},{5,1},{6,2},{7,3},{8,12},{9,13},{10,... | collective-permute-start | bytes 4718600 | tf_op jit(solution)/shard_map/ppermute | solution.py:84
  76.9 16.2 %collective-permute-start.18 = (bf16[3,160,1280]{2,1,0:T(8,128)(2,1)}, bf16[3,160,1280]{2,1,0:T(8,128)(2,1)S(1)}, u32[]{:S(2)}, u32[]{:S(2)}) collective-permute-start(bf16[3,160,1280]{2,1,0:T(8,128)(2,1)} %collective-permute-done.15.refs_8_), channel_id=1, source_target_pairs={{0,4},{1,5},{2,6},{3,7},{4,0},{5,1},{6,2},{7,3},{8,12},{9,13},{10,... | collective-permute-start | bytes 3686408 | tf_op jit(solution)/shard_map/ppermute | solution.py:84
  77.4 15.7 %collective-permute-start.19 = (bf16[3,160,1280]{2,1,0:T(8,128)(2,1)}, bf16[3,160,1280]{2,1,0:T(8,128)(2,1)S(1)}, u32[]{:S(2)}, u32[]{:S(2)}) collective-permute-start(bf16[3,160,1280]{2,1,0:T(8,128)(2,1)} %collective-permute-done.16.refs_9_), channel_id=1, source_target_pairs={{0,4},{1,5},{2,6},{3,7},{4,0},{5,1},{6,2},{7,3},{8,12},{9,13},{10,... | collective-permute-start | bytes 3686408 | tf_op jit(solution)/shard_map/ppermute | solution.py:84
  108.0 11.7 %collective-permute-start.26 = (bf16[32,1280]{1,0:T(8,128)(2,1)}, bf16[32,1280]{1,0:T(8,128)(2,1)S(1)}, u32[]{:S(2)}, u32[]{:S(2)}) collective-permute-start(bf16[32,1280]{1,0:T(8,128)(2,1)} %get-tuple-element.125), channel_id=1, source_target_pairs={{0,4},{1,5},{2,6},{3,7},{4,0},{5,1},{6,2},{7,3},{8,12},{9,13},{10,... | collective-permute-start | bytes 245768 | tf_op jit(solution)/shard_map/ppermute | solution.py:84
  108.4 11.4 %collective-permute-start.22 = (bf16[64,1408]{1,0:T(8,128)(2,1)}, bf16[64,1408]{1,0:T(8,128)(2,1)S(1)}, u32[]{:S(2)}, u32[]{:S(2)}) collective-permute-start(bf16[64,1408]{1,0:T(8,128)(2,1)} %get-tuple-element.120), channel_id=1, source_target_pairs={{0,1},{1,0},{2,3},{3,2},{4,5},{5,4},{6,7},{7,6},{8,9},{9,8},{10,11... | collective-permute-start | bytes 540680 | tf_op jit(solution)/shard_map/ppermute | solution.py:84
  108.9 10.9 %collective-permute-start.23 = (bf16[64,1408]{1,0:T(8,128)(2,1)}, bf16[64,1408]{1,0:T(8,128)(2,1)S(1)}, u32[]{:S(2)}, u32[]{:S(2)}) collective-permute-start(bf16[64,1408]{1,0:T(8,128)(2,1)} %get-tuple-element.121), channel_id=1, source_target_pairs={{0,2},{1,3},{2,0},{3,1},{4,6},{5,7},{6,4},{7,5},{8,10},{9,11},{10,... | collective-permute-start | bytes 540680 | tf_op jit(solution)/shard_map/ppermute | solution.py:84
  119.0 44.0 %collective-permute-start.31 = (bf16[2,3,160,1280]{3,2,1,0:T(8,128)(2,1)}, bf16[2,3,160,1280]{3,2,1,0:T(8,128)(2,1)S(1)}, u32[]{:S(2)}, u32[]{:S(2)}) collective-permute-start(bf16[2,3,160,1280]{3,2,1,0:T(8,128)(2,1)} %get-tuple-element.137), channel_id=1, source_target_pairs={{0,2},{1,3},{2,0},{3,1},{4,5},{5,4},{6,7},{7,6},{8,10},{9,11},{10,... | collective-permute-start | bytes 7372808 | tf_op jit(solution)/shard_map/ppermute | solution.py:84
  145.2 30.3 %collective-permute-start.35 = (bf16[1280,1024]{1,0:T(8,128)(2,1)}, bf16[1280,1024]{1,0:T(8,128)(2,1)S(1)}, u32[]{:S(2)}, u32[]{:S(2)}) collective-permute-start(bf16[1280,1024]{1,0:T(8,128)(2,1)} %get-tuple-element.127.refs_4_), channel_id=1, source_target_pairs={{0,4},{1,5},{2,6},{3,7},{4,0},{5,1},{6,2},{7,3},{8,12},{9,13},{10,... | collective-permute-start | bytes 7864328 | tf_op jit(solution)/shard_map/ppermute | solution.py:84
  168.1 21.2 %collective-permute-start.37 = (bf16[1,3,160,1280]{3,2,1,0:T(8,128)(2,1)}, bf16[1,3,160,1280]{3,2,1,0:T(8,128)(2,1)S(1)}, u32[]{:S(2)}, u32[]{:S(2)}) collective-permute-start(bf16[1,3,160,1280]{3,2,1,0:T(8,128)(2,1)} %square_step.1.refs_4_), channel_id=1, source_target_pairs={{0,1},{1,0},{2,3},{3,2},{4,6},{5,7},{6,4},{7,5},{8,9},{9,8},{10,11... | collective-permute-start | bytes 3686408 | tf_op jit(solution)/shard_map/ppermute | solution.py:84
  171.1 15.8 %collective-permute-start.34 = (bf16[160,256]{1,0:T(8,128)(2,1)}, bf16[160,256]{1,0:T(8,128)(2,1)S(1)}, u32[]{:S(2)}, u32[]{:S(2)}) collective-permute-start(bf16[160,256]{1,0:T(8,128)(2,1)} %query_hid.1.refs_4_.refs_0_), channel_id=1, source_target_pairs={{0,24},{1,25},{2,26},{3,27},{4,28},{5,29},{6,30},{7,31},{8,16},{9,... | collective-permute-start | bytes 245768 | tf_op jit(solution)/shard_map/ppermute | solution.py:84
  174.7 12.2 %collective-permute-start.33 = (bf16[160,256]{1,0:T(8,128)(2,1)}, bf16[160,256]{1,0:T(8,128)(2,1)S(1)}, u32[]{:S(2)}, u32[]{:S(2)}) collective-permute-start(bf16[160,256]{1,0:T(8,128)(2,1)} %query_hid.1.refs_4_.refs_0_), channel_id=1, source_target_pairs={{0,16},{1,17},{2,18},{3,19},{4,20},{5,21},{6,22},{7,23},{8,24},{9,... | collective-permute-start | bytes 245768 | tf_op jit(solution)/shard_map/ppermute | solution.py:84
  174.7 12.3 %collective-permute-start.32 = (bf16[160,256]{1,0:T(8,128)(2,1)}, bf16[160,256]{1,0:T(8,128)(2,1)S(1)}, u32[]{:S(2)}, u32[]{:S(2)}) collective-permute-start(bf16[160,256]{1,0:T(8,128)(2,1)} %query_hid.1.refs_4_.refs_0_), channel_id=1, source_target_pairs={{0,8},{1,9},{2,10},{3,11},{4,12},{5,13},{6,14},{7,15},{8,0},{9,1},... | collective-permute-start | bytes 245768 | tf_op jit(solution)/shard_map/ppermute | solution.py:84
  186.1 14.3 %collective-permute-start.41 = (bf16[2,320,768]{2,1,0:T(8,128)(2,1)}, bf16[2,320,768]{2,1,0:T(8,128)(2,1)S(1)}, u32[]{:S(2)}, u32[]{:S(2)}) collective-permute-start(bf16[2,320,768]{2,1,0:T(8,128)(2,1)} %get-tuple-element.147), channel_id=1, source_target_pairs={{0,2},{1,3},{2,0},{3,1},{4,5},{5,4},{6,7},{7,6},{8,10},{9,11},{10,... | collective-permute-start | bytes 2949128 | tf_op jit(solution)/shard_map/ppermute | solution.py:84
  194.2 13.9 %collective-permute-start.43 = (bf16[2,320,512]{2,1,0:T(8,128)(2,1)}, bf16[2,320,512]{2,1,0:T(8,128)(2,1)S(1)}, u32[]{:S(2)}, u32[]{:S(2)}) collective-permute-start(bf16[2,320,512]{2,1,0:T(8,128)(2,1)} %get-tuple-element.148), channel_id=1, source_target_pairs={{0,8},{1,9},{2,10},{3,11},{4,12},{5,13},{6,14},{7,15},{8,0},{9,1},... | collective-permute-start | bytes 1966088 | tf_op jit(solution)/shard_map/ppermute | solution.py:84
  203.4 12.4 %collective-permute-start.42 = (bf16[1,320,768]{2,1,0:T(8,128)(2,1)}, bf16[1,320,768]{2,1,0:T(8,128)(2,1)S(1)}, u32[]{:S(2)}, u32[]{:S(2)}) collective-permute-start(bf16[1,320,768]{2,1,0:T(8,128)(2,1)} %bitcast.29), channel_id=1, source_target_pairs={{0,1},{1,0},{2,3},{3,2},{4,6},{5,7},{6,4},{7,5},{8,9},{9,8},{10,11... | collective-permute-start | bytes 1474568 | tf_op jit(solution)/shard_map/ppermute | solution.py:84
  204.5 15.4 %collective-permute-start.38 = (bf16[64,1280]{1,0:T(8,128)(2,1)S(1)}, bf16[64,1280]{1,0:T(8,128)(2,1)S(1)}, u32[]{:S(2)}, u32[]{:S(2)}) collective-permute-start(bf16[64,1280]{1,0:T(8,128)(2,1)S(1)} %copy-done.39), channel_id=1, source_target_pairs={{0,1},{1,0},{2,3},{3,2},{4,5},{5,4},{6,7},{7,6},{8,9},{9,8},{10,11... | collective-permute-start | bytes 491528 | tf_op jit(solution)/shard_map/ppermute | solution.py:84
  205.5 14.5 %collective-permute-start.39 = (bf16[64,1280]{1,0:T(8,128)(2,1)S(1)}, bf16[64,1280]{1,0:T(8,128)(2,1)S(1)}, u32[]{:S(2)}, u32[]{:S(2)}) collective-permute-start(bf16[64,1280]{1,0:T(8,128)(2,1)S(1)} %copy-done.38), channel_id=1, source_target_pairs={{0,2},{1,3},{2,0},{3,1},{4,6},{5,7},{6,4},{7,5},{8,10},{9,11},{10,... | collective-permute-start | bytes 491528 | tf_op jit(solution)/shard_map/ppermute | solution.py:84
  206.6 13.3 %collective-permute-start.40 = (bf16[64,1280]{1,0:T(8,128)(2,1)S(1)}, bf16[64,1280]{1,0:T(8,128)(2,1)S(1)}, u32[]{:S(2)}, u32[]{:S(2)}) collective-permute-start(bf16[64,1280]{1,0:T(8,128)(2,1)S(1)} %copy-done.15), channel_id=1, source_target_pairs={{0,3},{1,2},{2,1},{3,0},{4,7},{5,6},{6,5},{7,4},{8,11},{9,10},{10,... | collective-permute-start | bytes 491528 | tf_op jit(solution)/shard_map/ppermute | solution.py:84
  210.8 25.8 %collective-permute-start.46 = (bf16[1,320,512]{2,1,0:T(8,128)(2,1)}, bf16[1,320,512]{2,1,0:T(8,128)(2,1)S(1)}, u32[]{:S(2)}, u32[]{:S(2)}) collective-permute-start(bf16[1,320,512]{2,1,0:T(8,128)(2,1)} %bitcast.30), channel_id=1, source_target_pairs={{0,16},{1,17},{2,18},{3,19},{4,20},{5,21},{6,22},{7,23},{8,24},{9,... | collective-permute-start | bytes 983048 | tf_op jit(solution)/shard_map/ppermute | solution.py:84
  219.1 15.1 %collective-permute-start.44 = (bf16[2,192,320]{2,1,0:T(8,128)(2,1)}, bf16[2,192,320]{2,1,0:T(8,128)(2,1)S(1)}, u32[]{:S(2)}, u32[]{:S(2)}) collective-permute-start(bf16[2,192,320]{2,1,0:T(8,128)(2,1)} %get-tuple-element.152), channel_id=1, source_target_pairs={{0,8},{1,9},{2,10},{3,11},{4,12},{5,13},{6,14},{7,15},{8,0},{9,1},... | collective-permute-start | bytes 737288 | tf_op jit(solution)/shard_map/ppermute | solution.py:84
  (76 other events, 308.6 us)

commit v3 on v2

--- a/solution.py
+++ b/solution.py
@@ -74,6 +74,10 @@
         self.s = lax.axis_index("seq")
         self.j = lax.axis_index("hid")
         self.core = self.s & 1
+        self.paired = self.H == 4 and self.S >= 4
+
+    def side(self, s):
+        return (s & 1) ^ ((s >> 1) & 1) if self.paired else s & 1
 
     def swap(self, x, dest):
         pairs = []
@@ -94,9 +98,14 @@
 
     def swap_step(self, x, i):
         even, odd = 1 << i, 1 << (self.hb - 1 - i)
-        return self.swap(x, lambda s, j: (s, j ^ (odd if s & 1 else even)))
+        return self.swap(x, lambda s, j: (s, j ^ (odd if self.side(s) else even)))
+
+    def first(self, x):
+        return [self.swap_step(x, i) for i in range(1 if self.paired else self.hb)]
 
     def spread(self, first):
+        if self.paired:
+            return [first[0], self.swap_seq(first[0], 2), self.swap_step(first[0], 1)]
         blocks = [None]
         for i, x in enumerate(first):
             blocks += [x] + [self.swap_step(y, i) for y in blocks[1:]]
@@ -127,9 +136,10 @@
         self.s = where[0]
         self.j = where[1]
         self.core = self.s & 1
+        self.parity = where[2]
 
     def block(self, r, core):
-        return self.j ^ jnp.where(core == 0, r, flip(r, self.hb))
+        return self.j ^ jnp.where((core ^ self.parity) == 0, r, flip(r, self.hb))
 
     def halves(self):
         mine = [(self.block(r, self.core), self.core) for r in range(self.H)]
@@ -161,7 +171,7 @@
     "latent": 11.0,
     "square_grad": 5.0,
     "attention_back": 12.0,
-    "token_grad_0": 0.1,
+    "token_grad_0": 22.0,
     "query_core": 0.1,
     "square_step": 4.0,
     "query_hid": 0.1,
@@ -731,7 +741,8 @@
 ):
     L = Links()
     S, H = L.S, L.H
-    go = Order(jnp.stack([L.s, L.j]).astype(jnp.int32))
+    parity = (L.s >> 1) & 1 if L.paired else 0 * L.s
+    go = Order(jnp.stack([L.s, L.j, parity]).astype(jnp.int32))
     rows, d_in = inputs.shape
     parts = SEQ_LEN // rows
     seqs = H // parts
@@ -752,7 +763,7 @@
     square_t, kv_t = jnp.swapaxes(square, 1, 2), jnp.swapaxes(kv_weights, 1, 2)
     (lat_low,) = go(lat_kernel, [latents, lat_params], [low(lat_rows, d_lat)], name="lat_norm")
     kv_pair = go(fix(kv_weight_kernel, H), [kv_t], [low(wide, d_in)] * 2, name="kv_weight")
-    kv_first = [L.swap_step(kv_pair[0], i) for i in range(L.hb)]
+    kv_first = L.first(kv_pair[0])
     lat_near = L.near(lat_low)
     (w0,) = go(
         first_weight_kernel,
@@ -795,8 +806,8 @@
         in_specs=[pl.BlockSpec((1, wide, d_lat), lambda i: (1 + i, 0, 0))],
         out_specs=[pl.BlockSpec((1, half_wide, d_lat), lambda i: (i, 0, 0))] * 2,
     )
-    sq_sent = after(sq_mine, kv_mine[-1], *query_near)
-    sq_near = [L.swap_step(sq_sent, i) for i in range(L.hb)]
+    sq_sent = after(sq_mine, *kv_mine[1:], *query_near)
+    sq_first = L.first(sq_sent)
 
     kv, kv_all = go(
         fix(kv_kernel, H),
@@ -813,6 +824,8 @@
         out_specs=[ANY] * 2,
         after=[sq_sent],
     )
+    sq_all = [sq_mine] + L.spread(after(sq_first, kv))
+    in_other = L.swap_core(in_low)
     query, *packs = go(
         fix(attention_kernel, H),
         [*query_near, kv],
@@ -822,6 +835,7 @@
             pltpu.VMEM((nlat, d_lat + SIDE), bf16),
         ],
         name="attention",
+        after=[in_other],
     )
     got = [packs[0]] + [L.swap_hid(packs[m], m) for m in range(1, H)]
     sq_old = lax.dynamic_slice_in_dim(square, L.s * d_part, d_part, 1)
@@ -837,9 +851,7 @@
         out_specs=[pl.BlockSpec((1, d_in, d_lat), lambda i: (i, 0, 0))],
         after=[sq_old, kv_old, lat_old],
     )
-    in_other = L.swap_core(in_low)
-    sq_near = after(sq_near, *got, kv_turned)
-    sq_all = [sq_mine] + L.spread(sq_near)
+    sq_all = after(sq_all, *got, kv_turned)
     sq_halves = sq_all + [sq_other] + [L.swap_core(x) for x in sq_all[1:]]
 
     latents_out, acts, mid_small, res_mine, res_send, *backs = go(
@@ -858,7 +870,6 @@
         ],
         name="latent",
         in_specs=[VMEM] * (H + 3) + [ANY] * (2 * H),
-        after=[in_other],
     )
     back = [backs[0]] + [L.swap_hid(backs[m], m) for m in range(1, H)]
 
@@ -918,9 +929,9 @@
         )
         in_sums.append(sums)
 
-    token_grad()
     gq_all = go(query_core_kernel, [gq_keep, gq_got], [low(half_wide, nlat)] * H, name="query_core")
     gq_near = [L.swap_hid(gq_all[m], m) for m in range(1, H)]
+    token_grad()
     sq.terms = after(sq.terms, *gq_near)
     sq.step()
     gq_mine = go.tree([gq_all[0]] + gq_near, "query_hid")

time: 277 us -> 270 us (0.975)
  waiting for transfers between devices: 45.8 us -> 34.3 us
    ppermute x56, waiting for transfers between devices: 45.8 us -> 34.3 us  [swap(): return lax.ppermute(x, ('seq', 'hid'), pairs)]
  transfers between devices with their start and end apart: 56 -> 56, of which waited for: 18 -> 21; matrix products, arithmetic and copies ran while one was open for 3% -> 3% of each run, Pallas kernels for 45% -> 47%
where the time goes in v3:
time: 270 us; the launch traced here: 265 us
  Pallas kernels  147 us (54%)
  starting transfers between devices  53.5 us (20%)
  waiting for transfers between devices  34.3 us (13%)
  local copies, waits for them, and re-layouts  26.7 us (10%)
    pallas_call x30, Pallas kernels, __call__(): pl.pallas_call(body, out_shape=outs, grid=grid, in_specs=[SMEM] + (in_spe...  147 us
    ppermute x56, starting transfers between devices, swap(): return lax.ppermute(x, ('seq', 'hid'), pairs)  53.5 us
    ppermute x56, waiting for transfers between devices, swap(): return lax.ppermute(x, ('seq', 'hid'), pairs)  34.3 us
    unnamed x106, local copies, waits for them, and re-layouts  20.9 us
  transfers between devices with their start and end apart: 56, of which 21 were waited for; matrix products, arithmetic and copies ran while one was open for 3% of the time, Pallas kernels for 47%

profile of v3, /device:TPU:0, one launch (start us, length us, event | category | flops | bytes accessed | tf_op | source)
XLA Modules:
  0.0 264.9 jit_solution(10758849281307044952)
XLA Ops:
  3.1 3.9 %collective-permute-start.2 = (bf16[64,1280]{1,0:T(8,128)(2,1)}, bf16[64,1280]{1,0:T(8,128)(2,1)S(1)}, u32[]{:S(2)}, u32[]{:S(2)}) collective-permute-start(bf16[64,1280]{1,0:T(8,128)(2,1)} %lat_norm.1.refs_1_.refs_0_), channel_id=1, source_target_pairs={{0,3},{1,2},{2,1},{3,0},{4,7},{5,6},{6,5},{7,4},{8,11},{9,10},{10,... | collective-permute-start | bytes 491528 | tf_op jit(solution)/shard_map/ppermute | solution.py:88
  7.6 2.6 kv_weight.1
  13.2 2.5 first_weight.1.refs_4_.refs_5_.refs_1_
  17.1 2.6 query.1
  26.3 4.9 %token_norm.1 = (bf16[1024,768]{1,0:T(8,128)(2,1)}, bf16[768,1024]{1,0:T(8,128)(2,1)}) custom-call(s32[3]{0:T(128)} %pad_add_fusion.where, f32[1024,768]{1,0:T(8,128)} %refs_0_.7, s32[1024,1]{1,0:T(8,128)} %copy.34.refs_1_, f32[3,768]{1,0:T(4,128)} %refs_12_.1, bf16[320,256]{1,0:T(8,128)(2,1)} %get-tuple-element.102.refs_3_.refs_0_), custom_call_target="tpu_custom_call" | custom-call | flops 10000000000 | tf_op jit(solution)/shard_map/token_norm/pallas_call | solution.py:209
  31.2 4.7 %other_weights.1 = (bf16[3,160,1280]{2,1,0:T(8,128)(2,1)}, bf16[3,160,1280]{2,1,0:T(8,128)(2,1)}) custom-call(s32[3]{0:T(128)} %pad_add_fusion.where, f32[4,320,1280]{2,1,0:T(8,128)} %bitcast.26, bf16[768,1024]{1,0:T(8,128)(2,1)} %get-tuple-element.103.refs_1_.refs_0_), custom_call_target="tpu_custom_call" | custom-call | flops 100000000 | tf_op jit(solution)/shard_map/other_weights/pallas_call | solution.py:209
  37.7 2.7 %collective-permute-done.9.refs_6_ = bf16[320,768]{1,0:T(8,128)(2,1)S(1)} collective-permute-done((bf16[320,768]{1,0:T(8,128)(2,1)S(1)}, bf16[320,768]{1,0:T(8,128)(2,1)S(1)}, u32[]{:S(2)}, u32[]{:S(2)}) %collective-permute-start.9) | collective-permute-done | bytes 491552 | tf_op jit(solution)/shard_map/ppermute | solution.py:88
  43.0 8.9 %kv.1 = (bf16[2,1280,1024]{2,1,0:T(8,128)(2,1)}, bf16[2,1280,768]{2,1,0:T(8,128)(2,1)}) custom-call(s32[3]{0:T(128)} %pad_add_fusion.where, bf16[768,1024]{1,0:T(8,128)(2,1)} %get-tuple-element.103.refs_1_.refs_0_, bf16[320,768]{1,0:T(8,128)(2,1)} %get-tuple-element.104.refs_1_, bf16[320,768]{1,0:T(8,128)(2,1)} %copy-done.6, bf16[320,768]{1,0:T(8,128)(2,1)} %copy-done.8, ...), custom_call_target="tpu_custom_call" | custom-call | flops 100000000 | tf_op jit(solution)/shard_map/kv/pallas_call | solution.py:209
  58.2 7.8 %attention.1 = (bf16[1280,256]{1,0:T(8,128)(2,1)}, bf16[64,1408]{1,0:T(8,128)(2,1)}, bf16[64,1408]{1,0:T(8,128)(2,1)}, bf16[64,1408]{1,0:T(8,128)(2,1)}, bf16[64,1408]{1,0:T(8,128)(2,1)}) custom-call(s32[3]{0:T(128)} %pad_add_fusion.where, bf16[320,256]{1,0:T(8,128)(2,1)} %get-tuple-element.102.refs_3_.refs_0_, bf16[320,256]{1,0:T(8,128)(2,1)} %copy-done.19, ...), custom_call_target="tpu_custom_call" | custom-call | flops 100000000 | tf_op jit(solution)/shard_map/attention/pallas_call | solution.py:209
  74.6 4.3 %kv_turned.1.refs_15_.refs_5_ = bf16[2,768,1280]{2,1,0:T(8,128)(2,1)} custom-call(s32[3]{0:T(128)} %pad_add_fusion.where, bf16[2,1280,768]{2,1,0:T(8,128)(2,1)} %get-tuple-element.110.refs_5_.refs_0_, bf16[64,1408]{1,0:T(8,128)(2,1)} %get-tuple-element.115.refs_1_, f32[4,160,320]{2,1,0:T(8,128)} %copy.42.refs_2_.refs_1_, ...), custom_call_target="tpu_custom_call" | custom-call | flops 100000000 | tf_op jit(solution)/shard_map/kv_turned/pallas_call | solution.py:209
  79.0 3.5 %collective-permute-done.17.refs_9_ = bf16[3,160,1280]{2,1,0:T(8,128)(2,1)} collective-permute-done((bf16[3,160,1280]{2,1,0:T(8,128)(2,1)}, bf16[3,160,1280]{2,1,0:T(8,128)(2,1)}, u32[]{:S(2)}, u32[]{:S(2)}) %collective-permute-start.17) | collective-permute-done | bytes 1228832 | tf_op jit(solution)/shard_map/ppermute | solution.py:88
  83.1 2.6 collective-permute-done.19.refs_12_
  90.3 10.8 %latent.1 = (f32[128,1280]{1,0:T(8,128)}, bf16[6,128,1280]{2,1,0:T(8,128)(2,1)}, f32[2,1280]{1,0:T(2,128)}, bf16[32,1280]{1,0:T(8,128)(2,1)}, bf16[32,1280]{1,0:...) custom-call(s32[3]{0:T(128)} %pad_add_fusion.where, ...), custom_call_target="tpu_custom_call" | custom-call | flops 11000000512 | tf_op jit(solution)/shard_map/latent/pallas_call | solution.py:209
  106.6 5.6 %square_grad.1 = (bf16[2,3,160,1280]{3,2,1,0:T(8,128)(2,1)}, bf16[2,3,160,1280]{3,2,1,0:T(8,128)(2,1)}) custom-call(s32[3]{0:T(128)} %pad_add_fusion.where, bf16[6,128,1280]{2,1,0:T(8,128)(2,1)} %get-tuple-element.127.refs_0_, bf16[6,128,1280]{2,1,0:T(8,128)(2,1)} %copy-done.26, bf16[64,1408]{1,0:T(8,128)(2,1)} %get-tuple-element.126.refs_2_), custom_call_target="tpu_custom_call" | custom-call | flops 5000000000 | tf_op jit(solution)/shard_map/square_grad/pallas_call | solution.py:209
  113.7 24.5 %attention_back.1 = (bf16[1280,1024]{1,0:T(8,128)(2,1)}, bf16[1280,1024]{1,0:T(8,128)(2,1)}, bf16[4,160,256]{2,1,0:T(8,128)(2,1)}, bf16[4,160,256]{2,1,0:T(8,128)(2,1)}) custom-call(s32[3]{0:T(128)} %pad_add_fusion.where, bf16[1280,256]{1,0:T(8,128)(2,1)} %get-tuple-element.122.refs_0_, bf16[64,1408]{1,0:T(8,128)(2,1)} %get-tuple-element.123.refs_1_, ...), custom_call_target="tpu_custom_call" | custom-call | flops 12000000000 | tf_op jit(solution)/shard_map/attention_back/pallas_call | solution.py:209
  146.1 7.2 %token_grad_0.1 = (f32[1024,768]{1,0:T(8,128)}, f32[1,3,768]{2,1,0:T(4,128)}) custom-call(s32[3]{0:T(128)} %pad_add_fusion.where, f32[1024,768]{1,0:T(8,128)} %refs_0_.7, s32[1024,1]{1,0:T(8,128)} %copy.34.refs_1_, f32[3,768]{1,0:T(4,128)} %refs_12_.1, bf16[1280,1024]{1,0:T(8,128)(2,1)} %get-tuple-element.130.refs_3_.refs_0_, ...), custom_call_target="tpu_custom_call" | custom-call | flops 22000001024 | tf_op jit(solution)/shard_map/token_grad_0/pallas_call | solution.py:209
  154.8 3.6 %square_step.1.refs_4_ = bf16[1,3,160,1280]{3,2,1,0:T(8,128)(2,1)} custom-call(s32[3]{0:T(128)} %pad_add_fusion.where, bf16[2,3,160,1280]{3,2,1,0:T(8,128)(2,1)} %get-tuple-element.141.refs_6_.refs_0_, bf16[2,3,160,1280]{3,2,1,0:T(8,128)(2,1)} %copy-done.3, f32[1,3,768]{2,1,0:T(4,128)} %get-tuple-element.143.refs_2_.refs_6_), custom_call_target="tpu_custom_call" | custom-call | flops 4000000000 | tf_op jit(solution)/shard_map/square_step/pallas_call | solution.py:209
  161.6 3.6 %collective-permute-start.34 = (bf16[160,256]{1,0:T(8,128)(2,1)}, bf16[160,256]{1,0:T(8,128)(2,1)S(1)}, u32[]{:S(2)}, u32[]{:S(2)}) collective-permute-start(bf16[160,256]{1,0:T(8,128)(2,1)} %query_hid.1.refs_4_.refs_0_), channel_id=1, source_target_pairs={{0,24},{1,25},{2,26},{3,27},{4,28},{5,29},{6,30},{7,31},{8,16},{9,... | collective-permute-start | bytes 245768 | tf_op jit(solution)/shard_map/ppermute | solution.py:88
  167.5 9.1 %kv_grad.1 = (bf16[2,320,768]{2,1,0:T(8,128)(2,1)}, bf16[2,320,768]{2,1,0:T(8,128)(2,1)}) custom-call(s32[3]{0:T(128)} %pad_add_fusion.where, bf16[1280,1024]{1,0:T(8,128)(2,1)} %get-tuple-element.130.refs_3_.refs_0_, bf16[1280,1024]{1,0:T(8,128)(2,1)} %copy-done.2, bf16[1024,768]{1,0:T(8,128)(2,1)} %get-tuple-element.111.refs_2_, ...), custom_call_target="tpu_custom_call" | custom-call | flops 1000000000 | tf_op jit(solution)/shard_map/kv_grad/pallas_call | solution.py:209
  180.5 3.8 %square_turn.1 = (bf16[2,320,512]{2,1,0:T(8,128)(2,1)}, bf16[2,320,512]{2,1,0:T(8,128)(2,1)}) custom-call(s32[3]{0:T(128)} %pad_add_fusion.where, bf16[2,3,160,1280]{3,2,1,0:T(8,128)(2,1)} %get-tuple-element.141.refs_6_.refs_0_, bf16[2,3,160,1280]{3,2,1,0:T(8,128)(2,1)} %copy-done.3, bf16[1,3,160,1280]{3,2,1,0:T(8,128)(2,1)} %copy-done.4, ...), custom_call_target="tpu_custom_call" | custom-call | flops 100000000 | tf_op jit(solution)/shard_map/square_turn/pallas_call | solution.py:209
  187.5 3.1 %query_back.1 = (f32[160,320]{1,0:T(8,128)}, f32[1,1]{1,0:T(1,128)}, bf16[64,1280]{1,0:T(8,128)(2,1)}, bf16[64,1280]{1,0:T(8,128)(2,1)}, bf16[64,1280]{1,0:T(8,128)(2,1)}, /*index=5*/bf16[64,1280]{1,0:T(8,128)(2,1)}) custom-call(s32[3]{0:T(128)} %pad_add_fusion.where, bf16[256,1280]{1,0:T(8,128)(2,1)} %get-tuple-element.136.refs_0_, ...), custom_call_target="tpu_custom_call" | custom-call | flops 100000000 | tf_op jit(solution)/shard_map/query_back/pallas_call | solution.py:209
  201.9 2.4 collective-permute-start.46
  207.2 2.5 kv_turn.1
  211.5 2.6 %latent_end.1 = (f32[320,32]{1,0:T(8,128)}, f32[2,1280]{1,0:T(2,128)}) custom-call(s32[3]{0:T(128)} %pad_add_fusion.where, bf16[64,1280]{1,0:T(8,128)(2,1)} %get-tuple-element.147.refs_0_, bf16[64,1280]{1,0:T(8,128)(2,1)} %copy-done.41, bf16[64,1280]{1,0:T(8,128)(2,1)} %copy-done.42, bf16[64,1280]{1,0:T(8,128)(2,1)} %copy-done.43, f32[64,1280]{1,0:T(8,128)} %refs_4_.3, ...), custom_call_target="tpu_custom_call" | custom-call | flops 3000000000 | tf_op jit(solution)/shard_map/latent_end/pallas_call | solution.py:209
  214.2 7.2 %token_grad_1.1 = (f32[1024,768]{1,0:T(8,128)}, f32[1,3,768]{2,1,0:T(4,128)}) custom-call(s32[3]{0:T(128)} %pad_add_fusion.where, f32[1024,768]{1,0:T(8,128)} %refs_0_.7, s32[1024,1]{1,0:T(8,128)} %copy.34.refs_1_, f32[3,768]{1,0:T(4,128)} %refs_12_.1, bf16[1280,1024]{1,0:T(8,128)(2,1)} %get-tuple-element.130.refs_3_.refs_0_, ...), custom_call_target="tpu_custom_call", output_to_operand_aliasing={{0}: (7, {})} | custom-call | flops 100000000 | tf_op jit(solution)/shard_map/token_grad_1/pallas_call | solution.py:209
  221.4 3.3 %collective-permute-done.44.refs_1_ = bf16[2,192,320]{2,1,0:T(8,128)(2,1)S(1)} collective-permute-done((bf16[2,192,320]{2,1,0:T(8,128)(2,1)}, bf16[2,192,320]{2,1,0:T(8,128)(2,1)S(1)}, u32[]{:S(2)}, u32[]{:S(2)}) %collective-permute-start.44) | collective-permute-done | bytes 245792 | tf_op jit(solution)/shard_map/ppermute | solution.py:88
  227.8 2.9 %square_end.1 = (f32[160,512]{1,0:T(8,128)}, bf16[160,512]{1,0:T(8,128)(2,1)}, f32[1,1]{1,0:T(1,128)}) custom-call(s32[3]{0:T(128)} %pad_add_fusion.where, bf16[2,320,512]{2,1,0:T(8,128)(2,1)} %get-tuple-element.146.refs_4_.refs_0_, bf16[2,320,512]{2,1,0:T(8,128)(2,1)} %copy-done.5, bf16[1,320,512]{2,1,0:T(8,128)(2,1)} %copy-done.30, ...), custom_call_target="tpu_custom_call" | custom-call | flops 3000000000 | tf_op jit(solution)/shard_map/square_end/pallas_call | solution.py:209
  230.7 5.5 %collective-permute-done.45.refs_2_ = bf16[1,192,320]{2,1,0:T(8,128)(2,1)S(1)} collective-permute-done((bf16[1,192,320]{2,1,0:T(8,128)(2,1)}, bf16[1,192,320]{2,1,0:T(8,128)(2,1)S(1)}, u32[]{:S(2)}, u32[]{:S(2)}) %collective-permute-start.45) | collective-permute-done | bytes 122912 | tf_op jit(solution)/shard_map/ppermute | solution.py:88
  236.9 3.3 %kv_end.1 = (f32[96,320]{1,0:T(8,128)}, bf16[96,320]{1,0:T(8,128)(2,1)}, f32[8,1280]{1,0:T(8,128)}) custom-call(s32[3]{0:T(128)} %pad_add_fusion.where, bf16[2,192,320]{2,1,0:T(8,128)(2,1)} %get-tuple-element.153.refs_6_.refs_0_, bf16[2,192,320]{2,1,0:T(8,128)(2,1)} %copy-done.15, bf16[1,192,320]{2,1,0:T(8,128)(2,1)} %copy-done.47, ...), custom_call_target="tpu_custom_call" | custom-call | flops 2000000000 | tf_op jit(solution)/shard_map/kv_end/pallas_call | solution.py:209
  251.2 2.5 collective-permute-start.51
  254.4 2.6 finish.1
  257.6 7.0 %update.1 = (f32[1,1]{1,0:T(1,128)}, f32[2,4,160,320]{3,2,1,0:T(8,128)}, f32[2,4,160,320]{3,2,1,0:T(8,128)}, f32[2,2,96,320]{3,2,1,0:T(8,128)}, f32[2,2,96,320]{...) custom-call(s32[3]{0:T(128)} %pad_add_fusion.where, ...), custom_call_target="tpu_custom_call" | custom-call | flops 7000000000 | tf_op jit(solution)/shard_map/update/pallas_call | solution.py:209
  (224 shorter events, 99.2 us)
Async XLA Ops:
  3.1 12.6 %collective-permute-start.2 = (bf16[64,1280]{1,0:T(8,128)(2,1)}, bf16[64,1280]{1,0:T(8,128)(2,1)S(1)}, u32[]{:S(2)}, u32[]{:S(2)}) collective-permute-start(bf16[64,1280]{1,0:T(8,128)(2,1)} %lat_norm.1.refs_1_.refs_0_), channel_id=1, source_target_pairs={{0,3},{1,2},{2,1},{3,0},{4,7},{5,6},{6,5},{7,4},{8,11},{9,10},{10,... | collective-permute-start | bytes 491528 | tf_op jit(solution)/shard_map/ppermute | solution.py:88
  10.2 13.0 %collective-permute-start.6 = (bf16[320,768]{1,0:T(8,128)(2,1)}, bf16[320,768]{1,0:T(8,128)(2,1)S(1)}, u32[]{:S(2)}, u32[]{:S(2)}) collective-permute-start(bf16[320,768]{1,0:T(8,128)(2,1)} %get-tuple-element.104.refs_1_), channel_id=1, source_target_pairs={{0,1},{1,0},{2,3},{3,2},{4,6},{5,7},{6,4},{7,5},{8,10},{9,11},{10,... | collective-permute-start | bytes 1474568 | tf_op jit(solution)/shard_map/ppermute | solution.py:88
  19.7 16.2 %collective-permute-start.5 = (bf16[320,256]{1,0:T(8,128)(2,1)}, bf16[320,256]{1,0:T(8,128)(2,1)S(1)}, u32[]{:S(2)}, u32[]{:S(2)}) collective-permute-start(bf16[320,256]{1,0:T(8,128)(2,1)} %get-tuple-element.102.refs_3_.refs_0_), channel_id=1, source_target_pairs={{0,3},{1,2},{2,1},{3,0},{4,7},{5,6},{6,5},{7,4},{8,11},{9,10},{10,... | collective-permute-start | bytes 491528 | tf_op jit(solution)/shard_map/ppermute | solution.py:88
  21.6 14.3 %collective-permute-start.4 = (bf16[320,256]{1,0:T(8,128)(2,1)}, bf16[320,256]{1,0:T(8,128)(2,1)S(1)}, u32[]{:S(2)}, u32[]{:S(2)}) collective-permute-start(bf16[320,256]{1,0:T(8,128)(2,1)} %get-tuple-element.102.refs_3_.refs_0_), channel_id=1, source_target_pairs={{0,2},{1,3},{2,0},{3,1},{4,6},{5,7},{6,4},{7,5},{8,10},{9,11},{10,... | collective-permute-start | bytes 491528 | tf_op jit(solution)/shard_map/ppermute | solution.py:88
  22.1 13.8 %collective-permute-start.3 = (bf16[320,256]{1,0:T(8,128)(2,1)}, bf16[320,256]{1,0:T(8,128)(2,1)S(1)}, u32[]{:S(2)}, u32[]{:S(2)}) collective-permute-start(bf16[320,256]{1,0:T(8,128)(2,1)} %get-tuple-element.102.refs_3_.refs_0_), channel_id=1, source_target_pairs={{0,1},{1,0},{2,3},{3,2},{4,5},{5,4},{6,7},{7,6},{8,9},{9,8},{10,11... | collective-permute-start | bytes 491528 | tf_op jit(solution)/shard_map/ppermute | solution.py:88
  23.2 12.7 %collective-permute-start.8 = (bf16[320,768]{1,0:T(8,128)(2,1)S(1)}, bf16[320,768]{1,0:T(8,128)(2,1)S(1)}, u32[]{:S(2)}, u32[]{:S(2)}) collective-permute-start(bf16[320,768]{1,0:T(8,128)(2,1)S(1)} %collective-permute-done.6.refs_2_), channel_id=1, source_target_pairs={{0,2},{1,3},{2,0},{3,1},{4,5},{5,4},{6,7},{7,6},{8,9},{9,8},{10,11... | collective-permute-start | bytes 1474568 | tf_op jit(solution)/shard_map/ppermute | solution.py:88
  24.7 11.4 %collective-permute-start.7 = (bf16[320,768]{1,0:T(8,128)(2,1)S(1)}, bf16[320,768]{1,0:T(8,128)(2,1)S(1)}, u32[]{:S(2)}, u32[]{:S(2)}) collective-permute-start(bf16[320,768]{1,0:T(8,128)(2,1)S(1)} %collective-permute-done.6.refs_2_), channel_id=1, source_target_pairs={{0,8},{1,9},{2,10},{3,11},{4,12},{5,13},{6,14},{7,15},{8,0},{9,1},... | collective-permute-start | bytes 1474568 | tf_op jit(solution)/shard_map/ppermute | solution.py:88
  36.1 17.0 %collective-permute-start.16 = (bf16[3,160,1280]{2,1,0:T(8,128)(2,1)}, bf16[3,160,1280]{2,1,0:T(8,128)(2,1)}, u32[]{:S(2)}, u32[]{:S(2)}) collective-permute-start(bf16[3,160,1280]{2,1,0:T(8,128)(2,1)} %get-tuple-element.117.refs_10_.refs_7_), channel_id=1, source_target_pairs={{0,1},{1,0},{2,3},{3,2},{4,6},{5,7},{6,4},{7,5},{8,10},{9,11},{10,... | collective-permute-start | bytes 3686408 | tf_op jit(solution)/shard_map/ppermute | solution.py:88
  36.6 20.4 %collective-permute-start.12 = (bf16[1024,768]{1,0:T(8,128)(2,1)}, bf16[1024,768]{1,0:T(8,128)(2,1)S(1)}, u32[]{:S(2)}, u32[]{:S(2)}) collective-permute-start(bf16[1024,768]{1,0:T(8,128)(2,1)} %get-tuple-element.111.refs_2_), channel_id=1, source_target_pairs={{0,4},{1,5},{2,6},{3,7},{4,0},{5,1},{6,2},{7,3},{8,12},{9,13},{10,... | collective-permute-start | bytes 4718600 | tf_op jit(solution)/shard_map/ppermute | solution.py:88
  53.1 25.9 %collective-permute-start.18 = (bf16[3,160,1280]{2,1,0:T(8,128)(2,1)}, bf16[3,160,1280]{2,1,0:T(8,128)(2,1)}, u32[]{:S(2)}, u32[]{:S(2)}) collective-permute-start(bf16[3,160,1280]{2,1,0:T(8,128)(2,1)} %collective-permute-done.16.refs_8_), channel_id=1, source_target_pairs={{0,2},{1,3},{2,0},{3,1},{4,5},{5,4},{6,7},{7,6},{8,9},{9,8},{10,11... | collective-permute-start | bytes 3686408 | tf_op jit(solution)/shard_map/ppermute | solution.py:88
  53.7 28.9 %collective-permute-start.17 = (bf16[3,160,1280]{2,1,0:T(8,128)(2,1)}, bf16[3,160,1280]{2,1,0:T(8,128)(2,1)}, u32[]{:S(2)}, u32[]{:S(2)}) collective-permute-start(bf16[3,160,1280]{2,1,0:T(8,128)(2,1)} %collective-permute-done.16.refs_8_), channel_id=1, source_target_pairs={{0,8},{1,9},{2,10},{3,11},{4,12},{5,13},{6,14},{7,15},{8,0},{9,1},... | collective-permute-start | bytes 3686408 | tf_op jit(solution)/shard_map/ppermute | solution.py:88
  66.0 13.0 %collective-permute-start.13 = (bf16[64,1408]{1,0:T(8,128)(2,1)}, bf16[64,1408]{1,0:T(8,128)(2,1)S(1)}, u32[]{:S(2)}, u32[]{:S(2)}) collective-permute-start(bf16[64,1408]{1,0:T(8,128)(2,1)} %get-tuple-element.113), channel_id=1, source_target_pairs={{0,1},{1,0},{2,3},{3,2},{4,5},{5,4},{6,7},{7,6},{8,9},{9,8},{10,11... | collective-permute-start | bytes 540680 | tf_op jit(solution)/shard_map/ppermute | solution.py:88
  67.6 11.4 %collective-permute-start.14 = (bf16[64,1408]{1,0:T(8,128)(2,1)}, bf16[64,1408]{1,0:T(8,128)(2,1)S(1)}, u32[]{:S(2)}, u32[]{:S(2)}) collective-permute-start(bf16[64,1408]{1,0:T(8,128)(2,1)} %get-tuple-element.114), channel_id=1, source_target_pairs={{0,2},{1,3},{2,0},{3,1},{4,6},{5,7},{6,4},{7,5},{8,10},{9,11},{10,... | collective-permute-start | bytes 540680 | tf_op jit(solution)/shard_map/ppermute | solution.py:88
  68.1 10.9 %collective-permute-start.15 = (bf16[64,1408]{1,0:T(8,128)(2,1)}, bf16[64,1408]{1,0:T(8,128)(2,1)S(1)}, u32[]{:S(2)}, u32[]{:S(2)}) collective-permute-start(bf16[64,1408]{1,0:T(8,128)(2,1)} %get-tuple-element.115.refs_1_), channel_id=1, source_target_pairs={{0,3},{1,2},{2,1},{3,0},{4,7},{5,6},{6,5},{7,4},{8,11},{9,10},{10,... | collective-permute-start | bytes 540680 | tf_op jit(solution)/shard_map/ppermute | solution.py:88
  101.3 11.5 %collective-permute-start.26 = (bf16[32,1280]{1,0:T(8,128)(2,1)}, bf16[32,1280]{1,0:T(8,128)(2,1)S(1)}, u32[]{:S(2)}, u32[]{:S(2)}) collective-permute-start(bf16[32,1280]{1,0:T(8,128)(2,1)} %get-tuple-element.129), channel_id=1, source_target_pairs={{0,4},{1,5},{2,6},{3,7},{4,0},{5,1},{6,2},{7,3},{8,12},{9,13},{10,... | collective-permute-start | bytes 245768 | tf_op jit(solution)/shard_map/ppermute | solution.py:88
  101.7 11.2 %collective-permute-start.22 = (bf16[64,1408]{1,0:T(8,128)(2,1)}, bf16[64,1408]{1,0:T(8,128)(2,1)S(1)}, u32[]{:S(2)}, u32[]{:S(2)}) collective-permute-start(bf16[64,1408]{1,0:T(8,128)(2,1)} %get-tuple-element.124), channel_id=1, source_target_pairs={{0,1},{1,0},{2,3},{3,2},{4,5},{5,4},{6,7},{7,6},{8,9},{9,8},{10,11... | collective-permute-start | bytes 540680 | tf_op jit(solution)/shard_map/ppermute | solution.py:88
  102.3 10.6 %collective-permute-start.23 = (bf16[64,1408]{1,0:T(8,128)(2,1)}, bf16[64,1408]{1,0:T(8,128)(2,1)S(1)}, u32[]{:S(2)}, u32[]{:S(2)}) collective-permute-start(bf16[64,1408]{1,0:T(8,128)(2,1)} %get-tuple-element.125), channel_id=1, source_target_pairs={{0,2},{1,3},{2,0},{3,1},{4,6},{5,7},{6,4},{7,5},{8,10},{9,11},{10,... | collective-permute-start | bytes 540680 | tf_op jit(solution)/shard_map/ppermute | solution.py:88
  112.3 41.1 %collective-permute-start.31 = (bf16[2,3,160,1280]{3,2,1,0:T(8,128)(2,1)}, bf16[2,3,160,1280]{3,2,1,0:T(8,128)(2,1)S(1)}, u32[]{:S(2)}, u32[]{:S(2)}) collective-permute-start(bf16[2,3,160,1280]{3,2,1,0:T(8,128)(2,1)} %get-tuple-element.140), channel_id=1, source_target_pairs={{0,2},{1,3},{2,0},{3,1},{4,5},{5,4},{6,7},{7,6},{8,9},{9,8},{10,11... | collective-permute-start | bytes 7372808 | tf_op jit(solution)/shard_map/ppermute | solution.py:88
  138.2 27.8 %collective-permute-start.35 = (bf16[1280,1024]{1,0:T(8,128)(2,1)}, bf16[1280,1024]{1,0:T(8,128)(2,1)S(1)}, u32[]{:S(2)}, u32[]{:S(2)}) collective-permute-start(bf16[1280,1024]{1,0:T(8,128)(2,1)} %get-tuple-element.131.refs_4_), channel_id=1, source_target_pairs={{0,4},{1,5},{2,6},{3,7},{4,0},{5,1},{6,2},{7,3},{8,12},{9,13},{10,... | collective-permute-start | bytes 7864328 | tf_op jit(solution)/shard_map/ppermute | solution.py:88
  142.6 10.7 %collective-permute-start.28 = (bf16[160,256]{1,0:T(8,128)(2,1)}, bf16[160,256]{1,0:T(8,128)(2,1)S(1)}, u32[]{:S(2)}, u32[]{:S(2)}) collective-permute-start(bf16[160,256]{1,0:T(8,128)(2,1)} %get-tuple-element.138), channel_id=1, source_target_pairs={{0,1},{1,0},{2,3},{3,2},{4,5},{5,4},{6,7},{7,6},{8,9},{9,8},{10,11... | collective-permute-start | bytes 245768 | tf_op jit(solution)/shard_map/ppermute | solution.py:88
  158.4 21.1 %collective-permute-start.37 = (bf16[1,3,160,1280]{3,2,1,0:T(8,128)(2,1)}, bf16[1,3,160,1280]{3,2,1,0:T(8,128)(2,1)S(1)}, u32[]{:S(2)}, u32[]{:S(2)}) collective-permute-start(bf16[1,3,160,1280]{3,2,1,0:T(8,128)(2,1)} %square_step.1.refs_4_), channel_id=1, source_target_pairs={{0,1},{1,0},{2,3},{3,2},{4,6},{5,7},{6,4},{7,5},{8,10},{9,11},{10,... | collective-permute-start | bytes 3686408 | tf_op jit(solution)/shard_map/ppermute | solution.py:88
  161.6 15.5 %collective-permute-start.34 = (bf16[160,256]{1,0:T(8,128)(2,1)}, bf16[160,256]{1,0:T(8,128)(2,1)S(1)}, u32[]{:S(2)}, u32[]{:S(2)}) collective-permute-start(bf16[160,256]{1,0:T(8,128)(2,1)} %query_hid.1.refs_4_.refs_0_), channel_id=1, source_target_pairs={{0,24},{1,25},{2,26},{3,27},{4,28},{5,29},{6,30},{7,31},{8,16},{9,... | collective-permute-start | bytes 245768 | tf_op jit(solution)/shard_map/ppermute | solution.py:88
  165.2 11.9 %collective-permute-start.33 = (bf16[160,256]{1,0:T(8,128)(2,1)}, bf16[160,256]{1,0:T(8,128)(2,1)S(1)}, u32[]{:S(2)}, u32[]{:S(2)}) collective-permute-start(bf16[160,256]{1,0:T(8,128)(2,1)} %query_hid.1.refs_4_.refs_0_), channel_id=1, source_target_pairs={{0,16},{1,17},{2,18},{3,19},{4,20},{5,21},{6,22},{7,23},{8,24},{9,... | collective-permute-start | bytes 245768 | tf_op jit(solution)/shard_map/ppermute | solution.py:88
  165.2 11.9 %collective-permute-start.32 = (bf16[160,256]{1,0:T(8,128)(2,1)}, bf16[160,256]{1,0:T(8,128)(2,1)S(1)}, u32[]{:S(2)}, u32[]{:S(2)}) collective-permute-start(bf16[160,256]{1,0:T(8,128)(2,1)} %query_hid.1.refs_4_.refs_0_), channel_id=1, source_target_pairs={{0,8},{1,9},{2,10},{3,11},{4,12},{5,13},{6,14},{7,15},{8,0},{9,1},... | collective-permute-start | bytes 245768 | tf_op jit(solution)/shard_map/ppermute | solution.py:88
  176.6 14.3 %collective-permute-start.41 = (bf16[2,320,768]{2,1,0:T(8,128)(2,1)}, bf16[2,320,768]{2,1,0:T(8,128)(2,1)S(1)}, u32[]{:S(2)}, u32[]{:S(2)}) collective-permute-start(bf16[2,320,768]{2,1,0:T(8,128)(2,1)} %get-tuple-element.151), channel_id=1, source_target_pairs={{0,2},{1,3},{2,0},{3,1},{4,5},{5,4},{6,7},{7,6},{8,9},{9,8},{10,11... | collective-permute-start | bytes 2949128 | tf_op jit(solution)/shard_map/ppermute | solution.py:88
  184.4 14.7 %collective-permute-start.43 = (bf16[2,320,512]{2,1,0:T(8,128)(2,1)}, bf16[2,320,512]{2,1,0:T(8,128)(2,1)S(1)}, u32[]{:S(2)}, u32[]{:S(2)}) collective-permute-start(bf16[2,320,512]{2,1,0:T(8,128)(2,1)} %get-tuple-element.152), channel_id=1, source_target_pairs={{0,8},{1,9},{2,10},{3,11},{4,12},{5,13},{6,14},{7,15},{8,0},{9,1},... | collective-permute-start | bytes 1966088 | tf_op jit(solution)/shard_map/ppermute | solution.py:88
  193.9 12.5 %collective-permute-start.42 = (bf16[1,320,768]{2,1,0:T(8,128)(2,1)}, bf16[1,320,768]{2,1,0:T(8,128)(2,1)S(1)}, u32[]{:S(2)}, u32[]{:S(2)}) collective-permute-start(bf16[1,320,768]{2,1,0:T(8,128)(2,1)} %bitcast.30), channel_id=1, source_target_pairs={{0,1},{1,0},{2,3},{3,2},{4,6},{5,7},{6,4},{7,5},{8,10},{9,11},{10,... | collective-permute-start | bytes 1474568 | tf_op jit(solution)/shard_map/ppermute | solution.py:88
  195.1 15.6 %collective-permute-start.38 = (bf16[64,1280]{1,0:T(8,128)(2,1)S(1)}, bf16[64,1280]{1,0:T(8,128)(2,1)S(1)}, u32[]{:S(2)}, u32[]{:S(2)}) collective-permute-start(bf16[64,1280]{1,0:T(8,128)(2,1)S(1)} %copy-done.39), channel_id=1, source_target_pairs={{0,1},{1,0},{2,3},{3,2},{4,5},{5,4},{6,7},{7,6},{8,9},{9,8},{10,11... | collective-permute-start | bytes 491528 | tf_op jit(solution)/shard_map/ppermute | solution.py:88
  195.9 14.8 %collective-permute-start.39 = (bf16[64,1280]{1,0:T(8,128)(2,1)S(1)}, bf16[64,1280]{1,0:T(8,128)(2,1)S(1)}, u32[]{:S(2)}, u32[]{:S(2)}) collective-permute-start(bf16[64,1280]{1,0:T(8,128)(2,1)S(1)} %copy-done.38), channel_id=1, source_target_pairs={{0,2},{1,3},{2,0},{3,1},{4,6},{5,7},{6,4},{7,5},{8,10},{9,11},{10,... | collective-permute-start | bytes 491528 | tf_op jit(solution)/shard_map/ppermute | solution.py:88
  197.2 13.6 %collective-permute-start.40 = (bf16[64,1280]{1,0:T(8,128)(2,1)S(1)}, bf16[64,1280]{1,0:T(8,128)(2,1)S(1)}, u32[]{:S(2)}, u32[]{:S(2)}) collective-permute-start(bf16[64,1280]{1,0:T(8,128)(2,1)S(1)} %copy-done.16), channel_id=1, source_target_pairs={{0,3},{1,2},{2,1},{3,0},{4,7},{5,6},{6,5},{7,4},{8,11},{9,10},{10,... | collective-permute-start | bytes 491528 | tf_op jit(solution)/shard_map/ppermute | solution.py:88
  201.9 25.2 %collective-permute-start.46 = (bf16[1,320,512]{2,1,0:T(8,128)(2,1)}, bf16[1,320,512]{2,1,0:T(8,128)(2,1)S(1)}, u32[]{:S(2)}, u32[]{:S(2)}) collective-permute-start(bf16[1,320,512]{2,1,0:T(8,128)(2,1)} %bitcast.31), channel_id=1, source_target_pairs={{0,16},{1,17},{2,18},{3,19},{4,20},{5,21},{6,22},{7,23},{8,24},{9,... | collective-permute-start | bytes 983048 | tf_op jit(solution)/shard_map/ppermute | solution.py:88
  209.7 15.0 %collective-permute-start.44 = (bf16[2,192,320]{2,1,0:T(8,128)(2,1)}, bf16[2,192,320]{2,1,0:T(8,128)(2,1)S(1)}, u32[]{:S(2)}, u32[]{:S(2)}) collective-permute-start(bf16[2,192,320]{2,1,0:T(8,128)(2,1)} %get-tuple-element.156), channel_id=1, source_target_pairs={{0,8},{1,9},{2,10},{3,11},{4,12},{5,13},{6,14},{7,15},{8,0},{9,1},... | collective-permute-start | bytes 737288 | tf_op jit(solution)/shard_map/ppermute | solution.py:88
  (76 other events, 299.0 us)
